TPU v7x, 512 devices: a whole 4x8x8 slice. The times are simulated.
512 devices in a mesh: dp: 16 (over z_hi, x), space: 32 (over z_lo, y, core).
Axes of the slice: x: 4, y: 8, z: 8 (z_hi: 4, z_lo: 2; z = z_hi * 2 + z_lo), core: 2. Of those that a mesh axis runs over, the one named last changes fastest.
Arguments:
- activations: bfloat16 [16, 64, 14, 14, 256], P('dp', 'space'), may hold values from -7 to 7
- tissue: int32 [16, 64, 14, 14], P('dp', 'space'), may hold values from 0 to 1, as said below
- neighbours: int32 [16, 64, 8], P('dp', 'space'), may hold values from -1 to 63, as said below
- w_reduce: bfloat16 [256, 256], replicated, may hold values from -0.375 to 0.375
- w_group: bfloat16 [3, 3, 8, 256], replicated, may hold values from -0.75 to 0.75
- norm_gain: float32 [256], replicated, may hold values from 0.25 to 1.75
- norm_bias: float32 [256], replicated, may hold values from -3 to 3
- w_expand: bfloat16 [256, 512], replicated, may hold values from -0.375 to 0.375
- cotangent: bfloat16 [16, 64, 14, 14, 512], P('dp', 'space'), may hold values from -7 to 7
Outputs:
- input_grad: bfloat16 [16, 64, 14, 14, 256], P('dp', 'space')
- reduce_grad: float32 [256, 256], replicated
- group_grad: float32 [3, 3, 8, 256], replicated
- gain_grad: float32 [256], replicated
- bias_grad: float32 [256], replicated
- expand_grad: float32 [256, 512], replicated
Inputs may be any that keep to these rules, and one draw needn't show every extreme that they name: `neighbours`: tile slot t of a slide lies at row t // 4 and column t % 4 of its grid; an entry names the slot at the stated side only if both tiles hold tissue, so that tile b is a neighbour of tile a at one side exactly when a is the neighbour of b at the opposite side. Slots 0, 62 and 63 hold tissue. `tissue`: slots absent from a slide are 0 throughout; a present tile is 1 on the pixels its draw marks, always including its first pixel.
All inputs are finite; a program needn't handle non-finite values.
Results may differ from a plain program's by a relative error of at most 0.011.
Values may be sent and summed in bfloat16 or wider, within the bound.
No kernel may reach another device: no remote copies, remote signals or barrier semaphores. Data moves between devices by JAX's collectives and lax.ppermute only.
A program may use at most 128 MiB of HBM per device.

v0:
```python
import jax
import jax.numpy as jnp
from jax import lax
from jax.sharding import PartitionSpec as P

REACH = 3


epsilon = 1e-05


def passed_along(block, axis, distance):
    devices = range(lax.axis_size(axis))
    route = [(i - distance, i) for i in devices if i - distance in devices]
    return lax.ppermute(block, axis, route)


def extend(values, link_ids):
    tiles = values.shape[0]
    side = values.shape[1]
    width = values.shape[3]
    rims = jnp.stack([values[:, 0], values[:, -1], values[:, :, 0], values[:, :, -1]], axis=1)
    here = lax.axis_index("space")
    pieces = []
    label_parts = []
    for offset in range(-REACH, REACH + 1):
        if offset == 0:
            arrived = rims
        else:
            arrived = passed_along(rims, "space", -offset)
        pieces.append(arrived)
        label_parts.append((here + offset) * tiles + jnp.arange(tiles, dtype=jnp.int32))
    candidates = jnp.concatenate(pieces, axis=0)
    labels = jnp.concatenate(label_parts, axis=0)
    strips = candidates.reshape(candidates.shape[0], 4, side * width)

    def pick(which, column):
        select = (link_ids[:, column][:, None] == labels[None, :]).astype(jnp.bfloat16)
        taken = jnp.dot(select, strips[:, which], preferred_element_type=jnp.float32)
        return taken.astype(jnp.bfloat16).reshape(tiles, side, width)

    above = pick(1, 0)
    below = pick(0, 1)
    left_side = pick(3, 2)
    right_side = pick(2, 3)
    corner_nw = pick(1, 4)[:, -1]
    corner_ne = pick(1, 5)[:, 0]
    corner_sw = pick(0, 6)[:, -1]
    corner_se = pick(0, 7)[:, 0]
    upper = jnp.concatenate([corner_nw[:, None], above, corner_ne[:, None]], axis=1)
    lower = jnp.concatenate([corner_sw[:, None], below, corner_se[:, None]], axis=1)
    middle = jnp.concatenate([left_side[:, :, None], values, right_side[:, :, None]], axis=2)
    return jnp.concatenate([upper[:, None], middle, lower[:, None]], axis=1)


def grouped(padded, kernel):
    return lax.conv_general_dilated(
        padded,
        kernel,
        (1, 1),
        "VALID",
        dimension_numbers=("NHWC", "HWIO", "NHWC"),
        feature_group_count=padded.shape[-1] // kernel.shape[2],
        preferred_element_type=jnp.float32,
    )


def flipped(kernel):
    group_width = kernel.shape[2]
    width = kernel.shape[3]
    split = kernel.reshape(3, 3, group_width, width // group_width, group_width)[::-1, ::-1]
    return split.transpose(0, 1, 4, 3, 2).reshape(3, 3, group_width, width)


def kernel_grad(padded, grad, group_width):
    side = grad.shape[1]
    width = grad.shape[3]
    groups = width // group_width
    grad_groups = grad.reshape(-1, groups, group_width)
    rows_out = []
    for row_tap in range(3):
        cols_out = []
        for col_tap in range(3):
            window = padded[:, row_tap : row_tap + side, col_tap : col_tap + side, :].reshape(
                -1, groups, group_width
            )
            term = jnp.einsum(
                "pgi,pgj->igj", window, grad_groups, preferred_element_type=jnp.float32
            )
            cols_out.append(term.reshape(group_width, width))
        rows_out.append(jnp.stack(cols_out))
    return jnp.stack(rows_out)


def body(
    activations, tissue, neighbours, w_reduce, w_group, norm_gain, norm_bias, w_expand, cotangent
):
    slab = activations[0]
    width = slab.shape[3]
    pixel_count = slab.shape[0] * slab.shape[1] * slab.shape[2]
    flat_input = slab.reshape(pixel_count, width)
    reduced = (
        jnp.dot(flat_input, w_reduce, preferred_element_type=jnp.float32)
        .astype(jnp.bfloat16)
        .reshape(slab.shape)
    )
    link_ids = neighbours[0]
    padded = extend(reduced, link_ids)
    pre_norm = grouped(padded, w_group)
    tissue_weight = tissue[0].astype(jnp.float32)[..., None]
    first_sum, square_sum, counted = lax.psum(
        (
            jnp.sum(tissue_weight * pre_norm, axis=(0, 1, 2)),
            jnp.sum(tissue_weight * pre_norm * pre_norm, axis=(0, 1, 2)),
            jnp.sum(tissue_weight),
        ),
        ("dp", "space"),
    )
    centre = first_sum / counted
    spread = square_sum / counted - centre * centre
    inverse_std = lax.rsqrt(spread + epsilon)
    normed = (pre_norm - centre) * inverse_std
    before = norm_gain * normed + norm_bias
    sigma = jax.nn.sigmoid(before)
    hidden = (before * sigma).astype(jnp.bfloat16)
    out_grad = cotangent[0] * tissue[0][..., None].astype(jnp.bfloat16)
    hidden_flat = hidden.reshape(pixel_count, width)
    out_flat = out_grad.reshape(pixel_count, out_grad.shape[-1])
    expand_grad = lax.dot_general(
        hidden_flat, out_flat, (((0,), (0,)), ((), ())), preferred_element_type=jnp.float32
    )
    hidden_grad = lax.dot_general(
        out_flat, w_expand, (((1,), (1,)), ((), ())), preferred_element_type=jnp.float32
    ).reshape(pre_norm.shape)
    before_grad = hidden_grad * sigma * (1.0 + before * (1.0 - sigma))
    gain_grad, bias_grad = lax.psum(
        (jnp.sum(before_grad * normed, axis=(0, 1, 2)), jnp.sum(before_grad, axis=(0, 1, 2))),
        ("dp", "space"),
    )
    norm_grad = (
        norm_gain
        * inverse_std
        * (before_grad - tissue_weight * (bias_grad + normed * gain_grad) / counted)
    ).astype(jnp.bfloat16)
    padded_grad = extend(norm_grad, link_ids)
    reduced_grad = grouped(padded_grad, flipped(w_group)).astype(jnp.bfloat16)
    group_grad = kernel_grad(padded, norm_grad, w_group.shape[2])
    grad_flat = reduced_grad.reshape(pixel_count, width)
    reduce_grad = lax.dot_general(
        flat_input, grad_flat, (((0,), (0,)), ((), ())), preferred_element_type=jnp.float32
    )
    input_grad = (
        lax.dot_general(
            grad_flat, w_reduce, (((1,), (1,)), ((), ())), preferred_element_type=jnp.float32
        )
        .astype(jnp.bfloat16)
        .reshape(slab.shape)
    )
    reduce_grad, expand_grad, group_grad = lax.psum(
        (reduce_grad, expand_grad, group_grad), ("dp", "space")
    )
    return (input_grad[None], reduce_grad, group_grad, gain_grad, bias_grad, expand_grad)


def solution(mesh):
    return jax.shard_map(
        body,
        mesh=mesh,
        in_specs=(
            P("dp", "space", None, None, None),
            P("dp", "space", None, None),
            P("dp", "space", None),
            P(),
            P(),
            P(),
            P(),
            P(),
            P("dp", "space", None, None, None),
        ),
        out_specs=(P("dp", "space", None, None, None), P(), P(), P(), P(), P()),
        check_vma=False,
    )
```

profile of v0, /device:TPU:1, one launch (start us, length us, event | category | flops | bytes accessed | tf_op | source)
XLA Modules:
  0.0 757.1 jit_solution(13725550790717960648)
XLA Ops:
  10.4 6.2 collective-permute-start
  29.8 4.4 concatenate.107
  55.0 7.4 copy.293
  62.5 20.3 %fusion = (f32[32,8]{1,0:T(8,128)S(1)}, f32[32,8]{1,0:T(8,128)S(1)}, f32[2,14,14,32,8]{4,0,3,2,1:T(2,128)}) fusion(f32[2,14,14]{0,2,1:T(8,128)S(1)} %copy.277, bf16[2,16,16,32,8]{4,0,3,2,1:T(2,128)(2,1)} %copy.293, bf16[3,3,8,32,8]{4,3,2,1,0:T(8,128)(2,1)S(1)} %shard_map.138), kind=kOutput, calls=%fused_computation.2 | convolution fusion | flops 14851584 | bytes 704032 | tf_op jit(solution)/shard_map/conv_general_dilated | solution.py:57
  82.9 6.5 copy.353
  89.4 5.7 reshape.204
  95.1 105.3 %all-reduce.1 = (f32[256]{0:T(256)S(1)}, f32[]{:T(128)}, f32[256]{0:T(256)S(1)}) all-reduce(f32[256]{0:T(256)S(1)} %reduce_sum.53, f32[]{:T(128)} %convert_reduce_fusion, f32[256]{0:T(256)S(1)} %reduce_sum.50), channel_id=1, replica_groups=mesh['dp'=16,'space'=32] {'dp','space'}, use_global_device_ids=true, to_apply=%region_5.0 | all-reduce | flops 513 | bytes 4104 | tf_op jit(solution)/shard_map/psum | solution.py:111
  201.5 94.9 %all-reduce = (f32[256]{0:T(256)S(1)}, f32[256]{0:T(256)S(1)}) all-reduce(f32[256]{0:T(256)S(1)} %get-tuple-element.39, f32[256]{0:T(256)S(1)} %get-tuple-element.38), channel_id=1, replica_groups=mesh['dp'=16,'space'=32] {'dp','space'}, use_global_device_ids=true, to_apply=%region_9.0 | all-reduce | flops 512 | bytes 4096 | tf_op jit(solution)/shard_map/psum | solution.py:136
  298.0 4.5 collective-permute-start.6
  302.5 3.9 collective-permute-start.7
  312.6 4.3 reshape.205
  316.9 4.0 copy.317
  324.3 8.3 %copy.342 = f32[2,14,14,32,8]{3,4,2,1,0:T(8,128)} copy(f32[2,14,14,32,8]{4,0,3,2,1:T(2,128)} %get-tuple-element.95) | data formatting | bytes 802816 | tf_op jit(solution)/shard_map/conv_general_dilated | solution.py:57
  336.9 4.3 reshape.191
  350.5 4.1 copy.335
  358.2 3.4 copy.334
  382.3 3.7 reshape.195
  396.5 3.3 reshape.193
  407.0 5.0 reshape.206
  427.9 7.3 copy.314
  435.1 25.7 %convolution_convert_fusion = bf16[2,14,14,32,8]{4,0,3,2,1:T(2,128)(2,1)} fusion(bf16[2,16,16,32,8]{4,0,3,2,1:T(2,128)(2,1)} %copy.314, bf16[3,3,8,32,8]{4,3,2,1,0:T(8,128)(2,1)S(1)} %copy-done.13), kind=kOutput, calls=%fused_computation.3 | convolution fusion | flops 14551040 | bytes 499712 | tf_op jit(solution)/shard_map/conv_general_dilated | solution.py:57
  460.9 11.2 %copy.316 = bf16[2,14,14,32,8]{2,1,0,4,3:T(8,128)(2,1)S(1)} copy(bf16[2,14,14,32,8]{4,0,3,2,1:T(2,128)(2,1)} %convolution_convert_fusion) | data formatting | bytes 401408 | tf_op jit(solution)/shard_map/convert_element_type | solution.py:146
  472.1 3.3 convert_element_type.136
  477.6 267.3 %all-reduce.5.cloned.1.call-done = (f32[256,256]{0,1:T(8,128)}, f32[3,3,8,256]{3,2,1,0:T(8,128)}, f32[256,512]{1,0:T(8,128)}) async-done(((f32[256,256]{0,1:T(8,128)}, f32[3,3,8,256]{3,2,1,0:T(8,128)}, f32[256,512]{1,0:T(8,128)}), (f32[256,256]{0,1:T(8,128)}, f32[3,3,8,256]{3,2,1,0:T(8,128)}, f32[256,512]{1,0:T(8,128)})) %all-reduce.5.cloned.1.call-update) | async-done | bytes 860176 | tf_op jit(solution)/shard_map/psum | solution.py:159
  (330 shorter events, 127.0 us)
Async XLA Ops:
  7.2 193.9 %copy-start = (bf16[256,512]{1,0:T(8,128)(2,1)S(1)}, bf16[256,512]{1,0:T(8,128)(2,1)}, u32[]{:S(2)}) copy-start(bf16[256,512]{1,0:T(8,128)(2,1)} %param.16) | copy-start | bytes 786436
  7.2 19.2 %copy-start.27 = (s32[1,2,14,14]{3,1,2,0:T(2,128)S(1)}, s32[1,2,14,14]{3,1,2,0:T(2,128)}, u32[]{:S(2)}) copy-start(s32[1,2,14,14]{3,1,2,0:T(2,128)} %param.10) | copy-start | bytes 4708
  7.2 20.2 %copy-start.9 = (bf16[1,2,14,14,512]{4,1,3,2,0:T(2,128)(2,1)S(1)}, bf16[1,2,14,14,512]{4,1,3,2,0:T(2,128)(2,1)}, u32[]{:S(2)}) copy-start(bf16[1,2,14,14,512]{4,1,3,2,0:T(2,128)(2,1)} %param.17) | copy-start | bytes 1204228
  7.2 737.7 %all-reduce.5.cloned.1.call-start = ((), (), s32[]{:S(2)}) async-start(), calls=%async_computation | async-start | bytes 1720320 | tf_op jit(solution)/shard_map/psum | solution.py:159
  10.2 19.6 %copy-start.3 = (bf16[2,14,14,256]{3,2,1,0:T(8,128)(2,1)}, bf16[2,14,14,256]{3,2,1,0:T(8,128)(2,1)S(1)}, u32[]{:S(2)}) copy-start(bf16[2,14,14,256]{3,2,1,0:T(8,128)(2,1)S(1)} %reshape.180) | copy-start | bytes 602116
  10.4 29.6 %collective-permute-start = (bf16[2,4,14,256]{3,2,1,0:T(8,128)(2,1)S(1)}, bf16[2,4,14,256]{3,2,1,0:T(8,128)(2,1)}, u32[]{:S(2)}, u32[]{:S(2)}) collective-permute-start(bf16[2,4,14,256]{3,2,1,0:T(8,128)(2,1)S(1)} %pad_maximum_fusion.4), channel_id=1, source_target_pairs={{0,3},{1,4},{2,5},{3,6},{4,7},{5,8},{6,9},{7,10},{8,11},{9,12},{10... | collective-permute-start | bytes 172040 | tf_op jit(solution)/shard_map/ppermute | solution.py:15
  16.6 25.5 %collective-permute-start.1 = (bf16[2,4,14,256]{3,2,1,0:T(8,128)(2,1)S(1)}, bf16[2,4,14,256]{3,2,1,0:T(8,128)(2,1)}, u32[]{:S(2)}, u32[]{:S(2)}) collective-permute-start(bf16[2,4,14,256]{3,2,1,0:T(8,128)(2,1)S(1)} %pad_maximum_fusion.4), channel_id=1, source_target_pairs={{0,2},{1,3},{2,4},{3,5},{4,6},{5,7},{6,8},{7,9},{8,10},{9,11},{10,... | collective-permute-start | bytes 172040 | tf_op jit(solution)/shard_map/ppermute | solution.py:15
  19.8 23.1 %collective-permute-start.2 = (bf16[2,4,14,256]{3,2,1,0:T(8,128)(2,1)S(1)}, bf16[2,4,14,256]{3,2,1,0:T(8,128)(2,1)}, u32[]{:S(2)}, u32[]{:S(2)}) collective-permute-start(bf16[2,4,14,256]{3,2,1,0:T(8,128)(2,1)S(1)} %pad_maximum_fusion.4), channel_id=1, source_target_pairs={{0,1},{1,2},{2,3},{3,4},{4,5},{5,6},{6,7},{7,8},{8,9},{9,10},{10,1... | collective-permute-start | bytes 172040 | tf_op jit(solution)/shard_map/ppermute | solution.py:15
  21.8 22.1 %collective-permute-start.3 = (bf16[2,4,14,256]{3,2,1,0:T(8,128)(2,1)S(1)}, bf16[2,4,14,256]{3,2,1,0:T(8,128)(2,1)}, u32[]{:S(2)}, u32[]{:S(2)}) collective-permute-start(bf16[2,4,14,256]{3,2,1,0:T(8,128)(2,1)S(1)} %pad_maximum_fusion.4), channel_id=1, source_target_pairs={{1,0},{2,1},{3,2},{4,3},{5,4},{6,5},{7,6},{8,7},{9,8},{10,9},{11,1... | collective-permute-start | bytes 172040 | tf_op jit(solution)/shard_map/ppermute | solution.py:15
  24.9 19.8 %collective-permute-start.4 = (bf16[2,4,14,256]{3,2,1,0:T(8,128)(2,1)S(1)}, bf16[2,4,14,256]{3,2,1,0:T(8,128)(2,1)S(1)}, u32[]{:S(2)}, u32[]{:S(2)}) collective-permute-start(bf16[2,4,14,256]{3,2,1,0:T(8,128)(2,1)S(1)} %pad_maximum_fusion.4), channel_id=1, source_target_pairs={{2,0},{3,1},{4,2},{5,3},{6,4},{7,5},{8,6},{9,7},{10,8},{11,9},{12,... | collective-permute-start | bytes 172040 | tf_op jit(solution)/shard_map/ppermute | solution.py:15
  37.9 24.5 %copy-start.12 = (bf16[3,3,8,32,8]{4,3,2,1,0:T(8,128)(2,1)}, bf16[3,3,8,32,8]{4,3,2,1,0:T(8,128)(2,1)S(1)}, u32[]{:S(2)}) copy-start(bf16[3,3,8,32,8]{4,3,2,1,0:T(8,128)(2,1)S(1)} %shard_map.138) | copy-start | bytes 110596
  40.0 7.2 collective-permute-start.5
  89.4 111.7 %copy-start.15 = (bf16[2,14,14,512]{3,0,2,1:T(2,128)(2,1)S(1)}, bf16[2,14,14,512]{3,0,2,1:T(2,128)(2,1)}, u32[]{:S(2)}) copy-start(bf16[2,14,14,512]{3,0,2,1:T(2,128)(2,1)} %bitcast_multiply_fusion) | copy-start | bytes 1204228
  296.4 20.5 %copy-start.40 = (f32[256]{0:T(256)}, f32[256]{0:T(256)S(1)}, u32[]{:S(2)}) copy-start(f32[256]{0:T(256)S(1)} %get-tuple-element.108) | copy-start | bytes 3076
  296.4 20.5 %copy-start.41 = (f32[256]{0:T(256)}, f32[256]{0:T(256)S(1)}, u32[]{:S(2)}) copy-start(f32[256]{0:T(256)S(1)} %get-tuple-element.109) | copy-start | bytes 3076
  297.2 23.7 %copy-start.16 = (bf16[2,1,14,256]{3,2,1,0:T(8,128)(2,1)}, bf16[2,1,14,256]{3,2,1,0:T(8,128)(2,1)S(1)}, u32[]{:S(2)}) copy-start(bf16[2,1,14,256]{3,2,1,0:T(8,128)(2,1)S(1)} %get-tuple-element.78) | copy-start | bytes 43012
  297.3 23.6 %copy-start.18 = (bf16[2,1,14,256]{3,2,1,0:T(8,128)(2,1)}, bf16[2,1,14,256]{3,2,1,0:T(8,128)(2,1)S(1)}, u32[]{:S(2)}) copy-start(bf16[2,1,14,256]{3,2,1,0:T(8,128)(2,1)S(1)} %copy.303) | copy-start | bytes 43012
  298.0 117.0 %collective-permute-start.6 = (bf16[2,4,14,256]{3,2,1,0:T(8,128)(2,1)}, bf16[2,4,14,256]{3,2,1,0:T(8,128)(2,1)}, u32[]{:S(2)}, u32[]{:S(2)}) collective-permute-start(bf16[2,4,14,256]{3,2,1,0:T(8,128)(2,1)} %pad_maximum_fusion.5), channel_id=1, source_target_pairs={{0,3},{1,4},{2,5},{3,6},{4,7},{5,8},{6,9},{7,10},{8,11},{9,12},{10... | collective-permute-start | bytes 172040 | tf_op jit(solution)/shard_map/ppermute | solution.py:15
  302.5 114.8 %collective-permute-start.7 = (bf16[2,4,14,256]{3,2,1,0:T(8,128)(2,1)}, bf16[2,4,14,256]{3,2,1,0:T(8,128)(2,1)}, u32[]{:S(2)}, u32[]{:S(2)}) collective-permute-start(bf16[2,4,14,256]{3,2,1,0:T(8,128)(2,1)} %pad_maximum_fusion.5), channel_id=1, source_target_pairs={{0,2},{1,3},{2,4},{3,5},{4,6},{5,7},{6,8},{7,9},{8,10},{9,11},{10,... | collective-permute-start | bytes 172040 | tf_op jit(solution)/shard_map/ppermute | solution.py:15
  306.3 111.8 %collective-permute-start.8 = (bf16[2,4,14,256]{3,2,1,0:T(8,128)(2,1)}, bf16[2,4,14,256]{3,2,1,0:T(8,128)(2,1)}, u32[]{:S(2)}, u32[]{:S(2)}) collective-permute-start(bf16[2,4,14,256]{3,2,1,0:T(8,128)(2,1)} %pad_maximum_fusion.5), channel_id=1, source_target_pairs={{0,1},{1,2},{2,3},{3,4},{4,5},{5,6},{6,7},{7,8},{8,9},{9,10},{10,1... | collective-permute-start | bytes 172040 | tf_op jit(solution)/shard_map/ppermute | solution.py:15
  308.3 110.8 %collective-permute-start.9 = (bf16[2,4,14,256]{3,2,1,0:T(8,128)(2,1)}, bf16[2,4,14,256]{3,2,1,0:T(8,128)(2,1)}, u32[]{:S(2)}, u32[]{:S(2)}) collective-permute-start(bf16[2,4,14,256]{3,2,1,0:T(8,128)(2,1)} %pad_maximum_fusion.5), channel_id=1, source_target_pairs={{1,0},{2,1},{3,2},{4,3},{5,4},{6,5},{7,6},{8,7},{9,8},{10,9},{11,1... | collective-permute-start | bytes 172040 | tf_op jit(solution)/shard_map/ppermute | solution.py:15
  311.3 108.6 %collective-permute-start.10 = (bf16[2,4,14,256]{3,2,1,0:T(8,128)(2,1)}, bf16[2,4,14,256]{3,2,1,0:T(8,128)(2,1)}, u32[]{:S(2)}, u32[]{:S(2)}) collective-permute-start(bf16[2,4,14,256]{3,2,1,0:T(8,128)(2,1)} %pad_maximum_fusion.5), channel_id=1, source_target_pairs={{2,0},{3,1},{4,2},{5,3},{6,4},{7,5},{8,6},{9,7},{10,8},{11,9},{12,... | collective-permute-start | bytes 172040 | tf_op jit(solution)/shard_map/ppermute | solution.py:15
  415.0 7.3 collective-permute-start.11
  475.5 274.6 %copy-start.1 = (bf16[256,512]{1,0:T(8,128)(2,1)S(1)}, bf16[256,512]{1,0:T(8,128)(2,1)}, u32[]{:S(2)}) copy-start(bf16[256,512]{1,0:T(8,128)(2,1)} %param.16) | copy-start | bytes 786436
  (50 other events, 339.3 us)
Sparse Core Ops, SparseCore 0:
  476.5 268.3 all-reduce.4
where the time goes:
time: 765 us; the launch traced here: 757 us
  waiting for transfers between devices  271 us (35%)
  blocking collectives  200 us (26%)
  local copies, waits for them, and re-layouts  170 us (22%)
  matrix products  55.9 us (7%)
  starting transfers between devices  33.1 us (4%)
  between operations  15.8 us (2%)
  other arithmetic  10.5 us (1%)
    psum x1, waiting for transfers between devices, body(): lax.psum((reduce_grad, expand_grad, group_grad), ('dp', 'space'))  267 us
    psum x1, blocking collectives, body(): lax.psum((jnp.sum(tissue_weight * pre_norm, axis=(0, 1, 2)), jnp.sum(tiss...  105 us
    psum x1, blocking collectives, body(): lax.psum((jnp.sum(before_grad * normed, axis=(0, 1, 2)), jnp.sum(before_g...  94.9 us
    conv_general_dilated x2, matrix products, grouped(): lax.conv_general_dilated(padded, kernel, (1, 1), 'VALID', dimension_numbe...  46 us
    ppermute x12, starting transfers between devices, passed_along(): return lax.ppermute(block, axis, route)  33.1 us
    slice x10, local copies, waits for them, and re-layouts, kernel_grad(): padded[:, row_tap:row_tap + side, col_tap:col_tap + side, :]  27.7 us
    reshape x8, local copies, waits for them, and re-layouts, kernel_grad(): padded[:, row_tap:row_tap + side, col_tap:col_tap + side, :]  27.2 us
    conv_general_dilated x3, local copies, waits for them, and re-layouts, grouped(): lax.conv_general_dilated(padded, kernel, (1, 1), 'VALID', dimension_numbe...  20.5 us
  transfers between devices with their start and end apart: 13, of which 3 were waited for; matrix products, arithmetic and copies ran while one was open for 16% of the time, Pallas kernels for 0%

commit v1 on v0

v1 whole, which is shorter than its diff:
```python
import functools

import jax
import jax.numpy as jnp
from jax import lax
from jax.experimental import pallas as pl
from jax.experimental.pallas import tpu as pltpu
from jax.sharding import PartitionSpec as P

EPS = 1e-05
SIDE = 14
WIDE = 16
TILE_ROWS = SIDE * WIDE
ROWS = 2 * TILE_ROWS
EXT = WIDE * WIDE
CH = 256
OUT = 512
F32 = jnp.float32
BF16 = jnp.bfloat16

VMEM = pl.BlockSpec(memory_space=pltpu.VMEM)
SMEM = pl.BlockSpec(memory_space=pltpu.SMEM)
PARAMS = pltpu.CompilerParams(vmem_limit_bytes=24 * 1024 * 1024)


def call(kernel, outs, specs, scratch=()):
    return pl.pallas_call(
        kernel,
        out_shape=outs,
        in_specs=specs,
        out_specs=jax.tree.map(lambda _: VMEM, outs),
        scratch_shapes=scratch,
        compiler_params=PARAMS,
    )


def shape(dims, kind):
    return jax.ShapeDtypeStruct(dims, kind)


def dot(a, b, dims=((1,), (0,))):
    return lax.dot_general(a, b, (dims, ((), ())), preferred_element_type=F32)


def iota(dims, axis):
    return lax.broadcasted_iota(jnp.int32, dims, axis)


def rims_of(values, top_ref, bottom_ref):
    for t in range(2):
        first = t * TILE_ROWS
        last = first + TILE_ROWS - WIDE
        top_ref[t * WIDE : (t + 1) * WIDE] = values[first : first + WIDE]
        bottom_ref[t * WIDE : (t + 1) * WIDE] = values[last : last + WIDE]


def strips(values, up, down):
    out = []
    for t in range(2):
        out.append(
            jnp.concatenate(
                [
                    up[t * WIDE : (t + 1) * WIDE],
                    values[t * TILE_ROWS : (t + 1) * TILE_ROWS],
                    down[t * WIDE : (t + 1) * WIDE],
                ],
                axis=0,
            )
        )
    return out


def column_kernel(odd_ref, values_ref, up_ref, down_ref, column_ref):
    left, right = strips(values_ref[...], up_ref[...], down_ref[...])
    row = iota((WIDE, EXT), 0)
    place = iota((WIDE, EXT), 1)
    odd = odd_ref[0] == 1
    wanted = row * WIDE + jnp.where(odd, 0, SIDE - 1)
    pick = (place == wanted).astype(F32).astype(BF16)
    from_left = dot(pick, left)
    from_right = dot(pick, right)
    column_ref[...] = jnp.where(odd, from_left, from_right).astype(BF16)


def extended(values, up, down, side, links_ref):
    left, right = strips(values.astype(F32), up.astype(F32), down.astype(F32))
    r = iota((EXT, CH), 0) // WIDE
    c = iota((EXT, CH), 0) % WIDE
    spread_row = iota((EXT, WIDE), 0) // WIDE
    spread = (spread_row == iota((EXT, WIDE), 1)).astype(F32).astype(BF16)
    side_rows = dot(spread, side)

    def gate(t, first, middle, last):
        def on(k):
            return (links_ref[0, t, k] >= 0).astype(jnp.int32)

        level = jnp.where(r == 0, on(first), jnp.where(r == WIDE - 1, on(last), on(middle)))
        return level > 0

    out = []
    for t, own, other in ((0, left, right), (1, right, left)):
        keep = jnp.where(r == 0, (links_ref[0, t, 0] >= 0).astype(jnp.int32), 1)
        keep = jnp.where(r == WIDE - 1, (links_ref[0, t, 1] >= 0).astype(jnp.int32), keep)
        centre = pltpu.roll(jnp.where(keep > 0, own, 0.0), 1, 0)
        at_left = side_rows if t == 0 else pltpu.roll(other, EXT - (SIDE - 1), 0)
        at_right = pltpu.roll(other, WIDE - 1, 0) if t == 0 else side_rows
        value = jnp.where(c == 0, jnp.where(gate(t, 4, 2, 6), at_left, 0.0), centre)
        value = jnp.where(c == WIDE - 1, jnp.where(gate(t, 5, 3, 7), at_right, 0.0), value)
        out.append(value)
    return out


def shifted(tiles):
    moved = []
    for b in range(3):
        moved.append([(t if b == 0 else pltpu.roll(t, EXT - b, 0)).astype(BF16) for t in tiles])
    return moved


def window(moved, a, b):
    return jnp.concatenate([t[a * WIDE : a * WIDE + TILE_ROWS] for t in moved[b]], axis=0)


def reduce_kernel(act_ref, w_ref, tissue_ref, values_ref, top_ref, bottom_ref, mask_ref, wide):
    wide[...] = jnp.zeros_like(wide)
    wide[:, :, :SIDE, :] = act_ref[0]
    values = dot(wide[...].reshape(ROWS, CH), w_ref[...]).astype(BF16)
    values_ref[...] = values
    rims_of(values, top_ref, bottom_ref)
    row = iota((TILE_ROWS, SIDE), 0) // WIDE
    pick = (row == iota((TILE_ROWS, SIDE), 1)).astype(F32).astype(BF16)
    col = iota((TILE_ROWS, SIDE), 0) % WIDE
    here = col == iota((TILE_ROWS, SIDE), 1)
    ones = jnp.ones((SIDE, 128), BF16)
    for t in range(2):
        rows = dot(pick, tissue_ref[0, t].astype(F32).astype(BF16))
        mask_ref[t * TILE_ROWS : (t + 1) * TILE_ROWS] = dot(
            jnp.where(here, rows, 0.0).astype(BF16), ones
        )


def spread_kernel(group_ref, dense_ref):
    same = iota((CH, CH), 0) // 8 == iota((CH, CH), 1) // 8
    for tap in range(9):
        taps = group_ref[tap // 3, tap % 3].astype(F32)
        full = jnp.concatenate([taps] * (CH // 8), axis=0)
        dense_ref[tap] = jnp.where(same, full, 0.0).astype(BF16)


def as_rows(first, second, third):
    pieces = [first[:, :128], first[:, 128:], second[:, :128], second[:, 128:], third]
    return jnp.concatenate(pieces + [jnp.zeros((3, 128), F32)], axis=0)


def per_channel(block, row):
    return jnp.concatenate([block[row : row + 1], block[row + 1 : row + 2]], axis=1)


def both(mask):
    return jnp.concatenate([mask, mask], axis=1)


def conv_kernel(
    links_ref, values_ref, up_ref, down_ref, side_ref, dense_ref, mask_ref,
    pre_ref, padded_ref, sums_ref,
):
    tiles = extended(values_ref[...], up_ref[...], down_ref[...], side_ref[...], links_ref)
    for t in range(2):
        padded_ref[t] = tiles[t].astype(BF16)
    moved = shifted(tiles)
    pre = jnp.zeros((ROWS, CH), F32)
    for a in range(3):
        for b in range(3):
            pre += dot(window(moved, a, b), dense_ref[3 * a + b])
    pre_ref[...] = pre
    mask = mask_ref[...]
    held = pre * both(mask)
    block = as_rows(
        jnp.sum(held, axis=0, keepdims=True),
        jnp.sum(held * pre, axis=0, keepdims=True),
        jnp.sum(mask, axis=0, keepdims=True),
    )
    sums_ref[...] = jnp.broadcast_to(block[None], sums_ref.shape)


def between_kernel(parts_ref, sums_ref):
    block = jnp.sum(parts_ref[...], axis=0)
    sums_ref[...] = jnp.broadcast_to(block[None], sums_ref.shape)


def moments(parts_ref):
    block = jnp.sum(parts_ref[...], axis=0)
    counted = both(block[4:5])
    centre = per_channel(block, 0) / counted
    spread = per_channel(block, 2) / counted - centre * centre
    return centre, lax.rsqrt(spread + EPS), counted


def head_kernel(
    parts_ref, pre_ref, mask_ref, gain_ref, bias_ref, expand_ref, cot_ref,
    before_ref, expand_grad_ref, sums_ref, wide,
):
    wide[...] = jnp.zeros_like(wide)
    wide[:, :, :SIDE, :] = cot_ref[0]
    mask = mask_ref[...]
    keep = jnp.concatenate([mask] * (OUT // 128), axis=1) > 0
    out_grad = jnp.where(keep, wide[...].reshape(ROWS, OUT).astype(F32), 0.0).astype(BF16)
    centre, inverse, _ = moments(parts_ref)
    normed = (pre_ref[...] - centre) * inverse
    before = gain_ref[...] * normed + bias_ref[...]
    sigma = jax.nn.sigmoid(before)
    hidden = (before * sigma).astype(BF16)
    expand_grad_ref[...] = dot(hidden, out_grad, ((0,), (0,)))
    hidden_grad = dot(out_grad, expand_ref[...], ((1,), (1,)))
    before_grad = hidden_grad * sigma * (1.0 + before * (1.0 - sigma))
    before_ref[...] = before_grad
    block = as_rows(
        jnp.sum(before_grad * normed, axis=0, keepdims=True),
        jnp.sum(before_grad, axis=0, keepdims=True),
        jnp.zeros((1, 128), F32),
    )
    sums_ref[...] = jnp.broadcast_to(block[None], sums_ref.shape)


def norm_kernel(
    parts_ref, totals_ref, pre_ref, mask_ref, gain_ref, before_ref,
    grad_ref, top_ref, bottom_ref, gain_grad_ref, bias_grad_ref,
):
    centre, inverse, counted = moments(parts_ref)
    totals = jnp.sum(totals_ref[...], axis=0)
    gain_grad = per_channel(totals, 0)
    bias_grad = per_channel(totals, 2)
    gain_grad_ref[...] = gain_grad
    bias_grad_ref[...] = bias_grad
    normed = (pre_ref[...] - centre) * inverse
    taken = both(mask_ref[...]) * (bias_grad + normed * gain_grad) / counted
    grad = (gain_ref[...] * inverse * (before_ref[...] - taken)).astype(BF16)
    grad_ref[...] = grad
    rims_of(grad, top_ref, bottom_ref)


def back_kernel(
    links_ref, grad_ref, up_ref, down_ref, side_ref, dense_ref, padded_ref, act_ref, w_ref,
    expand_grad_ref, input_grad_ref, packed_ref, wide,
):
    wide[...] = jnp.zeros_like(wide)
    wide[:, :, :SIDE, :] = act_ref[0]
    act = wide[...].reshape(ROWS, CH)
    grad = grad_ref[...]
    moved = shifted(extended(grad, up_ref[...], down_ref[...], side_ref[...], links_ref))
    reduced = jnp.zeros((ROWS, CH), F32)
    for a in range(3):
        for b in range(3):
            reduced += dot(window(moved, a, b), dense_ref[8 - 3 * a - b], ((1,), (1,)))
    in_tile = iota((ROWS, CH), 0) % WIDE < SIDE
    reduced = jnp.where(in_tile, reduced, 0.0).astype(BF16)
    input_grad = dot(reduced, w_ref[...], ((1,), (1,))).astype(BF16)
    input_grad_ref[0] = input_grad.reshape(2, SIDE, WIDE, CH)[:, :, :SIDE, :]
    reduce_grad = dot(act, reduced, ((0,), (0,))).astype(BF16)
    packed_ref[:CH, :128] = reduce_grad[:, :128]
    packed_ref[CH:, :128] = reduce_grad[:, 128:]
    expand_grad = expand_grad_ref[...].astype(BF16)
    packed_ref[:CH, 128:256] = expand_grad[:, :128]
    packed_ref[CH:, 128:256] = expand_grad[:, 128:256]
    packed_ref[:CH, 256:384] = expand_grad[:, 256:384]
    packed_ref[CH:, 256:384] = expand_grad[:, 384:]
    lowered = []
    for a in range(3):
        parts = []
        for t in range(2):
            own = grad[t * TILE_ROWS : (t + 1) * TILE_ROWS]
            if a:
                parts.append(jnp.zeros((a * WIDE, CH), BF16))
            parts.append(own)
            if a < 2:
                parts.append(jnp.zeros(((2 - a) * WIDE, CH), BF16))
        lowered.append(jnp.concatenate(parts, axis=0))
    lowered = jnp.concatenate(lowered, axis=1)
    windows = shifted([padded_ref[t].astype(F32) for t in range(2)])
    same = iota((CH, CH), 0) // 8 == iota((CH, CH), 1) // 8
    taps = [None] * 9
    for b in range(3):
        product = dot(jnp.concatenate(windows[b], axis=0), lowered, ((0,), (0,)))
        for a in range(3):
            own = jnp.where(same, product[:, a * CH : (a + 1) * CH], 0.0)
            taps[3 * a + b] = jnp.sum(own.reshape(CH // 8, 8, CH), axis=0)
    group = jnp.concatenate(taps + [jnp.zeros((CH - 72, CH), F32)], axis=0).astype(BF16)
    packed_ref[:CH, 384:] = group[:, :128]
    packed_ref[CH:, 384:] = group[:, 128:]


def total_kernel(parts_ref, total_ref):
    ones = jnp.ones(total_ref.shape[:1] + parts_ref.shape[:1], BF16)
    total_ref[...] = dot(ones, parts_ref[...]).astype(BF16)


def unpack_kernel(packed_ref, reduce_ref, group_ref, expand_ref):
    packed = packed_ref[...].astype(F32)
    reduce_ref[:, :128] = packed[:CH, :128]
    reduce_ref[:, 128:] = packed[CH:, :128]
    expand_ref[:, :128] = packed[:CH, 128:256]
    expand_ref[:, 128:256] = packed[CH:, 128:256]
    expand_ref[:, 256:384] = packed[:CH, 256:384]
    expand_ref[:, 384:] = packed[CH:, 256:384]
    group_ref[:, :128] = packed[:72, 384:]
    group_ref[:, 128:] = packed[CH : CH + 72, 384:]


def body(
    sizes, activations, tissue, neighbours, w_reduce, w_group, norm_gain, norm_bias, w_expand,
    cotangent,
):
    dp, space = sizes
    everyone = ("dp", "space")
    odd = (lax.axis_index("space") % 2).astype(jnp.int32).reshape(1)
    gain = norm_gain.reshape(1, CH)
    bias = norm_bias.reshape(1, CH)
    rim = shape((2 * WIDE, CH), BF16)
    flat = shape((ROWS, CH), BF16)

    def halo(values, top, bottom):
        up = lax.ppermute(bottom, "space", [(i, i + 2) for i in range(space - 2)])
        down = lax.ppermute(top, "space", [(i + 2, i) for i in range(space - 2)])
        column = call(
            column_kernel, shape((WIDE, CH), BF16), [SMEM, VMEM, VMEM, VMEM]
        )(odd, values, up, down)
        side = lax.ppermute(column, "space", [(i, i ^ 1) for i in range(space)])
        return up, down, side

    def summed(blocks):
        parts = lax.all_to_all(blocks, "space", 0, 0)
        blocks = call(between_kernel, shape((dp, 8, 128), F32), [VMEM])(parts)
        return lax.all_to_all(blocks, "dp", 0, 0)

    values, top, bottom, mask = call(
        reduce_kernel,
        (flat, rim, rim, shape((ROWS, 128), F32)),
        [VMEM] * 3,
        [pltpu.VMEM((2, SIDE, WIDE, CH), BF16)],
    )(activations, w_reduce, tissue)
    dense = call(spread_kernel, shape((9, CH, CH), BF16), [VMEM])(w_group)
    up, down, side = halo(values, top, bottom)
    blocks = shape((space, 8, 128), F32)
    pre, padded, sums = call(
        conv_kernel,
        (shape((ROWS, CH), F32), shape((2, EXT, CH), BF16), blocks),
        [SMEM] + [VMEM] * 6,
    )(neighbours, values, up, down, side, dense, mask)
    parts = summed(sums)
    before_grad, expand_grad, sums = call(
        head_kernel,
        (shape((ROWS, CH), F32), shape((CH, OUT), F32), blocks),
        [VMEM] * 7,
        [pltpu.VMEM((2, SIDE, WIDE, OUT), BF16)],
    )(parts, pre, mask, gain, bias, w_expand, cotangent)
    totals = summed(sums)
    grad, top, bottom, gain_grad, bias_grad = call(
        norm_kernel,
        (flat, rim, rim, shape((1, CH), F32), shape((1, CH), F32)),
        [VMEM] * 6,
    )(parts, totals, pre, mask, gain, before_grad)
    up, down, side = halo(grad, top, bottom)
    count = dp * space
    input_grad, packed = call(
        back_kernel,
        (shape((1, 2, SIDE, SIDE, CH), BF16), shape((2 * CH, 4 * 128), BF16)),
        [SMEM] + [VMEM] * 9,
        [pltpu.VMEM((2, SIDE, WIDE, CH), BF16)],
    )(neighbours, grad, up, down, side, dense, padded, activations, w_reduce, expand_grad)
    share = packed.size // count
    received = lax.all_to_all(packed.reshape(count, 1, share), everyone, 0, 0)
    total = call(total_kernel, shape((count, share), BF16), [VMEM])(
        received.reshape(count, share)
    )
    gathered = lax.all_to_all(total.reshape(count, 1, share), everyone, 0, 0)
    reduce_grad, group_grad, expand_grad = call(
        unpack_kernel,
        (shape((CH, CH), F32), shape((72, CH), F32), shape((CH, OUT), F32)),
        [VMEM],
    )(gathered.reshape(packed.shape))
    return (
        input_grad,
        reduce_grad,
        group_grad.reshape(3, 3, 8, CH),
        gain_grad.reshape(CH),
        bias_grad.reshape(CH),
        expand_grad,
    )


def solution(mesh):
    sizes = (mesh.shape["dp"], mesh.shape["space"])
    return jax.shard_map(
        functools.partial(body, sizes),
        mesh=mesh,
        in_specs=(
            P("dp", "space", None, None, None),
            P("dp", "space", None, None),
            P("dp", "space", None),
            P(),
            P(),
            P(),
            P(),
            P(),
            P("dp", "space", None, None, None),
        ),
        out_specs=(P("dp", "space", None, None, None), P(), P(), P(), P(), P()),
        check_vma=False,
    )
```

time: 765 us -> 174 us (0.23)
  waiting for transfers between devices: 271 us -> 36.7 us
  local copies, waits for them, and re-layouts: 170 us -> 7.99 us
  blocking collectives: 200 us -> 73.7 us
  matrix products: 55.9 us -> 0 us
  between operations: 15.8 us -> 0.89 us
  starting transfers between devices: 33.1 us -> 42.9 us
  Pallas kernels: 0 us -> 8.83 us
  other arithmetic: 10.5 us -> 2.06 us
    psum x1 -> x0, waiting for transfers between devices: 267 us -> none  [body(): lax.psum((reduce_grad, expand_grad, group_grad), ('dp', 'space'))]
    psum x2 -> x0, blocking collectives: 200 us -> none  [the longest x1 105 us: body(): lax.psum((jnp.sum(tissue_weight * pre_norm, axis=(0, 1, 2)), jnp.sum(tiss...]
    all_to_all x0 -> x4, blocking collectives: none -> 73.7 us  [the longest x1 32.2 us: body(): received = lax.all_to_all(packed.reshape(count, 1, share), everyone, 0, 0)]
    conv_general_dilated x2 -> x0, matrix products: 46 us -> none  [grouped(): lax.conv_general_dilated(padded, kernel, (1, 1), 'VALID', dimension_numbe...]
    reshape x22 -> x1, local copies, waits for them, and re-layouts: 34.8 us -> 0.51 us  [body(): received = lax.all_to_all(packed.reshape(count, 1, share), everyone, 0, 0)]
    concatenate x41 -> x0, local copies, waits for them, and re-layouts: 34.1 us -> none  [the longest x12 16.2 us: extend(): jnp.concatenate([left_side[:, :, None], values, right_side[:, :, None]],...]
    slice x27 -> x0, local copies, waits for them, and re-layouts: 31.6 us -> none  [the longest x10 27.7 us: kernel_grad(): padded[:, row_tap:row_tap + side, col_tap:col_tap + side, :]]
    all_to_all x0 -> x2, waiting for transfers between devices: none -> 29.5 us  [the longest x1 21.7 us: body(): gathered = lax.all_to_all(total.reshape(count, 1, share), everyone, 0, 0)]
  transfers between devices with their start and end apart: 13 -> 8, of which waited for: 3 -> 5; matrix products, arithmetic and copies ran while one was open for 16% -> 1% of each run, Pallas kernels for 0% -> 0%
where the time goes in v1:
time: 174 us; the launch traced here: 173 us
  blocking collectives  73.7 us (42%)
  starting transfers between devices  42.9 us (25%)
  waiting for transfers between devices  36.7 us (21%)
  Pallas kernels  8.83 us (5%)
  local copies, waits for them, and re-layouts  7.99 us (5%)
  other arithmetic  2.06 us (1%)
    all_to_all x1, blocking collectives, body(): received = lax.all_to_all(packed.reshape(count, 1, share), everyone, 0, 0)  32.2 us
    all_to_all x2, blocking collectives, summed(): parts = lax.all_to_all(blocks, 'space', 0, 0)  30.1 us
    all_to_all x1, waiting for transfers between devices, body(): gathered = lax.all_to_all(total.reshape(count, 1, share), everyone, 0, 0)  21.7 us
    ppermute x2, starting transfers between devices, halo(): side = lax.ppermute(column, 'space', [(i, i ^ 1) for i in range(space)])  13.4 us
    all_to_all x1, starting transfers between devices, summed(): return lax.all_to_all(blocks, 'dp', 0, 0)  11.7 us
    all_to_all x1, blocking collectives, summed(): return lax.all_to_all(blocks, 'dp', 0, 0)  11.5 us
    all_to_all x1, starting transfers between devices, body(): gathered = lax.all_to_all(total.reshape(count, 1, share), everyone, 0, 0)  8.88 us
    all_to_all x1, waiting for transfers between devices, summed(): return lax.all_to_all(blocks, 'dp', 0, 0)  7.86 us
  transfers between devices with their start and end apart: 8, of which 5 were waited for; matrix products, arithmetic and copies ran while one was open for 1% of the time, Pallas kernels for 0%

profile of v1, /device:TPU:1, one launch (start us, length us, event | category | flops | bytes accessed | tf_op | source)
XLA Modules:
  0.0 173.1 jit_solution(3089695033983825238)
XLA Ops:
  0.6 1.0 copy.27.act_ref
  3.7 4.0 %collective-permute-start = (bf16[32,256]{1,0:T(8,128)(2,1)S(1)}, bf16[32,256]{1,0:T(8,128)(2,1)S(1)}, u32[]{:S(2)}, u32[]{:S(2)}) collective-permute-start(bf16[32,256]{1,0:T(8,128)(2,1)S(1)} %get-tuple-element.27), channel_id=1, source_target_pairs={{0,2},{1,3},{2,4},{3,5},{4,6},{5,7},{6,8},{7,9},{8,10},{9,11},{10,... | collective-permute-start | bytes 49160 | tf_op jit(solution)/shard_map/ppermute | solution.py:322
  7.7 1.3 collective-permute-start.1
  9.0 3.2 %collective-permute-done.1.down_ref = bf16[32,256]{1,0:T(8,128)(2,1)S(1)} collective-permute-done((bf16[32,256]{1,0:T(8,128)(2,1)S(1)}, bf16[32,256]{1,0:T(8,128)(2,1)S(1)}, u32[]{:S(2)}, u32[]{:S(2)}) %collective-permute-start.1) | collective-permute-done | bytes 16416 | tf_op jit(solution)/shard_map/ppermute | solution.py:323
  12.3 7.2 %collective-permute-start.2 = (bf16[16,256]{1,0:T(8,128)(2,1)S(1)}, bf16[16,256]{1,0:T(8,128)(2,1)S(1)}, u32[]{:S(2)}, u32[]{:S(2)}) collective-permute-start(bf16[16,256]{1,0:T(8,128)(2,1)S(1)} %shard_map.137), channel_id=1, source_target_pairs={{0,1},{1,0},{2,3},{3,2},{4,5},{5,4},{6,7},{7,6},{8,9},{9,8},{10,11... | collective-permute-start | bytes 24584 | tf_op jit(solution)/shard_map/ppermute | solution.py:327
  20.5 1.5 shard_map.139
  22.0 15.1 %all_to_all.30.parts_ref = f32[32,8,128]{2,1,0:T(8,128)S(1)} all-to-all(f32[32,8,128]{2,1,0:T(8,128)S(1)} %get-tuple-element.30), channel_id=1, replica_groups=mesh['dp'=16,'space'=32] {'space'}, dimensions={0} | all-to-all | bytes 262144 | tf_op jit(solution)/shard_map/all_to_all | solution.py:331
  37.8 11.7 %all-to-all-start.1 = ((f32[16,8,128]{2,1,0:T(8,128)}), f32[16,8,128]{2,1,0:T(8,128)S(1)}, u32[]{:S(2)}, u32[]{:S(2)}) async-start(f32[16,8,128]{2,1,0:T(8,128)} %shard_map.140), calls=%async_computation.1 | async-start | bytes 131072 | tf_op jit(solution)/shard_map/all_to_all | solution.py:333
  49.5 1.1 copy.29.cot_ref
  50.5 7.9 %all-to-all-done.1.parts_ref = f32[16,8,128]{2,1,0:T(8,128)S(1)} async-done(((f32[16,8,128]{2,1,0:T(8,128)}), f32[16,8,128]{2,1,0:T(8,128)S(1)}, u32[]{:S(2)}, u32[]{:S(2)}) %all-to-all-start.1) | async-done | bytes 65568 | tf_op jit(solution)/shard_map/all_to_all | solution.py:333
  59.0 15.0 %all_to_all.31.parts_ref = f32[32,8,128]{2,1,0:T(8,128)S(1)} all-to-all(f32[32,8,128]{2,1,0:T(8,128)S(1)} %get-tuple-element.32), channel_id=1, replica_groups=mesh['dp'=16,'space'=32] {'space'}, dimensions={0} | all-to-all | bytes 262144 | tf_op jit(solution)/shard_map/all_to_all | solution.py:331
  74.1 11.5 %all_to_all.32.totals_ref = f32[16,8,128]{2,1,0:T(8,128)S(1)} all-to-all(f32[16,8,128]{2,1,0:T(8,128)S(1)} %shard_map.142), channel_id=1, replica_groups=mesh['dp'=16,'space'=32] {'dp'}, dimensions={0} | all-to-all | bytes 131072 | tf_op jit(solution)/shard_map/all_to_all | solution.py:333
  86.2 2.4 %collective-permute-start.3 = (bf16[32,256]{1,0:T(8,128)(2,1)S(1)}, bf16[32,256]{1,0:T(8,128)(2,1)S(1)}, u32[]{:S(2)}, u32[]{:S(2)}) collective-permute-start(bf16[32,256]{1,0:T(8,128)(2,1)S(1)} %get-tuple-element.35), channel_id=1, source_target_pairs={{0,2},{1,3},{2,4},{3,5},{4,6},{5,7},{6,8},{7,9},{8,10},{9,11},{10,... | collective-permute-start | bytes 49160 | tf_op jit(solution)/shard_map/ppermute | solution.py:322
  88.6 1.3 collective-permute-start.4
  89.9 3.2 %collective-permute-done.4.down_ref = bf16[32,256]{1,0:T(8,128)(2,1)S(1)} collective-permute-done((bf16[32,256]{1,0:T(8,128)(2,1)S(1)}, bf16[32,256]{1,0:T(8,128)(2,1)S(1)}, u32[]{:S(2)}, u32[]{:S(2)}) %collective-permute-start.4) | collective-permute-done | bytes 16416 | tf_op jit(solution)/shard_map/ppermute | solution.py:323
  93.2 6.2 %collective-permute-start.5 = (bf16[16,256]{1,0:T(8,128)(2,1)S(1)}, bf16[16,256]{1,0:T(8,128)(2,1)S(1)}, u32[]{:S(2)}, u32[]{:S(2)}) collective-permute-start(bf16[16,256]{1,0:T(8,128)(2,1)S(1)} %shard_map.144), channel_id=1, source_target_pairs={{0,1},{1,0},{2,3},{3,2},{4,5},{5,4},{6,7},{7,6},{8,9},{9,8},{10,11... | collective-permute-start | bytes 24584 | tf_op jit(solution)/shard_map/ppermute | solution.py:327
  100.2 3.2 %shard_map.145 = (bf16[1,2,14,14,256]{4,3,2,1,0:T(8,128)(2,1)S(1)}, bf16[512,512]{1,0:T(8,128)(2,1)S(1)}) custom-call(s32[1,2,8]{2,1,0:T(2,128)S(1)} %copy-done.4, bf16[448,256]{1,0:T(8,128)(2,1)S(1)} %get-tuple-element.34.values_ref.grad_ref, bf16[32,256]{1,0:T(8,128)(2,1)S(1)} %collective-permute-done.3.up_ref, ...), custom_call_target="tpu_custom_call" | custom-call | tf_op jit(solution)/shard_map/pallas_call | solution.py:364
  103.9 1.0 reduce
  105.1 32.2 %all_to_all.33 = bf16[512,2,256]{2,1,0:T(2,128)(2,1)S(1)} all-to-all(bf16[512,2,256]{2,1,0:T(2,128)(2,1)S(1)} %reshape.52), channel_id=1, replica_groups=mesh['dp'=16,'space'=32] {'dp','space'}, dimensions={0} | all-to-all | bytes 1048576 | tf_op jit(solution)/shard_map/all_to_all | solution.py:371
  138.2 1.0 reduce.1
  139.3 0.9 reshape.54
  140.2 8.9 %all-to-all-start.5 = ((bf16[512,2,256]{2,1,0:T(2,128)(2,1)}), bf16[512,2,256]{2,1,0:T(2,128)(2,1)S(1)}, u32[]{:S(2)}, u32[]{:S(2)}) async-start(bf16[512,2,256]{2,1,0:T(2,128)(2,1)} %reshape.54), calls=%async_computation.5 | async-start | bytes 1048576 | tf_op jit(solution)/shard_map/all_to_all | solution.py:375
  150.0 21.7 %all-to-all-done.5 = bf16[512,2,256]{2,1,0:T(2,128)(2,1)S(1)} async-done(((bf16[512,2,256]{2,1,0:T(2,128)(2,1)}), bf16[512,2,256]{2,1,0:T(2,128)(2,1)S(1)}, u32[]{:S(2)}, u32[]{:S(2)}) %all-to-all-start.5) | async-done | bytes 524320 | tf_op jit(solution)/shard_map/all_to_all | solution.py:375
  172.2 1.0 shard_map.147
  (35 shorter events, 9.1 us)
Async XLA Ops:
  0.6 19.9 %copy-start.4 = (s32[1,2,8]{2,1,0:T(2,128)S(1)}, s32[1,2,8]{2,1,0:T(2,128)}, u32[]{:S(2)}) copy-start(s32[1,2,8]{2,1,0:T(2,128)} %links_ref.3) | copy-start | bytes 196
  2.3 0.9 copy-start
  3.7 5.4 %collective-permute-start = (bf16[32,256]{1,0:T(8,128)(2,1)S(1)}, bf16[32,256]{1,0:T(8,128)(2,1)S(1)}, u32[]{:S(2)}, u32[]{:S(2)}) collective-permute-start(bf16[32,256]{1,0:T(8,128)(2,1)S(1)} %get-tuple-element.27), channel_id=1, source_target_pairs={{0,2},{1,3},{2,4},{3,5},{4,6},{5,7},{6,8},{7,9},{8,10},{9,11},{10,... | collective-permute-start | bytes 49160 | tf_op jit(solution)/shard_map/ppermute | solution.py:322
  7.7 4.5 %collective-permute-start.1 = (bf16[32,256]{1,0:T(8,128)(2,1)S(1)}, bf16[32,256]{1,0:T(8,128)(2,1)S(1)}, u32[]{:S(2)}, u32[]{:S(2)}) collective-permute-start(bf16[32,256]{1,0:T(8,128)(2,1)S(1)} %get-tuple-element.28), channel_id=1, source_target_pairs={{2,0},{3,1},{4,2},{5,3},{6,4},{7,5},{8,6},{9,7},{10,8},{11,9},{12,... | collective-permute-start | bytes 49160 | tf_op jit(solution)/shard_map/ppermute | solution.py:323
  12.3 8.2 %collective-permute-start.2 = (bf16[16,256]{1,0:T(8,128)(2,1)S(1)}, bf16[16,256]{1,0:T(8,128)(2,1)S(1)}, u32[]{:S(2)}, u32[]{:S(2)}) collective-permute-start(bf16[16,256]{1,0:T(8,128)(2,1)S(1)} %shard_map.137), channel_id=1, source_target_pairs={{0,1},{1,0},{2,3},{3,2},{4,5},{5,4},{6,7},{7,6},{8,9},{9,8},{10,11... | collective-permute-start | bytes 24584 | tf_op jit(solution)/shard_map/ppermute | solution.py:327
  19.5 0.8 copy-start.3
  20.5 37.9 %copy-start.2 = (bf16[256,512]{1,0:T(8,128)(2,1)S(1)}, bf16[256,512]{1,0:T(8,128)(2,1)}, u32[]{:S(2)}) copy-start(bf16[256,512]{1,0:T(8,128)(2,1)} %expand_ref.1) | copy-start | bytes 786436
  20.5 37.9 %copy-start.5 = (f32[256]{0:T(256)S(1)}, f32[256]{0:T(256)}, u32[]{:S(2)}) copy-start(f32[256]{0:T(256)} %param.14) | copy-start | bytes 3076
  20.5 37.9 %copy-start.6 = (f32[256]{0:T(256)S(1)}, f32[256]{0:T(256)}, u32[]{:S(2)}) copy-start(f32[256]{0:T(256)} %param.15) | copy-start | bytes 3076
  37.8 20.6 %all-to-all-start.1 = ((f32[16,8,128]{2,1,0:T(8,128)}), f32[16,8,128]{2,1,0:T(8,128)S(1)}, u32[]{:S(2)}, u32[]{:S(2)}) async-start(f32[16,8,128]{2,1,0:T(8,128)} %shard_map.140), calls=%async_computation.1 | async-start | bytes 131072 | tf_op jit(solution)/shard_map/all_to_all | solution.py:333
  59.0 41.2 %copy-start.1 = (bf16[256,256]{1,0:T(8,128)(2,1)S(1)}, bf16[256,256]{1,0:T(8,128)(2,1)}, u32[]{:S(2)}) copy-start(bf16[256,256]{1,0:T(8,128)(2,1)} %w_ref.3) | copy-start | bytes 393220
  86.2 3.7 %collective-permute-start.3 = (bf16[32,256]{1,0:T(8,128)(2,1)S(1)}, bf16[32,256]{1,0:T(8,128)(2,1)S(1)}, u32[]{:S(2)}, u32[]{:S(2)}) collective-permute-start(bf16[32,256]{1,0:T(8,128)(2,1)S(1)} %get-tuple-element.35), channel_id=1, source_target_pairs={{0,2},{1,3},{2,4},{3,5},{4,6},{5,7},{6,8},{7,9},{8,10},{9,11},{10,... | collective-permute-start | bytes 49160 | tf_op jit(solution)/shard_map/ppermute | solution.py:322
  88.6 4.5 %collective-permute-start.4 = (bf16[32,256]{1,0:T(8,128)(2,1)S(1)}, bf16[32,256]{1,0:T(8,128)(2,1)S(1)}, u32[]{:S(2)}, u32[]{:S(2)}) collective-permute-start(bf16[32,256]{1,0:T(8,128)(2,1)S(1)} %get-tuple-element.36), channel_id=1, source_target_pairs={{2,0},{3,1},{4,2},{5,3},{6,4},{7,5},{8,6},{9,7},{10,8},{11,9},{12,... | collective-permute-start | bytes 49160 | tf_op jit(solution)/shard_map/ppermute | solution.py:323
  93.2 7.0 %collective-permute-start.5 = (bf16[16,256]{1,0:T(8,128)(2,1)S(1)}, bf16[16,256]{1,0:T(8,128)(2,1)S(1)}, u32[]{:S(2)}, u32[]{:S(2)}) collective-permute-start(bf16[16,256]{1,0:T(8,128)(2,1)S(1)} %shard_map.144), channel_id=1, source_target_pairs={{0,1},{1,0},{2,3},{3,2},{4,5},{5,4},{6,7},{7,6},{8,9},{9,8},{10,11... | collective-permute-start | bytes 24584 | tf_op jit(solution)/shard_map/ppermute | solution.py:327
  140.2 31.4 %all-to-all-start.5 = ((bf16[512,2,256]{2,1,0:T(2,128)(2,1)}), bf16[512,2,256]{2,1,0:T(2,128)(2,1)S(1)}, u32[]{:S(2)}, u32[]{:S(2)}) async-start(bf16[512,2,256]{2,1,0:T(2,128)(2,1)} %reshape.54), calls=%async_computation.5 | async-start | bytes 1048576 | tf_op jit(solution)/shard_map/all_to_all | solution.py:375

commit v2 on v1

--- a/solution.py
+++ b/solution.py
@@ -5,8 +5,12 @@
 from jax import lax
 from jax.experimental import pallas as pl
 from jax.experimental.pallas import tpu as pltpu
+from jax.sharding import Mesh
 from jax.sharding import PartitionSpec as P
 
+SPACE = ("long", "near")
+FAR = ("dp", "long")
+ALL = ("dp", "long", "near")
 EPS = 1e-05
 SIDE = 14
 WIDE = 16
@@ -20,6 +24,7 @@
 
 VMEM = pl.BlockSpec(memory_space=pltpu.VMEM)
 SMEM = pl.BlockSpec(memory_space=pltpu.SMEM)
+HBM = pl.BlockSpec(memory_space=pl.ANY)
 PARAMS = pltpu.CompilerParams(vmem_limit_bytes=24 * 1024 * 1024)
 
 
@@ -70,7 +75,8 @@
     return out
 
 
-def column_kernel(odd_ref, values_ref, up_ref, down_ref, column_ref):
+def column_kernel(odd_ref, values_ref, up_ref, down_ref, after_ref, column_ref):
+    del after_ref
     left, right = strips(values_ref[...], up_ref[...], down_ref[...])
     row = iota((WIDE, EXT), 0)
     place = iota((WIDE, EXT), 1)
@@ -121,39 +127,40 @@
     return jnp.concatenate([t[a * WIDE : a * WIDE + TILE_ROWS] for t in moved[b]], axis=0)
 
 
-def reduce_kernel(act_ref, w_ref, tissue_ref, values_ref, top_ref, bottom_ref, mask_ref, wide):
+def reduce_kernel(act_ref, w_ref, values_ref, top_ref, bottom_ref, wide):
     wide[...] = jnp.zeros_like(wide)
     wide[:, :, :SIDE, :] = act_ref[0]
     values = dot(wide[...].reshape(ROWS, CH), w_ref[...]).astype(BF16)
     values_ref[...] = values
     rims_of(values, top_ref, bottom_ref)
+
+
+def prepare_kernel(
+    tissue_ref, group_ref, cot_ref, expand_ref,
+    mask_ref, dense_ref, out_grad_ref, hidden_grad_ref, wide,
+):
     row = iota((TILE_ROWS, SIDE), 0) // WIDE
     pick = (row == iota((TILE_ROWS, SIDE), 1)).astype(F32).astype(BF16)
     col = iota((TILE_ROWS, SIDE), 0) % WIDE
     here = col == iota((TILE_ROWS, SIDE), 1)
     ones = jnp.ones((SIDE, 128), BF16)
+    masks = []
     for t in range(2):
         rows = dot(pick, tissue_ref[0, t].astype(F32).astype(BF16))
-        mask_ref[t * TILE_ROWS : (t + 1) * TILE_ROWS] = dot(
-            jnp.where(here, rows, 0.0).astype(BF16), ones
-        )
-
-
-def spread_kernel(group_ref, dense_ref):
+        masks.append(dot(jnp.where(here, rows, 0.0).astype(BF16), ones))
+    mask = jnp.concatenate(masks, axis=0)
+    mask_ref[...] = mask
     same = iota((CH, CH), 0) // 8 == iota((CH, CH), 1) // 8
     for tap in range(9):
         taps = group_ref[tap // 3, tap % 3].astype(F32)
         full = jnp.concatenate([taps] * (CH // 8), axis=0)
         dense_ref[tap] = jnp.where(same, full, 0.0).astype(BF16)
-
-
-def as_rows(first, second, third):
-    pieces = [first[:, :128], first[:, 128:], second[:, :128], second[:, 128:], third]
-    return jnp.concatenate(pieces + [jnp.zeros((3, 128), F32)], axis=0)
-
-
-def per_channel(block, row):
-    return jnp.concatenate([block[row : row + 1], block[row + 1 : row + 2]], axis=1)
+    wide[...] = jnp.zeros_like(wide)
+    wide[:, :, :SIDE, :] = cot_ref[0]
+    keep = jnp.concatenate([mask] * (OUT // 128), axis=1) > 0
+    out_grad = jnp.where(keep, wide[...].reshape(ROWS, OUT).astype(F32), 0.0).astype(BF16)
+    out_grad_ref[...] = out_grad
+    hidden_grad_ref[...] = dot(out_grad, expand_ref[...], ((1,), (1,)))
 
 
 def both(mask):
@@ -175,10 +182,13 @@
     pre_ref[...] = pre
     mask = mask_ref[...]
     held = pre * both(mask)
-    block = as_rows(
-        jnp.sum(held, axis=0, keepdims=True),
-        jnp.sum(held * pre, axis=0, keepdims=True),
-        jnp.sum(mask, axis=0, keepdims=True),
+    block = jnp.concatenate(
+        [
+            jnp.sum(held, axis=0, keepdims=True),
+            jnp.sum(held * pre, axis=0, keepdims=True),
+            jnp.sum(mask, axis=0, keepdims=True),
+        ],
+        axis=1,
     )
     sums_ref[...] = jnp.broadcast_to(block[None], sums_ref.shape)
 
@@ -190,35 +200,27 @@
 
 def moments(parts_ref):
     block = jnp.sum(parts_ref[...], axis=0)
-    counted = both(block[4:5])
-    centre = per_channel(block, 0) / counted
-    spread = per_channel(block, 2) / counted - centre * centre
+    counted = both(block[:, 2 * CH :])
+    centre = block[:, :CH] / counted
+    spread = block[:, CH : 2 * CH] / counted - centre * centre
     return centre, lax.rsqrt(spread + EPS), counted
 
 
 def head_kernel(
-    parts_ref, pre_ref, mask_ref, gain_ref, bias_ref, expand_ref, cot_ref,
-    before_ref, expand_grad_ref, sums_ref, wide,
-):
-    wide[...] = jnp.zeros_like(wide)
-    wide[:, :, :SIDE, :] = cot_ref[0]
-    mask = mask_ref[...]
-    keep = jnp.concatenate([mask] * (OUT // 128), axis=1) > 0
-    out_grad = jnp.where(keep, wide[...].reshape(ROWS, OUT).astype(F32), 0.0).astype(BF16)
+    parts_ref, pre_ref, gain_ref, bias_ref, out_grad_ref, hidden_grad_ref,
+    before_ref, expand_grad_ref, sums_ref,
+):
     centre, inverse, _ = moments(parts_ref)
     normed = (pre_ref[...] - centre) * inverse
     before = gain_ref[...] * normed + bias_ref[...]
     sigma = jax.nn.sigmoid(before)
     hidden = (before * sigma).astype(BF16)
-    expand_grad_ref[...] = dot(hidden, out_grad, ((0,), (0,)))
-    hidden_grad = dot(out_grad, expand_ref[...], ((1,), (1,)))
-    before_grad = hidden_grad * sigma * (1.0 + before * (1.0 - sigma))
+    expand_grad_ref[...] = dot(hidden, out_grad_ref[...], ((0,), (0,)))
+    before_grad = hidden_grad_ref[...] * sigma * (1.0 + before * (1.0 - sigma))
     before_ref[...] = before_grad
-    block = as_rows(
-        jnp.sum(before_grad * normed, axis=0, keepdims=True),
-        jnp.sum(before_grad, axis=0, keepdims=True),
-        jnp.zeros((1, 128), F32),
-    )
+    gain_grad = jnp.sum(before_grad * normed, axis=0, keepdims=True)
+    bias_grad = jnp.sum(before_grad, axis=0, keepdims=True)
+    block = jnp.concatenate([gain_grad, bias_grad], axis=1)
     sums_ref[...] = jnp.broadcast_to(block[None], sums_ref.shape)
 
 
@@ -228,8 +230,8 @@
 ):
     centre, inverse, counted = moments(parts_ref)
     totals = jnp.sum(totals_ref[...], axis=0)
-    gain_grad = per_channel(totals, 0)
-    bias_grad = per_channel(totals, 2)
+    gain_grad = totals[:, :CH]
+    bias_grad = totals[:, CH:]
     gain_grad_ref[...] = gain_grad
     bias_grad_ref[...] = bias_grad
     normed = (pre_ref[...] - centre) * inverse
@@ -257,13 +259,10 @@
     input_grad = dot(reduced, w_ref[...], ((1,), (1,))).astype(BF16)
     input_grad_ref[0] = input_grad.reshape(2, SIDE, WIDE, CH)[:, :, :SIDE, :]
     reduce_grad = dot(act, reduced, ((0,), (0,))).astype(BF16)
-    packed_ref[:CH, :128] = reduce_grad[:, :128]
-    packed_ref[CH:, :128] = reduce_grad[:, 128:]
+    packed_ref[:CH] = reduce_grad
     expand_grad = expand_grad_ref[...].astype(BF16)
-    packed_ref[:CH, 128:256] = expand_grad[:, :128]
-    packed_ref[CH:, 128:256] = expand_grad[:, 128:256]
-    packed_ref[:CH, 256:384] = expand_grad[:, 256:384]
-    packed_ref[CH:, 256:384] = expand_grad[:, 384:]
+    packed_ref[CH : 2 * CH] = expand_grad[:, :CH]
+    packed_ref[2 * CH : 3 * CH] = expand_grad[:, CH:]
     lowered = []
     for a in range(3):
         parts = []
@@ -285,94 +284,98 @@
             own = jnp.where(same, product[:, a * CH : (a + 1) * CH], 0.0)
             taps[3 * a + b] = jnp.sum(own.reshape(CH // 8, 8, CH), axis=0)
     group = jnp.concatenate(taps + [jnp.zeros((CH - 72, CH), F32)], axis=0).astype(BF16)
-    packed_ref[:CH, 384:] = group[:, :128]
-    packed_ref[CH:, 384:] = group[:, 128:]
+    packed_ref[3 * CH :] = group
 
 
 def total_kernel(parts_ref, total_ref):
-    ones = jnp.ones(total_ref.shape[:1] + parts_ref.shape[:1], BF16)
-    total_ref[...] = dot(ones, parts_ref[...]).astype(BF16)
+    rows = parts_ref.shape[0]
+    own = total_ref.shape[1]
+    pick = iota((own, rows), 1) % own == iota((own, rows), 0)
+    total = dot(pick.astype(F32).astype(BF16), parts_ref[...]).astype(BF16)
+    total_ref[...] = jnp.broadcast_to(total[None], total_ref.shape)
 
 
 def unpack_kernel(packed_ref, reduce_ref, group_ref, expand_ref):
     packed = packed_ref[...].astype(F32)
-    reduce_ref[:, :128] = packed[:CH, :128]
-    reduce_ref[:, 128:] = packed[CH:, :128]
-    expand_ref[:, :128] = packed[:CH, 128:256]
-    expand_ref[:, 128:256] = packed[CH:, 128:256]
-    expand_ref[:, 256:384] = packed[:CH, 256:384]
-    expand_ref[:, 384:] = packed[CH:, 256:384]
-    group_ref[:, :128] = packed[:72, 384:]
-    group_ref[:, 128:] = packed[CH : CH + 72, 384:]
+    reduce_ref[...] = packed[:CH]
+    expand_ref[:, :CH] = packed[CH : 2 * CH]
+    expand_ref[:, CH:] = packed[2 * CH : 3 * CH]
+    group_ref[...] = packed[3 * CH : 3 * CH + 72]
 
 
 def body(
     sizes, activations, tissue, neighbours, w_reduce, w_group, norm_gain, norm_bias, w_expand,
     cotangent,
 ):
-    dp, space = sizes
-    everyone = ("dp", "space")
-    odd = (lax.axis_index("space") % 2).astype(jnp.int32).reshape(1)
+    dp, long, near = sizes
+    space = long * near
+    odd = (lax.axis_index(SPACE) % 2).astype(jnp.int32).reshape(1)
     gain = norm_gain.reshape(1, CH)
     bias = norm_bias.reshape(1, CH)
     rim = shape((2 * WIDE, CH), BF16)
     flat = shape((ROWS, CH), BF16)
-
-    def halo(values, top, bottom):
-        up = lax.ppermute(bottom, "space", [(i, i + 2) for i in range(space - 2)])
-        down = lax.ppermute(top, "space", [(i + 2, i) for i in range(space - 2)])
+    full = shape((ROWS, CH), F32)
+
+    def halo(values, top, bottom, after):
+        up = lax.ppermute(bottom, SPACE, [(i, i + 2) for i in range(space - 2)])
+        down = lax.ppermute(top, SPACE, [(i + 2, i) for i in range(space - 2)])
         column = call(
-            column_kernel, shape((WIDE, CH), BF16), [SMEM, VMEM, VMEM, VMEM]
-        )(odd, values, up, down)
-        side = lax.ppermute(column, "space", [(i, i ^ 1) for i in range(space)])
+            column_kernel, shape((WIDE, CH), BF16), [SMEM] + [VMEM] * 3 + [HBM]
+        )(odd, values, up, down, after)
+        side = lax.ppermute(column, SPACE, [(i, i ^ 1) for i in range(space)])
         return up, down, side
 
     def summed(blocks):
-        parts = lax.all_to_all(blocks, "space", 0, 0)
-        blocks = call(between_kernel, shape((dp, 8, 128), F32), [VMEM])(parts)
-        return lax.all_to_all(blocks, "dp", 0, 0)
-
-    values, top, bottom, mask = call(
-        reduce_kernel,
-        (flat, rim, rim, shape((ROWS, 128), F32)),
-        [VMEM] * 3,
-        [pltpu.VMEM((2, SIDE, WIDE, CH), BF16)],
-    )(activations, w_reduce, tissue)
-    dense = call(spread_kernel, shape((9, CH, CH), BF16), [VMEM])(w_group)
-    up, down, side = halo(values, top, bottom)
-    blocks = shape((space, 8, 128), F32)
+        parts = lax.all_to_all(blocks, "near", 0, 0)
+        blocks = call(
+            between_kernel, shape((dp * long,) + blocks.shape[1:], F32), [VMEM]
+        )(parts)
+        return lax.all_to_all(blocks, FAR, 0, 0)
+
+    values, top, bottom = call(
+        reduce_kernel, (flat, rim, rim), [VMEM] * 2, [pltpu.VMEM((2, SIDE, WIDE, CH), BF16)]
+    )(activations, w_reduce)
+    mask, dense, out_grad, hidden_grad = call(
+        prepare_kernel,
+        (
+            shape((ROWS, 128), F32),
+            shape((9, CH, CH), BF16),
+            shape((ROWS, OUT), BF16),
+            full,
+        ),
+        [VMEM] * 4,
+        [pltpu.VMEM((2, SIDE, WIDE, OUT), BF16)],
+    )(tissue, w_group, cotangent, w_expand)
+    up, down, side = halo(values, top, bottom, mask)
     pre, padded, sums = call(
         conv_kernel,
-        (shape((ROWS, CH), F32), shape((2, EXT, CH), BF16), blocks),
+        (full, shape((2, EXT, CH), BF16), shape((near, 1, 2 * CH + 128), F32)),
         [SMEM] + [VMEM] * 6,
     )(neighbours, values, up, down, side, dense, mask)
     parts = summed(sums)
     before_grad, expand_grad, sums = call(
         head_kernel,
-        (shape((ROWS, CH), F32), shape((CH, OUT), F32), blocks),
-        [VMEM] * 7,
-        [pltpu.VMEM((2, SIDE, WIDE, OUT), BF16)],
-    )(parts, pre, mask, gain, bias, w_expand, cotangent)
+        (full, shape((CH, OUT), F32), shape((near, 1, 2 * CH), F32)),
+        [VMEM] * 6,
+    )(parts, pre, gain, bias, out_grad, hidden_grad)
     totals = summed(sums)
     grad, top, bottom, gain_grad, bias_grad = call(
         norm_kernel,
         (flat, rim, rim, shape((1, CH), F32), shape((1, CH), F32)),
         [VMEM] * 6,
     )(parts, totals, pre, mask, gain, before_grad)
-    up, down, side = halo(grad, top, bottom)
-    count = dp * space
+    up, down, side = halo(grad, top, bottom, mask)
     input_grad, packed = call(
         back_kernel,
-        (shape((1, 2, SIDE, SIDE, CH), BF16), shape((2 * CH, 4 * 128), BF16)),
+        (shape((1, 2, SIDE, SIDE, CH), BF16), shape((4 * CH, CH), BF16)),
         [SMEM] + [VMEM] * 9,
         [pltpu.VMEM((2, SIDE, WIDE, CH), BF16)],
     )(neighbours, grad, up, down, side, dense, padded, activations, w_reduce, expand_grad)
-    share = packed.size // count
-    received = lax.all_to_all(packed.reshape(count, 1, share), everyone, 0, 0)
-    total = call(total_kernel, shape((count, share), BF16), [VMEM])(
-        received.reshape(count, share)
-    )
-    gathered = lax.all_to_all(total.reshape(count, 1, share), everyone, 0, 0)
+    count = dp * space
+    shares = (count, packed.shape[0] // count, CH)
+    received = lax.all_to_all(packed.reshape(shares), ALL, 0, 0)
+    total = call(total_kernel, shape(shares, BF16), [VMEM])(received.reshape(packed.shape))
+    gathered = lax.all_to_all(total, ALL, 0, 0)
     reduce_grad, group_grad, expand_grad = call(
         unpack_kernel,
         (shape((CH, CH), F32), shape((72, CH), F32), shape((CH, OUT), F32)),
@@ -389,21 +392,24 @@
 
 
 def solution(mesh):
-    sizes = (mesh.shape["dp"], mesh.shape["space"])
+    dp = mesh.shape["dp"]
+    near = min(16, mesh.shape["space"])
+    long = mesh.shape["space"] // near
+    cut = Mesh(mesh.devices.reshape(dp, long, near), ("dp", "long", "near"))
     return jax.shard_map(
-        functools.partial(body, sizes),
-        mesh=mesh,
+        functools.partial(body, (dp, long, near)),
+        mesh=cut,
         in_specs=(
-            P("dp", "space", None, None, None),
-            P("dp", "space", None, None),
-            P("dp", "space", None),
+            P("dp", SPACE, None, None, None),
+            P("dp", SPACE, None, None),
+            P("dp", SPACE, None),
             P(),
             P(),
             P(),
             P(),
             P(),
-            P("dp", "space", None, None, None),
+            P("dp", SPACE, None, None, None),
         ),
-        out_specs=(P("dp", "space", None, None, None), P(), P(), P(), P(), P()),
+        out_specs=(P("dp", SPACE, None, None, None), P(), P(), P(), P(), P()),
         check_vma=False,
     )

time: 174 us -> 163 us (0.937)
  blocking collectives: 73.7 us -> 90.4 us
  starting transfers between devices: 42.9 us -> 29.8 us
  waiting for transfers between devices: 36.7 us -> 27.2 us
  local copies, waits for them, and re-layouts: 7.99 us -> 5.18 us
  other arithmetic: 2.06 us -> 0 us
    all_to_all x4 -> x5, blocking collectives: 73.7 us -> 90.4 us  [the longest x2 33.7 us: summed(): return lax.all_to_all(blocks, FAR, 0, 0)]
    all_to_all x2 -> x1, starting transfers between devices: 20.6 us -> 8.88 us  [body(): gathered = lax.all_to_all(total, ALL, 0, 0)]
    all_to_all x2 -> x1, waiting for transfers between devices: 29.5 us -> 21.7 us  [body(): gathered = lax.all_to_all(total, ALL, 0, 0)]
    unnamed x24 -> x18, local copies, waits for them, and re-layouts: 7.48 us -> 4.59 us
    reshape x2 -> x0, other arithmetic: 2.06 us -> none  [the longest x1 1.03 us: body(): gathered = lax.all_to_all(total.reshape(count, 1, share), everyone, 0, 0)]
  transfers between devices with their start and end apart: 8 -> 7, of which waited for: 5 -> 5; matrix products, arithmetic and copies ran while one was open for 1% -> 2% of each run, Pallas kernels for 0% -> 0%
where the time goes in v2:
time: 163 us
  blocking collectives  90.4 us (55%)
  starting transfers between devices  29.8 us (18%)
  waiting for transfers between devices  27.2 us (17%)
  Pallas kernels  9.2 us (6%)
  local copies, waits for them, and re-layouts  5.18 us (3%)
    all_to_all x2, blocking collectives, summed(): return lax.all_to_all(blocks, FAR, 0, 0)  33.7 us
    all_to_all x1, blocking collectives, body(): received = lax.all_to_all(packed.reshape(shares), ALL, 0, 0)  33 us
    all_to_all x2, blocking collectives, summed(): parts = lax.all_to_all(blocks, 'near', 0, 0)  23.7 us
    all_to_all x1, waiting for transfers between devices, body(): gathered = lax.all_to_all(total, ALL, 0, 0)  21.7 us
    ppermute x2, starting transfers between devices, halo(): side = lax.ppermute(column, SPACE, [(i, i ^ 1) for i in range(space)])  12.2 us
    all_to_all x1, starting transfers between devices, body(): gathered = lax.all_to_all(total, ALL, 0, 0)  8.88 us
    ppermute x2, starting transfers between devices, halo(): up = lax.ppermute(bottom, SPACE, [(i, i + 2) for i in range(space - 2)])  6.14 us
    unnamed x18, local copies, waits for them, and re-layouts  4.59 us
  transfers between devices with their start and end apart: 7, of which 5 were waited for; matrix products, arithmetic and copies ran while one was open for 2% of the time, Pallas kernels for 0%

profile of v2, /device:TPU:1, one launch (start us, length us, event | category | flops | bytes accessed | tf_op | source)
XLA Modules:
  0.0 162.7 jit_solution(5225733145359931393)
XLA Ops:
  0.7 1.0 copy.15.act_ref
  1.7 0.9 copy-done
  2.8 4.0 %collective-permute-start = (bf16[32,256]{1,0:T(8,128)(2,1)S(1)}, bf16[32,256]{1,0:T(8,128)(2,1)S(1)}, u32[]{:S(2)}, u32[]{:S(2)}) collective-permute-start(bf16[32,256]{1,0:T(8,128)(2,1)S(1)} %get-tuple-element.30), channel_id=1, source_target_pairs={{0,2},{1,3},{2,4},{3,5},{4,6},{5,7},{6,8},{7,9},{8,10},{9,11},{10,... | collective-permute-start | bytes 49160 | tf_op jit(solution)/shard_map/ppermute | solution.py:320
  6.8 1.3 collective-permute-start.1
  8.9 1.1 copy.17.cot_ref
  11.5 7.2 %collective-permute-start.2 = (bf16[16,256]{1,0:T(8,128)(2,1)S(1)}, bf16[16,256]{1,0:T(8,128)(2,1)S(1)}, u32[]{:S(2)}, u32[]{:S(2)}) collective-permute-start(bf16[16,256]{1,0:T(8,128)(2,1)S(1)} %shard_map.138), channel_id=1, source_target_pairs={{0,1},{1,0},{2,3},{3,2},{4,5},{5,4},{6,7},{7,6},{8,9},{9,8},{10,11... | collective-permute-start | bytes 24584 | tf_op jit(solution)/shard_map/ppermute | solution.py:325
  18.7 0.8 collective-permute-done.2.side_ref
  19.5 1.5 shard_map.139
  20.9 11.9 %all_to_all.30.parts_ref = f32[16,1,640]{2,1,0:T(1,128)S(1)} all-to-all(f32[16,1,640]{2,1,0:T(1,128)S(1)} %get-tuple-element.34), channel_id=1, replica_groups=mesh['dp'=16,'long'=2,'near'=16] {'near'}, dimensions={0} | all-to-all | bytes 81920 | tf_op jit(solution)/shard_map/all_to_all | solution.py:329
  32.9 21.7 %all_to_all.31.parts_ref = f32[32,1,640]{2,1,0:T(1,128)S(1)} all-to-all(f32[32,1,640]{2,1,0:T(1,128)S(1)} %shard_map.140), channel_id=1, replica_groups=mesh['dp'=16,'long'=2,'near'=16] {'dp','long'}, dimensions={0} | all-to-all | bytes 163840 | tf_op jit(solution)/shard_map/all_to_all | solution.py:333
  55.2 11.8 %all_to_all.32.parts_ref = f32[16,1,512]{2,1,0:T(1,128)S(1)} all-to-all(f32[16,1,512]{2,1,0:T(1,128)S(1)} %get-tuple-element.38), channel_id=1, replica_groups=mesh['dp'=16,'long'=2,'near'=16] {'near'}, dimensions={0} | all-to-all | bytes 65536 | tf_op jit(solution)/shard_map/all_to_all | solution.py:329
  67.0 12.0 %all_to_all.33.totals_ref = f32[32,1,512]{2,1,0:T(1,128)S(1)} all-to-all(f32[32,1,512]{2,1,0:T(1,128)S(1)} %shard_map.142), channel_id=1, replica_groups=mesh['dp'=16,'long'=2,'near'=16] {'dp','long'}, dimensions={0} | all-to-all | bytes 131072 | tf_op jit(solution)/shard_map/all_to_all | solution.py:333
  79.7 2.1 %collective-permute-start.3 = (bf16[32,256]{1,0:T(8,128)(2,1)S(1)}, bf16[32,256]{1,0:T(8,128)(2,1)S(1)}, u32[]{:S(2)}, u32[]{:S(2)}) collective-permute-start(bf16[32,256]{1,0:T(8,128)(2,1)S(1)} %get-tuple-element.41), channel_id=1, source_target_pairs={{0,2},{1,3},{2,4},{3,5},{4,6},{5,7},{6,8},{7,9},{8,10},{9,11},{10,... | collective-permute-start | bytes 49160 | tf_op jit(solution)/shard_map/ppermute | solution.py:320
  81.8 1.3 collective-permute-start.4
  83.1 3.2 %collective-permute-done.4.down_ref = bf16[32,256]{1,0:T(8,128)(2,1)S(1)} collective-permute-done((bf16[32,256]{1,0:T(8,128)(2,1)S(1)}, bf16[32,256]{1,0:T(8,128)(2,1)S(1)}, u32[]{:S(2)}, u32[]{:S(2)}) %collective-permute-start.4) | collective-permute-done | bytes 16416 | tf_op jit(solution)/shard_map/ppermute | solution.py:321
  86.4 5.0 %collective-permute-start.5 = (bf16[16,256]{1,0:T(8,128)(2,1)S(1)}, bf16[16,256]{1,0:T(8,128)(2,1)S(1)}, u32[]{:S(2)}, u32[]{:S(2)}) collective-permute-start(bf16[16,256]{1,0:T(8,128)(2,1)S(1)} %shard_map.144), channel_id=1, source_target_pairs={{0,1},{1,0},{2,3},{3,2},{4,5},{5,4},{6,7},{7,6},{8,9},{9,8},{10,11... | collective-permute-start | bytes 24584 | tf_op jit(solution)/shard_map/ppermute | solution.py:325
  91.4 0.8 collective-permute-done.5.side_ref
  92.2 3.2 %shard_map.145 = (bf16[1,2,14,14,256]{4,3,2,1,0:T(8,128)(2,1)S(1)}, bf16[1024,256]{1,0:T(8,128)(2,1)S(1)}) custom-call(s32[1,2,8]{2,1,0:T(2,128)S(1)} %copy-done.4, bf16[448,256]{1,0:T(8,128)(2,1)S(1)} %get-tuple-element.40.values_ref.grad_ref, bf16[32,256]{1,0:T(8,128)(2,1)S(1)} %collective-permute-done.3.up_ref, ...), custom_call_target="tpu_custom_call" | custom-call | tf_op jit(solution)/shard_map/pallas_call | solution.py:368
  95.6 33.0 %all_to_all.34 = bf16[512,2,256]{2,1,0:T(2,128)(2,1)S(1)} all-to-all(bf16[512,2,256]{2,1,0:T(2,128)(2,1)S(1)} %reshape.42), channel_id=1, replica_groups=mesh['dp'=16,'long'=2,'near'=16] {'dp','long','near'}, dimensions={0} | all-to-all | bytes 1048576 | tf_op jit(solution)/shard_map/all_to_all | solution.py:376
  128.8 1.2 shard_map.146
  130.1 8.9 %all-to-all-start.5 = ((bf16[512,2,256]{2,1,0:T(2,128)(2,1)}), bf16[512,2,256]{2,1,0:T(2,128)(2,1)S(1)}, u32[]{:S(2)}, u32[]{:S(2)}) async-start(bf16[512,2,256]{2,1,0:T(2,128)(2,1)} %shard_map.146), calls=%async_computation.5 | async-start | bytes 1048576 | tf_op jit(solution)/shard_map/all_to_all | solution.py:378
  139.0 0.9 copy.19
  139.9 21.7 %all-to-all-done.5 = bf16[512,2,256]{2,1,0:T(2,128)(2,1)S(1)} async-done(((bf16[512,2,256]{2,1,0:T(2,128)(2,1)}), bf16[512,2,256]{2,1,0:T(2,128)(2,1)S(1)}, u32[]{:S(2)}, u32[]{:S(2)}) %all-to-all-start.5) | async-done | bytes 524320 | tf_op jit(solution)/shard_map/all_to_all | solution.py:378
  161.7 0.9 shard_map.147
  (28 shorter events, 4.5 us)
Async XLA Ops:
  0.6 9.3 %copy-start.2 = (bf16[256,512]{1,0:T(8,128)(2,1)S(1)}, bf16[256,512]{1,0:T(8,128)(2,1)}, u32[]{:S(2)}) copy-start(bf16[256,512]{1,0:T(8,128)(2,1)} %expand_ref.1) | copy-start | bytes 786436
  0.6 9.3 %copy-start.3 = (bf16[3,3,8,256]{3,2,1,0:T(8,128)(2,1)S(1)}, bf16[3,3,8,256]{3,2,1,0:T(8,128)(2,1)}, u32[]{:S(2)}) copy-start(bf16[3,3,8,256]{3,2,1,0:T(8,128)(2,1)} %group_ref.1) | copy-start | bytes 110596
  1.7 0.9 copy-start
  2.8 16.7 %copy-start.4 = (s32[1,2,8]{2,1,0:T(2,128)S(1)}, s32[1,2,8]{2,1,0:T(2,128)}, u32[]{:S(2)}) copy-start(s32[1,2,8]{2,1,0:T(2,128)} %links_ref.3) | copy-start | bytes 196
  2.8 7.7 %collective-permute-start = (bf16[32,256]{1,0:T(8,128)(2,1)S(1)}, bf16[32,256]{1,0:T(8,128)(2,1)S(1)}, u32[]{:S(2)}, u32[]{:S(2)}) collective-permute-start(bf16[32,256]{1,0:T(8,128)(2,1)S(1)} %get-tuple-element.30), channel_id=1, source_target_pairs={{0,2},{1,3},{2,4},{3,5},{4,6},{5,7},{6,8},{7,9},{8,10},{9,11},{10,... | collective-permute-start | bytes 49160 | tf_op jit(solution)/shard_map/ppermute | solution.py:320
  6.8 4.5 %collective-permute-start.1 = (bf16[32,256]{1,0:T(8,128)(2,1)S(1)}, bf16[32,256]{1,0:T(8,128)(2,1)S(1)}, u32[]{:S(2)}, u32[]{:S(2)}) collective-permute-start(bf16[32,256]{1,0:T(8,128)(2,1)S(1)} %get-tuple-element.31), channel_id=1, source_target_pairs={{2,0},{3,1},{4,2},{5,3},{6,4},{7,5},{8,6},{9,7},{10,8},{11,9},{12,... | collective-permute-start | bytes 49160 | tf_op jit(solution)/shard_map/ppermute | solution.py:321
  11.3 43.3 %copy-start.5 = (f32[256]{0:T(256)S(1)}, f32[256]{0:T(256)}, u32[]{:S(2)}) copy-start(f32[256]{0:T(256)} %param.14) | copy-start | bytes 3076
  11.3 43.3 %copy-start.6 = (f32[256]{0:T(256)S(1)}, f32[256]{0:T(256)}, u32[]{:S(2)}) copy-start(f32[256]{0:T(256)} %param.15) | copy-start | bytes 3076
  11.5 8.0 %collective-permute-start.2 = (bf16[16,256]{1,0:T(8,128)(2,1)S(1)}, bf16[16,256]{1,0:T(8,128)(2,1)S(1)}, u32[]{:S(2)}, u32[]{:S(2)}) collective-permute-start(bf16[16,256]{1,0:T(8,128)(2,1)S(1)} %shard_map.138), channel_id=1, source_target_pairs={{0,1},{1,0},{2,3},{3,2},{4,5},{5,4},{6,7},{7,6},{8,9},{9,8},{10,11... | collective-permute-start | bytes 24584 | tf_op jit(solution)/shard_map/ppermute | solution.py:325
  55.1 37.0 %copy-start.1 = (bf16[256,256]{1,0:T(8,128)(2,1)S(1)}, bf16[256,256]{1,0:T(8,128)(2,1)}, u32[]{:S(2)}) copy-start(bf16[256,256]{1,0:T(8,128)(2,1)} %w_ref.3) | copy-start | bytes 393220
  79.7 3.4 %collective-permute-start.3 = (bf16[32,256]{1,0:T(8,128)(2,1)S(1)}, bf16[32,256]{1,0:T(8,128)(2,1)S(1)}, u32[]{:S(2)}, u32[]{:S(2)}) collective-permute-start(bf16[32,256]{1,0:T(8,128)(2,1)S(1)} %get-tuple-element.41), channel_id=1, source_target_pairs={{0,2},{1,3},{2,4},{3,5},{4,6},{5,7},{6,8},{7,9},{8,10},{9,11},{10,... | collective-permute-start | bytes 49160 | tf_op jit(solution)/shard_map/ppermute | solution.py:320
  81.8 4.5 %collective-permute-start.4 = (bf16[32,256]{1,0:T(8,128)(2,1)S(1)}, bf16[32,256]{1,0:T(8,128)(2,1)S(1)}, u32[]{:S(2)}, u32[]{:S(2)}) collective-permute-start(bf16[32,256]{1,0:T(8,128)(2,1)S(1)} %get-tuple-element.42), channel_id=1, source_target_pairs={{2,0},{3,1},{4,2},{5,3},{6,4},{7,5},{8,6},{9,7},{10,8},{11,9},{12,... | collective-permute-start | bytes 49160 | tf_op jit(solution)/shard_map/ppermute | solution.py:321
  86.4 5.8 %collective-permute-start.5 = (bf16[16,256]{1,0:T(8,128)(2,1)S(1)}, bf16[16,256]{1,0:T(8,128)(2,1)S(1)}, u32[]{:S(2)}, u32[]{:S(2)}) collective-permute-start(bf16[16,256]{1,0:T(8,128)(2,1)S(1)} %shard_map.144), channel_id=1, source_target_pairs={{0,1},{1,0},{2,3},{3,2},{4,5},{5,4},{6,7},{7,6},{8,9},{9,8},{10,11... | collective-permute-start | bytes 24584 | tf_op jit(solution)/shard_map/ppermute | solution.py:325
  130.1 31.4 %all-to-all-start.5 = ((bf16[512,2,256]{2,1,0:T(2,128)(2,1)}), bf16[512,2,256]{2,1,0:T(2,128)(2,1)S(1)}, u32[]{:S(2)}, u32[]{:S(2)}) async-start(bf16[512,2,256]{2,1,0:T(2,128)(2,1)} %shard_map.146), calls=%async_computation.5 | async-start | bytes 1048576 | tf_op jit(solution)/shard_map/all_to_all | solution.py:378

commit v3 on v2

--- a/solution.py
+++ b/solution.py
@@ -135,10 +135,20 @@
     rims_of(values, top_ref, bottom_ref)
 
 
+def spread_taps(group_ref, dense_ref):
+    same = iota((CH, CH), 0) // 8 == iota((CH, CH), 1) // 8
+    for tap in range(9):
+        taps = group_ref[tap // 3, tap % 3].astype(F32)
+        full = jnp.concatenate([taps] * (CH // 8), axis=0)
+        dense_ref[tap] = jnp.where(same, full, 0.0).astype(BF16)
+
+
 def prepare_kernel(
-    tissue_ref, group_ref, cot_ref, expand_ref,
-    mask_ref, dense_ref, out_grad_ref, hidden_grad_ref, wide,
-):
+    tissue_ref, group_ref, cot_ref, expand_ref, gain_ref, bias_ref,
+    scale_ref, mask_ref, dense_ref, out_grad_ref, hidden_grad_ref, wide,
+):
+    scale_ref[0:1] = gain_ref[...]
+    scale_ref[1:2] = bias_ref[...]
     row = iota((TILE_ROWS, SIDE), 0) // WIDE
     pick = (row == iota((TILE_ROWS, SIDE), 1)).astype(F32).astype(BF16)
     col = iota((TILE_ROWS, SIDE), 0) % WIDE
@@ -150,11 +160,7 @@
         masks.append(dot(jnp.where(here, rows, 0.0).astype(BF16), ones))
     mask = jnp.concatenate(masks, axis=0)
     mask_ref[...] = mask
-    same = iota((CH, CH), 0) // 8 == iota((CH, CH), 1) // 8
-    for tap in range(9):
-        taps = group_ref[tap // 3, tap % 3].astype(F32)
-        full = jnp.concatenate([taps] * (CH // 8), axis=0)
-        dense_ref[tap] = jnp.where(same, full, 0.0).astype(BF16)
+    spread_taps(group_ref, dense_ref)
     wide[...] = jnp.zeros_like(wide)
     wide[:, :, :SIDE, :] = cot_ref[0]
     keep = jnp.concatenate([mask] * (OUT // 128), axis=1) > 0
@@ -168,8 +174,8 @@
 
 
 def conv_kernel(
-    links_ref, values_ref, up_ref, down_ref, side_ref, dense_ref, mask_ref,
-    pre_ref, padded_ref, sums_ref,
+    links_ref, values_ref, up_ref, down_ref, side_ref, dense_ref, mask_ref, hidden_grad_ref,
+    joint_ref, padded_ref, sums_ref, top_ref, bottom_ref,
 ):
     tiles = extended(values_ref[...], up_ref[...], down_ref[...], side_ref[...], links_ref)
     for t in range(2):
@@ -179,8 +185,10 @@
     for a in range(3):
         for b in range(3):
             pre += dot(window(moved, a, b), dense_ref[3 * a + b])
-    pre_ref[...] = pre
     mask = mask_ref[...]
+    joint = jnp.concatenate([pre, hidden_grad_ref[...], mask], axis=1)
+    joint_ref[...] = joint
+    rims_of(joint, top_ref, bottom_ref)
     held = pre * both(mask)
     block = jnp.concatenate(
         [
@@ -193,6 +201,20 @@
     sums_ref[...] = jnp.broadcast_to(block[None], sums_ref.shape)
 
 
+def between_rims_kernel(
+    odd_ref, parts_ref, joint_ref, up_ref, down_ref,
+    sums_ref, column_ref,
+):
+    between_kernel(parts_ref, sums_ref)
+    odd = odd_ref[0] == 1
+    in_rim = jnp.where(odd, 0, WIDE + SIDE - 1)
+    start = jnp.where(odd, 0, TILE_ROWS + SIDE - 1)
+    column_ref[0:1] = up_ref[pl.ds(in_rim, 1)]
+    column_ref[WIDE - 1 : WIDE] = down_ref[pl.ds(in_rim, 1)]
+    for r in range(SIDE):
+        column_ref[r + 1 : r + 2] = joint_ref[pl.ds(start + r * WIDE, 1)]
+
+
 def between_kernel(parts_ref, sums_ref):
     block = jnp.sum(parts_ref[...], axis=0)
     sums_ref[...] = jnp.broadcast_to(block[None], sums_ref.shape)
@@ -206,50 +228,58 @@
     return centre, lax.rsqrt(spread + EPS), counted
 
 
+def activated(normed, scale_ref):
+    before = scale_ref[0:1] * normed + scale_ref[1:2]
+    return before, jax.nn.sigmoid(before)
+
+
+def through_silu(hidden_grad, before, sigma):
+    return hidden_grad * sigma * (1.0 + before * (1.0 - sigma))
+
+
 def head_kernel(
-    parts_ref, pre_ref, gain_ref, bias_ref, out_grad_ref, hidden_grad_ref,
-    before_ref, expand_grad_ref, sums_ref,
-):
+    parts_ref, joint_ref, scale_ref, out_grad_ref, after_ref, expand_grad_ref, sums_ref,
+):
+    del after_ref
     centre, inverse, _ = moments(parts_ref)
-    normed = (pre_ref[...] - centre) * inverse
-    before = gain_ref[...] * normed + bias_ref[...]
-    sigma = jax.nn.sigmoid(before)
+    normed = (joint_ref[:, :CH] - centre) * inverse
+    before, sigma = activated(normed, scale_ref)
     hidden = (before * sigma).astype(BF16)
-    expand_grad_ref[...] = dot(hidden, out_grad_ref[...], ((0,), (0,)))
-    before_grad = hidden_grad_ref[...] * sigma * (1.0 + before * (1.0 - sigma))
-    before_ref[...] = before_grad
+    expand_grad = dot(hidden, out_grad_ref[...], ((0,), (0,))).astype(BF16)
+    expand_grad_ref[:CH] = expand_grad[:, :CH]
+    expand_grad_ref[CH:] = expand_grad[:, CH:]
+    before_grad = through_silu(joint_ref[:, CH : 2 * CH], before, sigma)
     gain_grad = jnp.sum(before_grad * normed, axis=0, keepdims=True)
     bias_grad = jnp.sum(before_grad, axis=0, keepdims=True)
     block = jnp.concatenate([gain_grad, bias_grad], axis=1)
     sums_ref[...] = jnp.broadcast_to(block[None], sums_ref.shape)
 
 
-def norm_kernel(
-    parts_ref, totals_ref, pre_ref, mask_ref, gain_ref, before_ref,
-    grad_ref, top_ref, bottom_ref, gain_grad_ref, bias_grad_ref,
-):
+def back_kernel(
+    links_ref, parts_ref, totals_ref, joint_ref, scale_ref,
+    up_ref, down_ref, side_ref, group_ref, padded_ref, act_ref, w_ref, expand_grad_ref,
+    input_grad_ref, packed_ref, gain_grad_ref, bias_grad_ref, wide, dense_ref,
+):
+    spread_taps(group_ref, dense_ref)
+    wide[...] = jnp.zeros_like(wide)
+    wide[:, :, :SIDE, :] = act_ref[0]
+    act = wide[...].reshape(ROWS, CH)
     centre, inverse, counted = moments(parts_ref)
     totals = jnp.sum(totals_ref[...], axis=0)
     gain_grad = totals[:, :CH]
     bias_grad = totals[:, CH:]
     gain_grad_ref[...] = gain_grad
     bias_grad_ref[...] = bias_grad
-    normed = (pre_ref[...] - centre) * inverse
-    taken = both(mask_ref[...]) * (bias_grad + normed * gain_grad) / counted
-    grad = (gain_ref[...] * inverse * (before_ref[...] - taken)).astype(BF16)
-    grad_ref[...] = grad
-    rims_of(grad, top_ref, bottom_ref)
-
-
-def back_kernel(
-    links_ref, grad_ref, up_ref, down_ref, side_ref, dense_ref, padded_ref, act_ref, w_ref,
-    expand_grad_ref, input_grad_ref, packed_ref, wide,
-):
-    wide[...] = jnp.zeros_like(wide)
-    wide[:, :, :SIDE, :] = act_ref[0]
-    act = wide[...].reshape(ROWS, CH)
-    grad = grad_ref[...]
-    moved = shifted(extended(grad, up_ref[...], down_ref[...], side_ref[...], links_ref))
+
+    def norm_grad(ref):
+        normed = (ref[:, :CH] - centre) * inverse
+        before, sigma = activated(normed, scale_ref)
+        before_grad = through_silu(ref[:, CH : 2 * CH], before, sigma)
+        taken = both(ref[:, 2 * CH :]) * (bias_grad + normed * gain_grad) / counted
+        return (scale_ref[0:1] * inverse * (before_grad - taken)).astype(BF16)
+
+    grad, up, down, side = (norm_grad(ref) for ref in (joint_ref, up_ref, down_ref, side_ref))
+    moved = shifted(extended(grad, up, down, side, links_ref))
     reduced = jnp.zeros((ROWS, CH), F32)
     for a in range(3):
         for b in range(3):
@@ -260,9 +290,7 @@
     input_grad_ref[0] = input_grad.reshape(2, SIDE, WIDE, CH)[:, :, :SIDE, :]
     reduce_grad = dot(act, reduced, ((0,), (0,))).astype(BF16)
     packed_ref[:CH] = reduce_grad
-    expand_grad = expand_grad_ref[...].astype(BF16)
-    packed_ref[CH : 2 * CH] = expand_grad[:, :CH]
-    packed_ref[2 * CH : 3 * CH] = expand_grad[:, CH:]
+    packed_ref[CH : 3 * CH] = expand_grad_ref[...]
     lowered = []
     for a in range(3):
         parts = []
@@ -310,67 +338,87 @@
     dp, long, near = sizes
     space = long * near
     odd = (lax.axis_index(SPACE) % 2).astype(jnp.int32).reshape(1)
-    gain = norm_gain.reshape(1, CH)
-    bias = norm_bias.reshape(1, CH)
     rim = shape((2 * WIDE, CH), BF16)
     flat = shape((ROWS, CH), BF16)
     full = shape((ROWS, CH), F32)
 
-    def halo(values, top, bottom, after):
+    def rows_passed(top, bottom):
         up = lax.ppermute(bottom, SPACE, [(i, i + 2) for i in range(space - 2)])
         down = lax.ppermute(top, SPACE, [(i + 2, i) for i in range(space - 2)])
-        column = call(
-            column_kernel, shape((WIDE, CH), BF16), [SMEM] + [VMEM] * 3 + [HBM]
-        )(odd, values, up, down, after)
-        side = lax.ppermute(column, SPACE, [(i, i ^ 1) for i in range(space)])
-        return up, down, side
-
-    def summed(blocks):
-        parts = lax.all_to_all(blocks, "near", 0, 0)
-        blocks = call(
-            between_kernel, shape((dp * long,) + blocks.shape[1:], F32), [VMEM]
-        )(parts)
-        return lax.all_to_all(blocks, FAR, 0, 0)
+        return up, down
+
+    def column_passed(column):
+        return lax.ppermute(column, SPACE, [(i, i ^ 1) for i in range(space)])
 
     values, top, bottom = call(
         reduce_kernel, (flat, rim, rim), [VMEM] * 2, [pltpu.VMEM((2, SIDE, WIDE, CH), BF16)]
     )(activations, w_reduce)
-    mask, dense, out_grad, hidden_grad = call(
+    scale, mask, dense, out_grad, hidden_grad = call(
         prepare_kernel,
         (
+            shape((2, CH), F32),
             shape((ROWS, 128), F32),
             shape((9, CH, CH), BF16),
             shape((ROWS, OUT), BF16),
             full,
         ),
-        [VMEM] * 4,
+        [VMEM] * 6,
         [pltpu.VMEM((2, SIDE, WIDE, OUT), BF16)],
-    )(tissue, w_group, cotangent, w_expand)
-    up, down, side = halo(values, top, bottom, mask)
-    pre, padded, sums = call(
+    )(
+        tissue, w_group, cotangent, w_expand, norm_gain.reshape(1, CH), norm_bias.reshape(1, CH)
+    )
+    up, down = rows_passed(top, bottom)
+    column = call(
+        column_kernel, shape((WIDE, CH), BF16), [SMEM] + [VMEM] * 3 + [HBM]
+    )(odd, values, up, down, mask)
+    side = column_passed(column)
+
+    width = 2 * CH + 128
+    rim = shape((2 * WIDE, width), F32)
+    joint, padded, sums, top, bottom = call(
         conv_kernel,
-        (full, shape((2, EXT, CH), BF16), shape((near, 1, 2 * CH + 128), F32)),
-        [SMEM] + [VMEM] * 6,
-    )(neighbours, values, up, down, side, dense, mask)
-    parts = summed(sums)
-    before_grad, expand_grad, sums = call(
+        (
+            shape((ROWS, width), F32),
+            shape((2, EXT, CH), BF16),
+            shape((near, 1, width), F32),
+            rim,
+            rim,
+        ),
+        [SMEM] + [VMEM] * 7,
+    )(neighbours, values, up, down, side, dense, mask, hidden_grad)
+    up, down = rows_passed(top, bottom)
+    parts = lax.all_to_all(sums, "near", 0, 0)
+    sums, column = call(
+        between_rims_kernel,
+        (shape((dp * long, 1, width), F32), shape((WIDE, width), F32)),
+        [SMEM] + [VMEM] * 4,
+    )(odd, parts, joint, up, down)
+    side = column_passed(column)
+    parts = lax.all_to_all(sums, FAR, 0, 0)
+
+    expand_grad, sums = call(
         head_kernel,
-        (full, shape((CH, OUT), F32), shape((near, 1, 2 * CH), F32)),
-        [VMEM] * 6,
-    )(parts, pre, gain, bias, out_grad, hidden_grad)
-    totals = summed(sums)
-    grad, top, bottom, gain_grad, bias_grad = call(
-        norm_kernel,
-        (flat, rim, rim, shape((1, CH), F32), shape((1, CH), F32)),
-        [VMEM] * 6,
-    )(parts, totals, pre, mask, gain, before_grad)
-    up, down, side = halo(grad, top, bottom, mask)
-    input_grad, packed = call(
+        (shape((2 * CH, CH), BF16), shape((near, 1, 2 * CH), F32)),
+        [VMEM] * 4 + [HBM],
+    )(parts, joint, scale, out_grad, side)
+    totals = lax.all_to_all(sums, "near", 0, 0)
+    sums = call(between_kernel, shape((dp * long, 1, 2 * CH), F32), [VMEM])(totals)
+    totals = lax.all_to_all(sums, FAR, 0, 0)
+
+    input_grad, packed, gain_grad, bias_grad = call(
         back_kernel,
-        (shape((1, 2, SIDE, SIDE, CH), BF16), shape((4 * CH, CH), BF16)),
-        [SMEM] + [VMEM] * 9,
-        [pltpu.VMEM((2, SIDE, WIDE, CH), BF16)],
-    )(neighbours, grad, up, down, side, dense, padded, activations, w_reduce, expand_grad)
+        (
+            shape((1, 2, SIDE, SIDE, CH), BF16),
+            shape((4 * CH, CH), BF16),
+            shape((1, CH), F32),
+            shape((1, CH), F32),
+        ),
+        [SMEM] + [VMEM] * 12,
+        [pltpu.VMEM((2, SIDE, WIDE, CH), BF16), pltpu.VMEM((9, CH, CH), BF16)],
+    )(
+        neighbours, parts, totals, joint, scale, up, down, side, w_group, padded,
+        activations, w_reduce, expand_grad,
+    )
     count = dp * space
     shares = (count, packed.shape[0] // count, CH)
     received = lax.all_to_all(packed.reshape(shares), ALL, 0, 0)

time: 163 us -> 159 us (0.975)
  blocking collectives: 90.4 us -> 71.6 us
  starting transfers between devices: 29.8 us -> 40.7 us
  waiting for transfers between devices: 27.2 us -> 29.7 us
    all_to_all x4 -> x3, blocking collectives: 57.4 us -> 38.9 us  [the longest x1 15.3 us: body(): parts = lax.all_to_all(sums, 'near', 0, 0)]
    all_to_all x0 -> x1, starting transfers between devices: none -> 13 us  [body(): parts = lax.all_to_all(sums, FAR, 0, 0)]
    all_to_all x0 -> x1, waiting for transfers between devices: none -> 5.61 us  [body(): parts = lax.all_to_all(sums, FAR, 0, 0)]
    ppermute x6, waiting for transfers between devices: 5.56 us -> 2.41 us  [the longest x2 1.65 us: column_passed(): return lax.ppermute(column, SPACE, [(i, i ^ 1) for i in range(space)])]
    ppermute x6, starting transfers between devices: 20.9 us -> 18.8 us  [the longest x2 9.77 us: column_passed(): return lax.ppermute(column, SPACE, [(i, i ^ 1) for i in range(space)])]
    pallas_call x8 -> x6, Pallas kernels: 3.62 us -> 3.43 us  [the longest x1 1.46 us: body(): call(conv_kernel, (shape((ROWS, width), F32), shape((2, EXT, CH), BF16),...]
  transfers between devices with their start and end apart: 7 -> 8, of which waited for: 5 -> 5; matrix products, arithmetic and copies ran while one was open for 2% -> 2% of each run, Pallas kernels for 0% -> 0%
where the time goes in v3:
time: 159 us; the launch traced here: 158 us
  blocking collectives  71.6 us (45%)
  starting transfers between devices  40.7 us (26%)
  waiting for transfers between devices  29.7 us (19%)
  Pallas kernels  9.89 us (6%)
  local copies, waits for them, and re-layouts  5.18 us (3%)
    all_to_all x1, blocking collectives, body(): received = lax.all_to_all(packed.reshape(shares), ALL, 0, 0)  32.7 us
    all_to_all x1, waiting for transfers between devices, body(): gathered = lax.all_to_all(total, ALL, 0, 0)  21.7 us
    all_to_all x1, blocking collectives, body(): parts = lax.all_to_all(sums, 'near', 0, 0)  15.3 us
    all_to_all x1, starting transfers between devices, body(): parts = lax.all_to_all(sums, FAR, 0, 0)  13 us
    all_to_all x1, blocking collectives, body(): totals = lax.all_to_all(sums, FAR, 0, 0)  12 us
    all_to_all x1, blocking collectives, body(): totals = lax.all_to_all(sums, 'near', 0, 0)  11.7 us
    ppermute x2, starting transfers between devices, column_passed(): return lax.ppermute(column, SPACE, [(i, i ^ 1) for i in range(space)])  9.77 us
    all_to_all x1, starting transfers between devices, body(): gathered = lax.all_to_all(total, ALL, 0, 0)  8.88 us
  transfers between devices with their start and end apart: 8, of which 5 were waited for; matrix products, arithmetic and copies ran while one was open for 2% of the time, Pallas kernels for 0%

profile of v3, /device:TPU:1, one launch (start us, length us, event | category | flops | bytes accessed | tf_op | source)
XLA Modules:
  0.0 157.9 jit_solution(10017622925112349647)
XLA Ops:
  0.7 1.0 copy.15.act_ref
  1.7 0.9 copy-done
  2.8 4.0 %collective-permute-start = (bf16[32,256]{1,0:T(8,128)(2,1)S(1)}, bf16[32,256]{1,0:T(8,128)(2,1)S(1)}, u32[]{:S(2)}, u32[]{:S(2)}) collective-permute-start(bf16[32,256]{1,0:T(8,128)(2,1)S(1)} %get-tuple-element.31), channel_id=1, source_target_pairs={{0,2},{1,3},{2,4},{3,5},{4,6},{5,7},{6,8},{7,9},{8,10},{9,11},{10,... | collective-permute-start | bytes 49160 | tf_op jit(solution)/shard_map/ppermute | solution.py:346
  6.9 1.3 collective-permute-start.1
  8.9 1.1 copy.17.cot_ref
  11.5 7.2 %collective-permute-start.2 = (bf16[16,256]{1,0:T(8,128)(2,1)S(1)}, bf16[16,256]{1,0:T(8,128)(2,1)S(1)}, u32[]{:S(2)}, u32[]{:S(2)}) collective-permute-start(bf16[16,256]{1,0:T(8,128)(2,1)S(1)} %shard_map.138), channel_id=1, source_target_pairs={{0,1},{1,0},{2,3},{3,2},{4,5},{5,4},{6,7},{7,6},{8,9},{9,8},{10,11... | collective-permute-start | bytes 24584 | tf_op jit(solution)/shard_map/ppermute | solution.py:351
  18.7 0.8 collective-permute-done.2.side_ref
  19.5 1.5 shard_map.139
  21.0 2.4 %collective-permute-start.3 = (f32[32,640]{1,0:T(8,128)S(1)}, f32[32,640]{1,0:T(8,128)S(1)}, u32[]{:S(2)}, u32[]{:S(2)}) collective-permute-start(f32[32,640]{1,0:T(8,128)S(1)} %get-tuple-element.38), channel_id=1, source_target_pairs={{0,2},{1,3},{2,4},{3,5},{4,6},{5,7},{6,8},{7,9},{8,10},{9,11},{10,... | collective-permute-start | bytes 245768 | tf_op jit(solution)/shard_map/ppermute | solution.py:346
  23.4 1.3 collective-permute-start.4
  24.6 15.3 %all_to_all.30.parts_ref = f32[16,1,640]{2,1,0:T(1,128)S(1)} all-to-all(f32[16,1,640]{2,1,0:T(1,128)S(1)} %get-tuple-element.36), channel_id=1, replica_groups=mesh['dp'=16,'long'=2,'near'=16] {'near'}, dimensions={0} | all-to-all | bytes 81920 | tf_op jit(solution)/shard_map/all_to_all | solution.py:390
  40.6 13.0 %all-to-all-start.1 = ((f32[32,1,640]{2,1,0:T(1,128)}), f32[32,1,640]{2,1,0:T(1,128)S(1)}, u32[]{:S(2)}, u32[]{:S(2)}) async-start(f32[32,1,640]{2,1,0:T(1,128)} %get-tuple-element.40), calls=%async_computation.1 | async-start | bytes 163840 | tf_op jit(solution)/shard_map/all_to_all | solution.py:397
  53.6 2.6 %collective-permute-start.5 = (f32[16,640]{1,0:T(8,128)S(1)}, f32[16,640]{1,0:T(8,128)S(1)}, u32[]{:S(2)}, u32[]{:S(2)}) collective-permute-start(f32[16,640]{1,0:T(8,128)S(1)} %get-tuple-element.43), channel_id=1, source_target_pairs={{0,1},{1,0},{2,3},{3,2},{4,5},{5,4},{6,7},{7,6},{8,9},{9,8},{10,11... | collective-permute-start | bytes 122888 | tf_op jit(solution)/shard_map/ppermute | solution.py:351
  56.2 0.8 collective-permute-done.5.after_ref.side_ref
  57.1 5.6 %all-to-all-done.1.parts_ref = f32[32,1,640]{2,1,0:T(1,128)S(1)} async-done(((f32[32,1,640]{2,1,0:T(1,128)}), f32[32,1,640]{2,1,0:T(1,128)S(1)}, u32[]{:S(2)}, u32[]{:S(2)}) %all-to-all-start.1) | async-done | bytes 81952 | tf_op jit(solution)/shard_map/all_to_all | solution.py:397
  63.2 11.7 %all_to_all.31.parts_ref = f32[16,1,512]{2,1,0:T(1,128)S(1)} all-to-all(f32[16,1,512]{2,1,0:T(1,128)S(1)} %get-tuple-element.44), channel_id=1, replica_groups=mesh['dp'=16,'long'=2,'near'=16] {'near'}, dimensions={0} | all-to-all | bytes 65536 | tf_op jit(solution)/shard_map/all_to_all | solution.py:404
  74.9 12.0 %all_to_all.32.totals_ref = f32[32,1,512]{2,1,0:T(1,128)S(1)} all-to-all(f32[32,1,512]{2,1,0:T(1,128)S(1)} %shard_map.142), channel_id=1, replica_groups=mesh['dp'=16,'long'=2,'near'=16] {'dp','long'}, dimensions={0} | all-to-all | bytes 131072 | tf_op jit(solution)/shard_map/all_to_all | solution.py:406
  86.9 4.1 %shard_map.143 = (bf16[1,2,14,14,256]{4,3,2,1,0:T(8,128)(2,1)S(1)}, bf16[1024,256]{1,0:T(8,128)(2,1)S(1)}, f32[1,256]{1,0:T(1,128)}, f32[1,256]{1,0:T(1,128)}) custom-call(s32[1,2,8]{2,1,0:T(2,128)S(1)} %copy-done.4, f32[32,1,640]{2,1,0:T(1,128)S(1)} %all-to-all-done.1.parts_ref, f32[32,1,512]{2,1,0:T(1,128)S(1)} %all_to_all.32.totals_ref, ...), custom_call_target="tpu_custom_call" | custom-call | tf_op jit(solution)/shard_map/pallas_call | solution.py:408
  91.2 32.7 %all_to_all.33 = bf16[512,2,256]{2,1,0:T(2,128)(2,1)S(1)} all-to-all(bf16[512,2,256]{2,1,0:T(2,128)(2,1)S(1)} %reshape.42), channel_id=1, replica_groups=mesh['dp'=16,'long'=2,'near'=16] {'dp','long','near'}, dimensions={0} | all-to-all | bytes 1048576 | tf_op jit(solution)/shard_map/all_to_all | solution.py:424
  124.1 1.2 shard_map.144
  125.3 8.9 %all-to-all-start.5 = ((bf16[512,2,256]{2,1,0:T(2,128)(2,1)}), bf16[512,2,256]{2,1,0:T(2,128)(2,1)S(1)}, u32[]{:S(2)}, u32[]{:S(2)}) async-start(bf16[512,2,256]{2,1,0:T(2,128)(2,1)} %shard_map.144), calls=%async_computation.5 | async-start | bytes 1048576 | tf_op jit(solution)/shard_map/all_to_all | solution.py:426
  134.2 0.9 copy.19
  135.1 21.7 %all-to-all-done.5 = bf16[512,2,256]{2,1,0:T(2,128)(2,1)S(1)} async-done(((bf16[512,2,256]{2,1,0:T(2,128)(2,1)}), bf16[512,2,256]{2,1,0:T(2,128)(2,1)S(1)}, u32[]{:S(2)}, u32[]{:S(2)}) %all-to-all-start.5) | async-done | bytes 524320 | tf_op jit(solution)/shard_map/all_to_all | solution.py:426
  157.0 0.9 shard_map.145
  (27 shorter events, 4.3 us)
Async XLA Ops:
  0.6 9.3 %copy-start.3 = (bf16[3,3,8,256]{3,2,1,0:T(8,128)(2,1)S(1)}, bf16[3,3,8,256]{3,2,1,0:T(8,128)(2,1)}, u32[]{:S(2)}) copy-start(bf16[3,3,8,256]{3,2,1,0:T(8,128)(2,1)} %group_ref.3) | copy-start | bytes 110596
  0.6 9.3 %copy-start.2 = (bf16[256,512]{1,0:T(8,128)(2,1)S(1)}, bf16[256,512]{1,0:T(8,128)(2,1)}, u32[]{:S(2)}) copy-start(bf16[256,512]{1,0:T(8,128)(2,1)} %expand_ref.1) | copy-start | bytes 786436
  0.7 9.3 %copy-start.6 = (f32[256]{0:T(256)S(1)}, f32[256]{0:T(256)}, u32[]{:S(2)}) copy-start(f32[256]{0:T(256)} %param.15) | copy-start | bytes 3076
  0.7 9.3 %copy-start.5 = (f32[256]{0:T(256)S(1)}, f32[256]{0:T(256)}, u32[]{:S(2)}) copy-start(f32[256]{0:T(256)} %param.14) | copy-start | bytes 3076
  1.7 0.9 copy-start
  2.8 16.7 %copy-start.4 = (s32[1,2,8]{2,1,0:T(2,128)S(1)}, s32[1,2,8]{2,1,0:T(2,128)}, u32[]{:S(2)}) copy-start(s32[1,2,8]{2,1,0:T(2,128)} %links_ref.3) | copy-start | bytes 196
  2.8 7.8 %collective-permute-start = (bf16[32,256]{1,0:T(8,128)(2,1)S(1)}, bf16[32,256]{1,0:T(8,128)(2,1)S(1)}, u32[]{:S(2)}, u32[]{:S(2)}) collective-permute-start(bf16[32,256]{1,0:T(8,128)(2,1)S(1)} %get-tuple-element.31), channel_id=1, source_target_pairs={{0,2},{1,3},{2,4},{3,5},{4,6},{5,7},{6,8},{7,9},{8,10},{9,11},{10,... | collective-permute-start | bytes 49160 | tf_op jit(solution)/shard_map/ppermute | solution.py:346
  6.9 4.5 %collective-permute-start.1 = (bf16[32,256]{1,0:T(8,128)(2,1)S(1)}, bf16[32,256]{1,0:T(8,128)(2,1)S(1)}, u32[]{:S(2)}, u32[]{:S(2)}) collective-permute-start(bf16[32,256]{1,0:T(8,128)(2,1)S(1)} %get-tuple-element.32), channel_id=1, source_target_pairs={{2,0},{3,1},{4,2},{5,3},{6,4},{7,5},{8,6},{9,7},{10,8},{11,9},{12,... | collective-permute-start | bytes 49160 | tf_op jit(solution)/shard_map/ppermute | solution.py:347
  11.5 8.0 %collective-permute-start.2 = (bf16[16,256]{1,0:T(8,128)(2,1)S(1)}, bf16[16,256]{1,0:T(8,128)(2,1)S(1)}, u32[]{:S(2)}, u32[]{:S(2)}) collective-permute-start(bf16[16,256]{1,0:T(8,128)(2,1)S(1)} %shard_map.138), channel_id=1, source_target_pairs={{0,1},{1,0},{2,3},{3,2},{4,5},{5,4},{6,7},{7,6},{8,9},{9,8},{10,11... | collective-permute-start | bytes 24584 | tf_op jit(solution)/shard_map/ppermute | solution.py:351
  21.0 19.0 %collective-permute-start.3 = (f32[32,640]{1,0:T(8,128)S(1)}, f32[32,640]{1,0:T(8,128)S(1)}, u32[]{:S(2)}, u32[]{:S(2)}) collective-permute-start(f32[32,640]{1,0:T(8,128)S(1)} %get-tuple-element.38), channel_id=1, source_target_pairs={{0,2},{1,3},{2,4},{3,5},{4,6},{5,7},{6,8},{7,9},{8,10},{9,11},{10,... | collective-permute-start | bytes 245768 | tf_op jit(solution)/shard_map/ppermute | solution.py:346
  23.4 16.6 %collective-permute-start.4 = (f32[32,640]{1,0:T(8,128)S(1)}, f32[32,640]{1,0:T(8,128)S(1)}, u32[]{:S(2)}, u32[]{:S(2)}) collective-permute-start(f32[32,640]{1,0:T(8,128)S(1)} %get-tuple-element.39), channel_id=1, source_target_pairs={{2,0},{3,1},{4,2},{5,3},{6,4},{7,5},{8,6},{9,7},{10,8},{11,9},{12,... | collective-permute-start | bytes 245768 | tf_op jit(solution)/shard_map/ppermute | solution.py:347
  40.6 46.3 %copy-start.1 = (bf16[256,256]{1,0:T(8,128)(2,1)S(1)}, bf16[256,256]{1,0:T(8,128)(2,1)}, u32[]{:S(2)}) copy-start(bf16[256,256]{1,0:T(8,128)(2,1)} %w_ref.3) | copy-start | bytes 393220
  40.6 22.1 %all-to-all-start.1 = ((f32[32,1,640]{2,1,0:T(1,128)}), f32[32,1,640]{2,1,0:T(1,128)S(1)}, u32[]{:S(2)}, u32[]{:S(2)}) async-start(f32[32,1,640]{2,1,0:T(1,128)} %get-tuple-element.40), calls=%async_computation.1 | async-start | bytes 163840 | tf_op jit(solution)/shard_map/all_to_all | solution.py:397
  53.6 3.4 %collective-permute-start.5 = (f32[16,640]{1,0:T(8,128)S(1)}, f32[16,640]{1,0:T(8,128)S(1)}, u32[]{:S(2)}, u32[]{:S(2)}) collective-permute-start(f32[16,640]{1,0:T(8,128)S(1)} %get-tuple-element.43), channel_id=1, source_target_pairs={{0,1},{1,0},{2,3},{3,2},{4,5},{5,4},{6,7},{7,6},{8,9},{9,8},{10,11... | collective-permute-start | bytes 122888 | tf_op jit(solution)/shard_map/ppermute | solution.py:351
  125.3 31.4 %all-to-all-start.5 = ((bf16[512,2,256]{2,1,0:T(2,128)(2,1)}), bf16[512,2,256]{2,1,0:T(2,128)(2,1)S(1)}, u32[]{:S(2)}, u32[]{:S(2)}) async-start(bf16[512,2,256]{2,1,0:T(2,128)(2,1)} %shard_map.144), calls=%async_computation.5 | async-start | bytes 1048576 | tf_op jit(solution)/shard_map/all_to_all | solution.py:426

commit v4 on v3

--- a/solution.py
+++ b/solution.py
@@ -175,7 +175,7 @@
 
 def conv_kernel(
     links_ref, values_ref, up_ref, down_ref, side_ref, dense_ref, mask_ref, hidden_grad_ref,
-    joint_ref, padded_ref, sums_ref, top_ref, bottom_ref,
+    joint_ref, padded_ref, sums_ref,
 ):
     tiles = extended(values_ref[...], up_ref[...], down_ref[...], side_ref[...], links_ref)
     for t in range(2):
@@ -188,7 +188,6 @@
     mask = mask_ref[...]
     joint = jnp.concatenate([pre, hidden_grad_ref[...], mask], axis=1)
     joint_ref[...] = joint
-    rims_of(joint, top_ref, bottom_ref)
     held = pre * both(mask)
     block = jnp.concatenate(
         [
@@ -201,9 +200,13 @@
     sums_ref[...] = jnp.broadcast_to(block[None], sums_ref.shape)
 
 
-def between_rims_kernel(
-    odd_ref, parts_ref, joint_ref, up_ref, down_ref,
-    sums_ref, column_ref,
+def between_rows_kernel(parts_ref, joint_ref, sums_ref, top_ref, bottom_ref):
+    between_kernel(parts_ref, sums_ref)
+    rims_of(joint_ref, top_ref, bottom_ref)
+
+
+def between_column_kernel(
+    odd_ref, parts_ref, joint_ref, up_ref, down_ref, sums_ref, column_ref
 ):
     between_kernel(parts_ref, sums_ref)
     odd = odd_ref[0] == 1
@@ -238,9 +241,8 @@
 
 
 def head_kernel(
-    parts_ref, joint_ref, scale_ref, out_grad_ref, after_ref, expand_grad_ref, sums_ref,
-):
-    del after_ref
+    parts_ref, joint_ref, scale_ref, out_grad_ref, expand_grad_ref, sums_ref,
+):
     centre, inverse, _ = moments(parts_ref)
     normed = (joint_ref[:, :CH] - centre) * inverse
     before, sigma = activated(normed, scale_ref)
@@ -291,26 +293,31 @@
     reduce_grad = dot(act, reduced, ((0,), (0,))).astype(BF16)
     packed_ref[:CH] = reduce_grad
     packed_ref[CH : 3 * CH] = expand_grad_ref[...]
+    tall = [grad[t * TILE_ROWS : (t + 1) * TILE_ROWS].astype(F32) for t in range(2)]
+    tall = [jnp.concatenate([own, jnp.zeros((2 * WIDE, CH), F32)], axis=0) for own in tall]
+    aside = [[(pltpu.roll(own, b, 0) if b else own).astype(BF16) for own in tall] for b in range(3)]
     lowered = []
     for a in range(3):
-        parts = []
-        for t in range(2):
-            own = grad[t * TILE_ROWS : (t + 1) * TILE_ROWS]
-            if a:
-                parts.append(jnp.zeros((a * WIDE, CH), BF16))
-            parts.append(own)
-            if a < 2:
-                parts.append(jnp.zeros(((2 - a) * WIDE, CH), BF16))
-        lowered.append(jnp.concatenate(parts, axis=0))
-    lowered = jnp.concatenate(lowered, axis=1)
-    windows = shifted([padded_ref[t].astype(F32) for t in range(2)])
-    same = iota((CH, CH), 0) // 8 == iota((CH, CH), 1) // 8
-    taps = [None] * 9
-    for b in range(3):
-        product = dot(jnp.concatenate(windows[b], axis=0), lowered, ((0,), (0,)))
-        for a in range(3):
-            own = jnp.where(same, product[:, a * CH : (a + 1) * CH], 0.0)
-            taps[3 * a + b] = jnp.sum(own.reshape(CH // 8, 8, CH), axis=0)
+        for b in range(3):
+            parts = []
+            for t in range(2):
+                if a:
+                    parts.append(jnp.zeros((a * WIDE, CH), BF16))
+                parts.append(aside[b][t][: EXT - a * WIDE])
+            lowered.append(jnp.concatenate(parts, axis=0))
+    padded = jnp.concatenate([padded_ref[0], padded_ref[1]], axis=0)
+    same = iota((128, 128), 0) // 8 == iota((128, 128), 1) // 8
+    halves = []
+    for h in range(2):
+        lanes = slice(h * 128, (h + 1) * 128)
+        right = jnp.concatenate([x[:, lanes] for x in lowered], axis=1)
+        product = dot(padded[:, lanes], right, ((0,), (0,)))
+        taps = []
+        for k in range(9):
+            own = jnp.where(same, product[:, k * 128 : (k + 1) * 128], 0.0)
+            taps.append(jnp.sum(own.reshape(128 // 8, 8, 128), axis=0))
+        halves.append(jnp.concatenate(taps, axis=0))
+    taps = [jnp.concatenate(halves, axis=1)]
     group = jnp.concatenate(taps + [jnp.zeros((CH - 72, CH), F32)], axis=0).astype(BF16)
     packed_ref[3 * CH :] = group
 
@@ -375,34 +382,34 @@
 
     width = 2 * CH + 128
     rim = shape((2 * WIDE, width), F32)
-    joint, padded, sums, top, bottom = call(
+    joint, padded, sums = call(
         conv_kernel,
         (
             shape((ROWS, width), F32),
             shape((2, EXT, CH), BF16),
             shape((near, 1, width), F32),
-            rim,
-            rim,
         ),
         [SMEM] + [VMEM] * 7,
     )(neighbours, values, up, down, side, dense, mask, hidden_grad)
+    parts = lax.all_to_all(sums, "near", 0, 0)
+    sums, top, bottom = call(
+        between_rows_kernel, (shape((dp * long, 1, width), F32), rim, rim), [VMEM] * 2
+    )(parts, joint)
     up, down = rows_passed(top, bottom)
-    parts = lax.all_to_all(sums, "near", 0, 0)
-    sums, column = call(
-        between_rims_kernel,
-        (shape((dp * long, 1, width), F32), shape((WIDE, width), F32)),
-        [SMEM] + [VMEM] * 4,
-    )(odd, parts, joint, up, down)
-    side = column_passed(column)
     parts = lax.all_to_all(sums, FAR, 0, 0)
 
     expand_grad, sums = call(
         head_kernel,
         (shape((2 * CH, CH), BF16), shape((near, 1, 2 * CH), F32)),
-        [VMEM] * 4 + [HBM],
-    )(parts, joint, scale, out_grad, side)
+        [VMEM] * 4,
+    )(parts, joint, scale, out_grad)
     totals = lax.all_to_all(sums, "near", 0, 0)
-    sums = call(between_kernel, shape((dp * long, 1, 2 * CH), F32), [VMEM])(totals)
+    sums, column = call(
+        between_column_kernel,
+        (shape((dp * long, 1, 2 * CH), F32), shape((WIDE, width), F32)),
+        [SMEM] + [VMEM] * 4,
+    )(odd, totals, joint, up, down)
+    side = column_passed(column)
     totals = lax.all_to_all(sums, FAR, 0, 0)
 
     input_grad, packed, gain_grad, bias_grad = call(

time: 159 us -> 157 us (0.987)
  blocking collectives: 71.6 us -> 44.8 us
  waiting for transfers between devices: 29.7 us -> 42.7 us
  starting transfers between devices: 40.7 us -> 51.9 us
    all_to_all x2 -> x0, blocking collectives: 23.7 us -> none  [the longest x1 12 us: body(): totals = lax.all_to_all(sums, FAR, 0, 0)]
    all_to_all x0 -> x2, waiting for transfers between devices: none -> 13 us  [the longest x1 7.46 us: body(): totals = lax.all_to_all(sums, 'near', 0, 0)]
    all_to_all x0 -> x2, starting transfers between devices: none -> 11.6 us  [the longest x1 6.4 us: body(): totals = lax.all_to_all(sums, FAR, 0, 0)]
    all_to_all x1, blocking collectives: 15.3 us -> 11.9 us  [body(): parts = lax.all_to_all(sums, 'near', 0, 0)]
  transfers between devices with their start and end apart: 8 -> 10, of which waited for: 5 -> 7; matrix products, arithmetic and copies ran while one was open for 2% -> 2% of each run, Pallas kernels for 0% -> 1%
where the time goes in v4:
time: 157 us; the launch traced here: 156 us
  starting transfers between devices  51.9 us (33%)
  blocking collectives  44.8 us (29%)
  waiting for transfers between devices  42.7 us (27%)
  Pallas kernels  10.6 us (7%)
  local copies, waits for them, and re-layouts  5.18 us (3%)
    all_to_all x1, blocking collectives, body(): received = lax.all_to_all(packed.reshape(shares), ALL, 0, 0)  32.9 us
    all_to_all x1, waiting for transfers between devices, body(): gathered = lax.all_to_all(total, ALL, 0, 0)  21.7 us
    all_to_all x1, starting transfers between devices, body(): parts = lax.all_to_all(sums, FAR, 0, 0)  12.9 us
    all_to_all x1, blocking collectives, body(): parts = lax.all_to_all(sums, 'near', 0, 0)  11.9 us
    ppermute x2, starting transfers between devices, column_passed(): return lax.ppermute(column, SPACE, [(i, i ^ 1) for i in range(space)])  9.77 us
    all_to_all x1, starting transfers between devices, body(): gathered = lax.all_to_all(total, ALL, 0, 0)  8.88 us
    all_to_all x1, waiting for transfers between devices, body(): totals = lax.all_to_all(sums, 'near', 0, 0)  7.46 us
    all_to_all x1, starting transfers between devices, body(): totals = lax.all_to_all(sums, FAR, 0, 0)  6.4 us
  transfers between devices with their start and end apart: 10, of which 7 were waited for; matrix products, arithmetic and copies ran while one was open for 2% of the time, Pallas kernels for 1%

profile of v4, /device:TPU:1, one launch (start us, length us, event | category | flops | bytes accessed | tf_op | source)
XLA Modules:
  0.0 156.1 jit_solution(15170156062871396907)
XLA Ops:
  0.7 1.0 copy.15.act_ref
  1.7 0.9 copy-done
  2.8 4.0 %collective-permute-start = (bf16[32,256]{1,0:T(8,128)(2,1)S(1)}, bf16[32,256]{1,0:T(8,128)(2,1)S(1)}, u32[]{:S(2)}, u32[]{:S(2)}) collective-permute-start(bf16[32,256]{1,0:T(8,128)(2,1)S(1)} %get-tuple-element.32), channel_id=1, source_target_pairs={{0,2},{1,3},{2,4},{3,5},{4,6},{5,7},{6,8},{7,9},{8,10},{9,11},{10,... | collective-permute-start | bytes 49160 | tf_op jit(solution)/shard_map/ppermute | solution.py:353
  6.9 1.3 collective-permute-start.1
  8.9 1.1 copy.17.cot_ref
  11.5 7.2 %collective-permute-start.2 = (bf16[16,256]{1,0:T(8,128)(2,1)S(1)}, bf16[16,256]{1,0:T(8,128)(2,1)S(1)}, u32[]{:S(2)}, u32[]{:S(2)}) collective-permute-start(bf16[16,256]{1,0:T(8,128)(2,1)S(1)} %shard_map.138), channel_id=1, source_target_pairs={{0,1},{1,0},{2,3},{3,2},{4,5},{5,4},{6,7},{7,6},{8,9},{9,8},{10,11... | collective-permute-start | bytes 24584 | tf_op jit(solution)/shard_map/ppermute | solution.py:358
  19.5 1.5 shard_map.139
  21.0 11.9 %all_to_all.30.parts_ref = f32[16,1,640]{2,1,0:T(1,128)S(1)} all-to-all(f32[16,1,640]{2,1,0:T(1,128)S(1)} %get-tuple-element.37), channel_id=1, replica_groups=mesh['dp'=16,'long'=2,'near'=16] {'near'}, dimensions={0} | all-to-all | bytes 81920 | tf_op jit(solution)/shard_map/all_to_all | solution.py:394
  33.5 12.9 %all-to-all-start.1 = ((f32[32,1,640]{2,1,0:T(1,128)}), f32[32,1,640]{2,1,0:T(1,128)S(1)}, u32[]{:S(2)}, u32[]{:S(2)}) async-start(f32[32,1,640]{2,1,0:T(1,128)} %get-tuple-element.39), calls=%async_computation.1 | async-start | bytes 163840 | tf_op jit(solution)/shard_map/all_to_all | solution.py:399
  46.4 2.1 %collective-permute-start.3 = (f32[32,640]{1,0:T(8,128)S(1)}, f32[32,640]{1,0:T(8,128)S(1)}, u32[]{:S(2)}, u32[]{:S(2)}) collective-permute-start(f32[32,640]{1,0:T(8,128)S(1)} %get-tuple-element.43), channel_id=1, source_target_pairs={{0,2},{1,3},{2,4},{3,5},{4,6},{5,7},{6,8},{7,9},{8,10},{9,11},{10,... | collective-permute-start | bytes 245768 | tf_op jit(solution)/shard_map/ppermute | solution.py:353
  48.6 1.3 collective-permute-start.4
  49.9 5.6 %all-to-all-done.1.parts_ref = f32[32,1,640]{2,1,0:T(1,128)S(1)} async-done(((f32[32,1,640]{2,1,0:T(1,128)}), f32[32,1,640]{2,1,0:T(1,128)S(1)}, u32[]{:S(2)}, u32[]{:S(2)}) %all-to-all-start.1) | async-done | bytes 81952 | tf_op jit(solution)/shard_map/all_to_all | solution.py:399
  55.5 1.0 shard_map.141
  56.5 5.2 %all-to-all-start.2 = ((f32[16,1,512]{2,1,0:T(1,128)}), f32[16,1,512]{2,1,0:T(1,128)S(1)}, u32[]{:S(2)}, u32[]{:S(2)}) async-start(f32[16,1,512]{2,1,0:T(1,128)} %get-tuple-element.42), calls=%async_computation.2 | async-start | bytes 65536 | tf_op jit(solution)/shard_map/all_to_all | solution.py:406
  61.7 7.5 %all-to-all-done.2.parts_ref = f32[16,1,512]{2,1,0:T(1,128)S(1)} async-done(((f32[16,1,512]{2,1,0:T(1,128)}), f32[16,1,512]{2,1,0:T(1,128)S(1)}, u32[]{:S(2)}, u32[]{:S(2)}) %all-to-all-start.2) | async-done | bytes 32800 | tf_op jit(solution)/shard_map/all_to_all | solution.py:406
  69.9 6.4 %all-to-all-start.3 = ((f32[32,1,512]{2,1,0:T(1,128)}), f32[32,1,512]{2,1,0:T(1,128)S(1)}, u32[]{:S(2)}, u32[]{:S(2)}) async-start(f32[32,1,512]{2,1,0:T(1,128)} %get-tuple-element.45), calls=%async_computation.3 | async-start | bytes 131072 | tf_op jit(solution)/shard_map/all_to_all | solution.py:413
  76.3 2.6 %collective-permute-start.5 = (f32[16,640]{1,0:T(8,128)S(1)}, f32[16,640]{1,0:T(8,128)S(1)}, u32[]{:S(2)}, u32[]{:S(2)}) collective-permute-start(f32[16,640]{1,0:T(8,128)S(1)} %get-tuple-element.46), channel_id=1, source_target_pairs={{0,1},{1,0},{2,3},{3,2},{4,5},{5,4},{6,7},{7,6},{8,9},{9,8},{10,11... | collective-permute-start | bytes 122888 | tf_op jit(solution)/shard_map/ppermute | solution.py:358
  79.7 5.5 %all-to-all-done.3.totals_ref = f32[32,1,512]{2,1,0:T(1,128)S(1)} async-done(((f32[32,1,512]{2,1,0:T(1,128)}), f32[32,1,512]{2,1,0:T(1,128)S(1)}, u32[]{:S(2)}, u32[]{:S(2)}) %all-to-all-start.3) | async-done | bytes 65568 | tf_op jit(solution)/shard_map/all_to_all | solution.py:413
  85.2 3.7 %shard_map.143 = (bf16[1,2,14,14,256]{4,3,2,1,0:T(8,128)(2,1)S(1)}, bf16[1024,256]{1,0:T(8,128)(2,1)S(1)}, f32[1,256]{1,0:T(1,128)}, f32[1,256]{1,0:T(1,128)}) custom-call(s32[1,2,8]{2,1,0:T(2,128)S(1)} %copy-done.4, f32[32,1,640]{2,1,0:T(1,128)S(1)} %all-to-all-done.1.parts_ref, f32[32,1,512]{2,1,0:T(1,128)S(1)} %all-to-all-done.3.totals_ref, ...), custom_call_target="tpu_custom_call" | custom-call | tf_op jit(solution)/shard_map/pallas_call | solution.py:415
  89.1 32.9 %all_to_all.31 = bf16[512,2,256]{2,1,0:T(2,128)(2,1)S(1)} all-to-all(bf16[512,2,256]{2,1,0:T(2,128)(2,1)S(1)} %reshape.42), channel_id=1, replica_groups=mesh['dp'=16,'long'=2,'near'=16] {'dp','long','near'}, dimensions={0} | all-to-all | bytes 1048576 | tf_op jit(solution)/shard_map/all_to_all | solution.py:431
  122.3 1.2 shard_map.144
  123.5 8.9 %all-to-all-start.5 = ((bf16[512,2,256]{2,1,0:T(2,128)(2,1)}), bf16[512,2,256]{2,1,0:T(2,128)(2,1)S(1)}, u32[]{:S(2)}, u32[]{:S(2)}) async-start(bf16[512,2,256]{2,1,0:T(2,128)(2,1)} %shard_map.144), calls=%async_computation.5 | async-start | bytes 1048576 | tf_op jit(solution)/shard_map/all_to_all | solution.py:433
  133.3 21.7 %all-to-all-done.5 = bf16[512,2,256]{2,1,0:T(2,128)(2,1)S(1)} async-done(((bf16[512,2,256]{2,1,0:T(2,128)(2,1)}), bf16[512,2,256]{2,1,0:T(2,128)(2,1)S(1)}, u32[]{:S(2)}, u32[]{:S(2)}) %all-to-all-start.5) | async-done | bytes 524320 | tf_op jit(solution)/shard_map/all_to_all | solution.py:433
  155.2 0.9 shard_map.145
  (29 shorter events, 6.9 us)
Async XLA Ops:
  0.6 9.3 %copy-start.3 = (bf16[3,3,8,256]{3,2,1,0:T(8,128)(2,1)S(1)}, bf16[3,3,8,256]{3,2,1,0:T(8,128)(2,1)}, u32[]{:S(2)}) copy-start(bf16[3,3,8,256]{3,2,1,0:T(8,128)(2,1)} %group_ref.3) | copy-start | bytes 110596
  0.6 9.3 %copy-start.2 = (bf16[256,512]{1,0:T(8,128)(2,1)S(1)}, bf16[256,512]{1,0:T(8,128)(2,1)}, u32[]{:S(2)}) copy-start(bf16[256,512]{1,0:T(8,128)(2,1)} %expand_ref.1) | copy-start | bytes 786436
  0.7 9.3 %copy-start.6 = (f32[256]{0:T(256)S(1)}, f32[256]{0:T(256)}, u32[]{:S(2)}) copy-start(f32[256]{0:T(256)} %param.15) | copy-start | bytes 3076
  0.7 9.3 %copy-start.5 = (f32[256]{0:T(256)S(1)}, f32[256]{0:T(256)}, u32[]{:S(2)}) copy-start(f32[256]{0:T(256)} %param.14) | copy-start | bytes 3076
  1.7 0.9 copy-start
  2.8 16.7 %copy-start.4 = (s32[1,2,8]{2,1,0:T(2,128)S(1)}, s32[1,2,8]{2,1,0:T(2,128)}, u32[]{:S(2)}) copy-start(s32[1,2,8]{2,1,0:T(2,128)} %links_ref.3) | copy-start | bytes 196
  2.8 7.8 %collective-permute-start = (bf16[32,256]{1,0:T(8,128)(2,1)S(1)}, bf16[32,256]{1,0:T(8,128)(2,1)S(1)}, u32[]{:S(2)}, u32[]{:S(2)}) collective-permute-start(bf16[32,256]{1,0:T(8,128)(2,1)S(1)} %get-tuple-element.32), channel_id=1, source_target_pairs={{0,2},{1,3},{2,4},{3,5},{4,6},{5,7},{6,8},{7,9},{8,10},{9,11},{10,... | collective-permute-start | bytes 49160 | tf_op jit(solution)/shard_map/ppermute | solution.py:353
  6.9 4.5 %collective-permute-start.1 = (bf16[32,256]{1,0:T(8,128)(2,1)S(1)}, bf16[32,256]{1,0:T(8,128)(2,1)S(1)}, u32[]{:S(2)}, u32[]{:S(2)}) collective-permute-start(bf16[32,256]{1,0:T(8,128)(2,1)S(1)} %get-tuple-element.33), channel_id=1, source_target_pairs={{2,0},{3,1},{4,2},{5,3},{6,4},{7,5},{8,6},{9,7},{10,8},{11,9},{12,... | collective-permute-start | bytes 49160 | tf_op jit(solution)/shard_map/ppermute | solution.py:354
  11.5 8.0 %collective-permute-start.2 = (bf16[16,256]{1,0:T(8,128)(2,1)S(1)}, bf16[16,256]{1,0:T(8,128)(2,1)S(1)}, u32[]{:S(2)}, u32[]{:S(2)}) collective-permute-start(bf16[16,256]{1,0:T(8,128)(2,1)S(1)} %shard_map.138), channel_id=1, source_target_pairs={{0,1},{1,0},{2,3},{3,2},{4,5},{5,4},{6,7},{7,6},{8,9},{9,8},{10,11... | collective-permute-start | bytes 24584 | tf_op jit(solution)/shard_map/ppermute | solution.py:358
  33.5 21.9 %all-to-all-start.1 = ((f32[32,1,640]{2,1,0:T(1,128)}), f32[32,1,640]{2,1,0:T(1,128)S(1)}, u32[]{:S(2)}, u32[]{:S(2)}) async-start(f32[32,1,640]{2,1,0:T(1,128)} %get-tuple-element.39), calls=%async_computation.1 | async-start | bytes 163840 | tf_op jit(solution)/shard_map/all_to_all | solution.py:399
  46.4 15.3 %collective-permute-start.3 = (f32[32,640]{1,0:T(8,128)S(1)}, f32[32,640]{1,0:T(8,128)S(1)}, u32[]{:S(2)}, u32[]{:S(2)}) collective-permute-start(f32[32,640]{1,0:T(8,128)S(1)} %get-tuple-element.43), channel_id=1, source_target_pairs={{0,2},{1,3},{2,4},{3,5},{4,6},{5,7},{6,8},{7,9},{8,10},{9,11},{10,... | collective-permute-start | bytes 245768 | tf_op jit(solution)/shard_map/ppermute | solution.py:353
  48.6 13.1 %collective-permute-start.4 = (f32[32,640]{1,0:T(8,128)S(1)}, f32[32,640]{1,0:T(8,128)S(1)}, u32[]{:S(2)}, u32[]{:S(2)}) collective-permute-start(f32[32,640]{1,0:T(8,128)S(1)} %get-tuple-element.44), channel_id=1, source_target_pairs={{2,0},{3,1},{4,2},{5,3},{6,4},{7,5},{8,6},{9,7},{10,8},{11,9},{12,... | collective-permute-start | bytes 245768 | tf_op jit(solution)/shard_map/ppermute | solution.py:354
  56.5 28.8 %copy-start.1 = (bf16[256,256]{1,0:T(8,128)(2,1)S(1)}, bf16[256,256]{1,0:T(8,128)(2,1)}, u32[]{:S(2)}) copy-start(bf16[256,256]{1,0:T(8,128)(2,1)} %w_ref.3) | copy-start | bytes 393220
  56.5 12.7 %all-to-all-start.2 = ((f32[16,1,512]{2,1,0:T(1,128)}), f32[16,1,512]{2,1,0:T(1,128)S(1)}, u32[]{:S(2)}, u32[]{:S(2)}) async-start(f32[16,1,512]{2,1,0:T(1,128)} %get-tuple-element.42), calls=%async_computation.2 | async-start | bytes 65536 | tf_op jit(solution)/shard_map/all_to_all | solution.py:406
  69.9 15.4 %all-to-all-start.3 = ((f32[32,1,512]{2,1,0:T(1,128)}), f32[32,1,512]{2,1,0:T(1,128)S(1)}, u32[]{:S(2)}, u32[]{:S(2)}) async-start(f32[32,1,512]{2,1,0:T(1,128)} %get-tuple-element.45), calls=%async_computation.3 | async-start | bytes 131072 | tf_op jit(solution)/shard_map/all_to_all | solution.py:413
  76.3 3.4 %collective-permute-start.5 = (f32[16,640]{1,0:T(8,128)S(1)}, f32[16,640]{1,0:T(8,128)S(1)}, u32[]{:S(2)}, u32[]{:S(2)}) collective-permute-start(f32[16,640]{1,0:T(8,128)S(1)} %get-tuple-element.46), channel_id=1, source_target_pairs={{0,1},{1,0},{2,3},{3,2},{4,5},{5,4},{6,7},{7,6},{8,9},{9,8},{10,11... | collective-permute-start | bytes 122888 | tf_op jit(solution)/shard_map/ppermute | solution.py:358
  123.5 31.4 %all-to-all-start.5 = ((bf16[512,2,256]{2,1,0:T(2,128)(2,1)}), bf16[512,2,256]{2,1,0:T(2,128)(2,1)S(1)}, u32[]{:S(2)}, u32[]{:S(2)}) async-start(bf16[512,2,256]{2,1,0:T(2,128)(2,1)} %shard_map.144), calls=%async_computation.5 | async-start | bytes 1048576 | tf_op jit(solution)/shard_map/all_to_all | solution.py:433

commit v5 on v4

--- a/solution.py
+++ b/solution.py
@@ -1,4 +1,5 @@
 import functools
+import math
 
 import jax
 import jax.numpy as jnp
@@ -8,14 +9,18 @@
 from jax.sharding import Mesh
 from jax.sharding import PartitionSpec as P
 
-SPACE = ("long", "near")
-FAR = ("dp", "long")
-ALL = ("dp", "long", "near")
+DP = ("zh", "x")
+SPACE = ("zl", "y", "core")
+NEAR = ("y", "core")
+FAR = ("zh", "x", "zl")
+FIRST = ("x", "core")
+SECOND = ("zh", "zl", "y")
 EPS = 1e-05
 SIDE = 14
 WIDE = 16
 TILE_ROWS = SIDE * WIDE
 ROWS = 2 * TILE_ROWS
+SPARE = WIDE - 1
 EXT = WIDE * WIDE
 CH = 256
 OUT = 512
@@ -75,19 +80,6 @@
     return out
 
 
-def column_kernel(odd_ref, values_ref, up_ref, down_ref, after_ref, column_ref):
-    del after_ref
-    left, right = strips(values_ref[...], up_ref[...], down_ref[...])
-    row = iota((WIDE, EXT), 0)
-    place = iota((WIDE, EXT), 1)
-    odd = odd_ref[0] == 1
-    wanted = row * WIDE + jnp.where(odd, 0, SIDE - 1)
-    pick = (place == wanted).astype(F32).astype(BF16)
-    from_left = dot(pick, left)
-    from_right = dot(pick, right)
-    column_ref[...] = jnp.where(odd, from_left, from_right).astype(BF16)
-
-
 def extended(values, up, down, side, links_ref):
     left, right = strips(values.astype(F32), up.astype(F32), down.astype(F32))
     r = iota((EXT, CH), 0) // WIDE
@@ -127,12 +119,23 @@
     return jnp.concatenate([t[a * WIDE : a * WIDE + TILE_ROWS] for t in moved[b]], axis=0)
 
 
-def reduce_kernel(act_ref, w_ref, values_ref, top_ref, bottom_ref, wide):
+def reduce_kernel(
+    odd_ref, act_ref, beside_ref, w_ref, values_ref, top_ref, bottom_ref, side_ref, wide
+):
     wide[...] = jnp.zeros_like(wide)
     wide[:, :, :SIDE, :] = act_ref[0]
     values = dot(wide[...].reshape(ROWS, CH), w_ref[...]).astype(BF16)
     values_ref[...] = values
-    rims_of(values, top_ref, bottom_ref)
+    down_one = iota((WIDE, SIDE), 0) == iota((WIDE, SIDE), 1) + 1
+    down_one = down_one.astype(F32).astype(BF16)
+    pixels = jnp.where(odd_ref[0] == 1, dot(down_one, beside_ref[0]), dot(down_one, beside_ref[1]))
+    side = dot(pixels.astype(BF16), w_ref[...])
+    side_ref[...] = side.astype(BF16)
+    for rim_ref, first, corner in ((top_ref, 0, 1), (bottom_ref, TILE_ROWS - WIDE, SIDE)):
+        strip = [values[t * TILE_ROWS + first :][:WIDE].astype(F32) for t in range(2)]
+        strip = jnp.concatenate(strip, axis=0)
+        spare = iota((2 * WIDE, CH), 0) == SPARE
+        rim_ref[...] = jnp.where(spare, side[corner : corner + 1], strip).astype(BF16)
 
 
 def spread_taps(group_ref, dense_ref):
@@ -177,7 +180,11 @@
     links_ref, values_ref, up_ref, down_ref, side_ref, dense_ref, mask_ref, hidden_grad_ref,
     joint_ref, padded_ref, sums_ref,
 ):
-    tiles = extended(values_ref[...], up_ref[...], down_ref[...], side_ref[...], links_ref)
+    up, down, side = up_ref[...], down_ref[...], side_ref[...].astype(F32)
+    row = iota((WIDE, CH), 0)
+    side = jnp.where(row == 0, up[SPARE : SPARE + 1].astype(F32), side)
+    side = jnp.where(row == WIDE - 1, down[SPARE : SPARE + 1].astype(F32), side)
+    tiles = extended(values_ref[...], up, down, side.astype(BF16), links_ref)
     for t in range(2):
         padded_ref[t] = tiles[t].astype(BF16)
     moved = shifted(tiles)
@@ -322,12 +329,19 @@
     packed_ref[3 * CH :] = group
 
 
+def near_total_kernel(parts_ref, total_ref):
+    total = jnp.sum(parts_ref[...].astype(F32), axis=0)
+    total_ref[...] = total.reshape(total_ref.shape)
+
+
 def total_kernel(parts_ref, total_ref):
-    rows = parts_ref.shape[0]
-    own = total_ref.shape[1]
-    pick = iota((own, rows), 1) % own == iota((own, rows), 0)
-    total = dot(pick.astype(F32).astype(BF16), parts_ref[...]).astype(BF16)
+    total = jnp.sum(parts_ref[...], axis=0).astype(BF16)
     total_ref[...] = jnp.broadcast_to(total[None], total_ref.shape)
+
+
+def repeat_kernel(part_ref, parts_ref):
+    part = part_ref[...].reshape(parts_ref.shape[1:])
+    parts_ref[...] = jnp.broadcast_to(part[None], parts_ref.shape)
 
 
 def unpack_kernel(packed_ref, reduce_ref, group_ref, expand_ref):
@@ -342,8 +356,7 @@
     sizes, activations, tissue, neighbours, w_reduce, w_group, norm_gain, norm_bias, w_expand,
     cotangent,
 ):
-    dp, long, near = sizes
-    space = long * near
+    space, near, far, first, second = sizes
     odd = (lax.axis_index(SPACE) % 2).astype(jnp.int32).reshape(1)
     rim = shape((2 * WIDE, CH), BF16)
     flat = shape((ROWS, CH), BF16)
@@ -357,9 +370,14 @@
     def column_passed(column):
         return lax.ppermute(column, SPACE, [(i, i ^ 1) for i in range(space)])
 
-    values, top, bottom = call(
-        reduce_kernel, (flat, rim, rim), [VMEM] * 2, [pltpu.VMEM((2, SIDE, WIDE, CH), BF16)]
-    )(activations, w_reduce)
+    pixels = activations[0]
+    beside = column_passed(jnp.stack([pixels[1, :, SIDE - 1], pixels[0, :, 0]]))
+    values, top, bottom, side = call(
+        reduce_kernel,
+        (flat, rim, rim, shape((WIDE, CH), BF16)),
+        [SMEM] + [VMEM] * 3,
+        [pltpu.VMEM((2, SIDE, WIDE, CH), BF16)],
+    )(odd, activations, beside, w_reduce)
     scale, mask, dense, out_grad, hidden_grad = call(
         prepare_kernel,
         (
@@ -375,10 +393,6 @@
         tissue, w_group, cotangent, w_expand, norm_gain.reshape(1, CH), norm_bias.reshape(1, CH)
     )
     up, down = rows_passed(top, bottom)
-    column = call(
-        column_kernel, shape((WIDE, CH), BF16), [SMEM] + [VMEM] * 3 + [HBM]
-    )(odd, values, up, down, mask)
-    side = column_passed(column)
 
     width = 2 * CH + 128
     rim = shape((2 * WIDE, width), F32)
@@ -391,9 +405,9 @@
         ),
         [SMEM] + [VMEM] * 7,
     )(neighbours, values, up, down, side, dense, mask, hidden_grad)
-    parts = lax.all_to_all(sums, "near", 0, 0)
+    parts = lax.all_to_all(sums, NEAR, 0, 0)
     sums, top, bottom = call(
-        between_rows_kernel, (shape((dp * long, 1, width), F32), rim, rim), [VMEM] * 2
+        between_rows_kernel, (shape((far, 1, width), F32), rim, rim), [VMEM] * 2
     )(parts, joint)
     up, down = rows_passed(top, bottom)
     parts = lax.all_to_all(sums, FAR, 0, 0)
@@ -403,10 +417,10 @@
         (shape((2 * CH, CH), BF16), shape((near, 1, 2 * CH), F32)),
         [VMEM] * 4,
     )(parts, joint, scale, out_grad)
-    totals = lax.all_to_all(sums, "near", 0, 0)
+    totals = lax.all_to_all(sums, NEAR, 0, 0)
     sums, column = call(
         between_column_kernel,
-        (shape((dp * long, 1, 2 * CH), F32), shape((WIDE, width), F32)),
+        (shape((far, 1, 2 * CH), F32), shape((WIDE, width), F32)),
         [SMEM] + [VMEM] * 4,
     )(odd, totals, joint, up, down)
     side = column_passed(column)
@@ -426,11 +440,15 @@
         neighbours, parts, totals, joint, scale, up, down, side, w_group, padded,
         activations, w_reduce, expand_grad,
     )
-    count = dp * space
-    shares = (count, packed.shape[0] // count, CH)
-    received = lax.all_to_all(packed.reshape(shares), ALL, 0, 0)
-    total = call(total_kernel, shape(shares, BF16), [VMEM])(received.reshape(packed.shape))
-    gathered = lax.all_to_all(total, ALL, 0, 0)
+    rows = packed.shape[0] // first
+    share = rows // second
+    parts = lax.all_to_all(packed.reshape(first, rows, CH), FIRST, 0, 0)
+    total = call(near_total_kernel, shape((second, share, CH), F32), [VMEM])(parts)
+    parts = lax.all_to_all(total, SECOND, 0, 0)
+    total = call(total_kernel, shape((second, share, CH), BF16), [VMEM])(parts)
+    part = lax.all_to_all(total, SECOND, 0, 0)
+    parts = call(repeat_kernel, shape((first, rows, CH), BF16), [VMEM])(part)
+    gathered = lax.all_to_all(parts, FIRST, 0, 0)
     reduce_grad, group_grad, expand_grad = call(
         unpack_kernel,
         (shape((CH, CH), F32), shape((72, CH), F32), shape((CH, OUT), F32)),
@@ -447,24 +465,30 @@
 
 
 def solution(mesh):
-    dp = mesh.shape["dp"]
-    near = min(16, mesh.shape["space"])
-    long = mesh.shape["space"] // near
-    cut = Mesh(mesh.devices.reshape(dp, long, near), ("dp", "long", "near"))
+    dp, space = mesh.shape["dp"], mesh.shape["space"]
+    zh = max(dp // 4, 1)
+    zl = max(space // 16, 1)
+    dims = (zh, dp // zh, zl, space // zl // 2, 2)
+    cut = Mesh(mesh.devices.reshape(dims), DP + SPACE)
+
+    def count(axes):
+        return math.prod(cut.shape[axis] for axis in axes)
+
+    sizes = tuple(count(axes) for axes in (SPACE, NEAR, FAR, FIRST, SECOND))
     return jax.shard_map(
-        functools.partial(body, (dp, long, near)),
+        functools.partial(body, sizes),
         mesh=cut,
         in_specs=(
-            P("dp", SPACE, None, None, None),
-            P("dp", SPACE, None, None),
-            P("dp", SPACE, None),
+            P(DP, SPACE, None, None, None),
+            P(DP, SPACE, None, None),
+            P(DP, SPACE, None),
             P(),
             P(),
             P(),
             P(),
             P(),
-            P("dp", SPACE, None, None, None),
+            P(DP, SPACE, None, None, None),
         ),
-        out_specs=(P("dp", SPACE, None, None, None), P(), P(), P(), P(), P()),
+        out_specs=(P(DP, SPACE, None, None, None), P(), P(), P(), P(), P()),
         check_vma=False,
     )

time: 157 us -> 152 us (0.968)
  waiting for transfers between devices: 42.7 us -> 30.5 us
  blocking collectives: 44.8 us -> 56.4 us
  starting transfers between devices: 51.9 us -> 48.7 us
    all_to_all x2, waiting for transfers between devices: 29.1 us -> 16.1 us  [the longest x1 8.61 us: body(): gathered = lax.all_to_all(parts, FIRST, 0, 0)]
    all_to_all x2 -> x4, blocking collectives: 44.8 us -> 56.4 us  [the longest x1 15.3 us: body(): parts = lax.all_to_all(total, SECOND, 0, 0)]
    ppermute x2, starting transfers between devices: 6.18 us -> 3.43 us  [rows_passed(): up = lax.ppermute(bottom, SPACE, [(i, i + 2) for i in range(space - 2)])]
    all_to_all x2, starting transfers between devices: 14.1 us -> 12 us  [the longest x1 6.76 us: body(): gathered = lax.all_to_all(parts, FIRST, 0, 0)]
    ppermute x2, waiting for transfers between devices: 0.75 us -> 2.45 us  [rows_passed(): down = lax.ppermute(top, SPACE, [(i + 2, i) for i in range(space - 2)])]
    ppermute x2, starting transfers between devices: 9.77 us -> 11.4 us  [column_passed(): return lax.ppermute(column, SPACE, [(i, i ^ 1) for i in range(space)])]
    unnamed x18 -> x23, local copies, waits for them, and re-layouts: 4.59 us -> 3.86 us
  transfers between devices with their start and end apart: 10 -> 10, of which waited for: 7 -> 6; matrix products, arithmetic and copies ran while one was open for 2% -> 1% of each run, Pallas kernels for 1% -> 1%
where the time goes in v5:
time: 152 us; the launch traced here: 151 us
  blocking collectives  56.4 us (37%)
  starting transfers between devices  48.7 us (32%)
  waiting for transfers between devices  30.5 us (20%)
  Pallas kernels  10.4 us (7%)
  local copies, waits for them, and re-layouts  3.87 us (3%)
    all_to_all x1, blocking collectives, body(): parts = lax.all_to_all(total, SECOND, 0, 0)  15.3 us
    all_to_all x1, blocking collectives, body(): part = lax.all_to_all(total, SECOND, 0, 0)  14.9 us
    all_to_all x1, blocking collectives, body(): parts = lax.all_to_all(packed.reshape(first, rows, CH), FIRST, 0, 0)  13.6 us
    all_to_all x1, starting transfers between devices, body(): parts = lax.all_to_all(sums, FAR, 0, 0)  12.9 us
    all_to_all x1, blocking collectives, body(): parts = lax.all_to_all(sums, NEAR, 0, 0)  12.6 us
    ppermute x2, starting transfers between devices, column_passed(): return lax.ppermute(column, SPACE, [(i, i ^ 1) for i in range(space)])  11.4 us
    all_to_all x1, waiting for transfers between devices, body(): gathered = lax.all_to_all(parts, FIRST, 0, 0)  8.61 us
    all_to_all x1, waiting for transfers between devices, body(): totals = lax.all_to_all(sums, NEAR, 0, 0)  7.46 us
  transfers between devices with their start and end apart: 10, of which 6 were waited for; matrix products, arithmetic and copies ran while one was open for 1% of the time, Pallas kernels for 1%

profile of v5, /device:TPU:1, one launch (start us, length us, event | category | flops | bytes accessed | tf_op | source)
XLA Modules:
  0.0 150.8 jit_solution(15256944710325320088)
XLA Ops:
  0.7 1.0 copy.22
  1.7 8.8 %collective-permute-start = (bf16[2,14,256]{2,1,0:T(8,128)(2,1)S(1)}, bf16[2,14,256]{2,1,0:T(8,128)(2,1)S(1)}, u32[]{:S(2)}, u32[]{:S(2)}) collective-permute-start(bf16[2,14,256]{2,1,0:T(8,128)(2,1)S(1)} %pad_maximum_fusion), channel_id=1, source_target_pairs={{0,1},{1,0},{2,3},{3,2},{4,5},{5,4},{6,7},{7,6},{8,9},{9,8},{10,11... | collective-permute-start | bytes 43016 | tf_op jit(solution)/shard_map/ppermute | solution.py:371
  10.6 1.0 copy.16.act_ref
  12.8 1.3 collective-permute-start.1
  14.1 1.3 collective-permute-start.2
  16.1 2.4 %collective-permute-done.2.down_ref = bf16[32,256]{1,0:T(8,128)(2,1)S(1)} collective-permute-done((bf16[32,256]{1,0:T(8,128)(2,1)S(1)}, bf16[32,256]{1,0:T(8,128)(2,1)S(1)}, u32[]{:S(2)}, u32[]{:S(2)}) %collective-permute-start.2) | collective-permute-done | bytes 16416 | tf_op jit(solution)/shard_map/ppermute | solution.py:367
  18.6 1.5 shard_map.138
  20.0 12.6 %all_to_all.40.parts_ref = f32[16,1,640]{2,1,0:T(1,128)S(1)} all-to-all(f32[16,1,640]{2,1,0:T(1,128)S(1)} %get-tuple-element.39), channel_id=1, replica_groups=mesh['zh'=4,'x'=4,'zl'=2,'y'=8,'core'=2] {'y','core'}, dimensions={0} | all-to-all | bytes 81920 | tf_op jit(solution)/shard_map/all_to_all | solution.py:408
  33.4 12.9 %all-to-all-start.1 = ((f32[32,1,640]{2,1,0:T(1,128)}), f32[32,1,640]{2,1,0:T(1,128)S(1)}, u32[]{:S(2)}, u32[]{:S(2)}) async-start(f32[32,1,640]{2,1,0:T(1,128)} %get-tuple-element.41), calls=%async_computation.1 | async-start | bytes 163840 | tf_op jit(solution)/shard_map/all_to_all | solution.py:413
  46.3 2.1 %collective-permute-start.3 = (f32[32,640]{1,0:T(8,128)S(1)}, f32[32,640]{1,0:T(8,128)S(1)}, u32[]{:S(2)}, u32[]{:S(2)}) collective-permute-start(f32[32,640]{1,0:T(8,128)S(1)} %get-tuple-element.45), channel_id=1, source_target_pairs={{0,2},{1,3},{2,4},{3,5},{4,6},{5,7},{6,8},{7,9},{8,10},{9,11},{10,... | collective-permute-start | bytes 245768 | tf_op jit(solution)/shard_map/ppermute | solution.py:366
  48.4 1.3 collective-permute-start.4
  49.7 5.6 %all-to-all-done.1.parts_ref = f32[32,1,640]{2,1,0:T(1,128)S(1)} async-done(((f32[32,1,640]{2,1,0:T(1,128)}), f32[32,1,640]{2,1,0:T(1,128)S(1)}, u32[]{:S(2)}, u32[]{:S(2)}) %all-to-all-start.1) | async-done | bytes 81952 | tf_op jit(solution)/shard_map/all_to_all | solution.py:413
  55.3 1.0 shard_map.140
  56.3 5.2 %all-to-all-start.2 = ((f32[16,1,512]{2,1,0:T(1,128)}), f32[16,1,512]{2,1,0:T(1,128)S(1)}, u32[]{:S(2)}, u32[]{:S(2)}) async-start(f32[16,1,512]{2,1,0:T(1,128)} %get-tuple-element.44), calls=%async_computation.2 | async-start | bytes 65536 | tf_op jit(solution)/shard_map/all_to_all | solution.py:420
  61.6 7.5 %all-to-all-done.2.parts_ref = f32[16,1,512]{2,1,0:T(1,128)S(1)} async-done(((f32[16,1,512]{2,1,0:T(1,128)}), f32[16,1,512]{2,1,0:T(1,128)S(1)}, u32[]{:S(2)}, u32[]{:S(2)}) %all-to-all-start.2) | async-done | bytes 32800 | tf_op jit(solution)/shard_map/all_to_all | solution.py:420
  69.7 6.4 %all-to-all-start.3 = ((f32[32,1,512]{2,1,0:T(1,128)}), f32[32,1,512]{2,1,0:T(1,128)S(1)}, u32[]{:S(2)}, u32[]{:S(2)}) async-start(f32[32,1,512]{2,1,0:T(1,128)} %get-tuple-element.47), calls=%async_computation.3 | async-start | bytes 131072 | tf_op jit(solution)/shard_map/all_to_all | solution.py:427
  76.1 2.6 %collective-permute-start.5 = (f32[16,640]{1,0:T(8,128)S(1)}, f32[16,640]{1,0:T(8,128)S(1)}, u32[]{:S(2)}, u32[]{:S(2)}) collective-permute-start(f32[16,640]{1,0:T(8,128)S(1)} %get-tuple-element.48), channel_id=1, source_target_pairs={{0,1},{1,0},{2,3},{3,2},{4,5},{5,4},{6,7},{7,6},{8,9},{9,8},{10,11... | collective-permute-start | bytes 122888 | tf_op jit(solution)/shard_map/ppermute | solution.py:371
  79.5 5.5 %all-to-all-done.3.totals_ref = f32[32,1,512]{2,1,0:T(1,128)S(1)} async-done(((f32[32,1,512]{2,1,0:T(1,128)}), f32[32,1,512]{2,1,0:T(1,128)S(1)}, u32[]{:S(2)}, u32[]{:S(2)}) %all-to-all-start.3) | async-done | bytes 65568 | tf_op jit(solution)/shard_map/all_to_all | solution.py:427
  85.1 3.7 %shard_map.142 = (bf16[1,2,14,14,256]{4,3,2,1,0:T(8,128)(2,1)S(1)}, bf16[1024,256]{1,0:T(8,128)(2,1)S(1)}, f32[1,256]{1,0:T(1,128)}, f32[1,256]{1,0:T(1,128)}) custom-call(s32[1,2,8]{2,1,0:T(2,128)S(1)} %copy-done.4, f32[32,1,640]{2,1,0:T(1,128)S(1)} %all-to-all-done.1.parts_ref, f32[32,1,512]{2,1,0:T(1,128)S(1)} %all-to-all-done.3.totals_ref, ...), custom_call_target="tpu_custom_call" | custom-call | tf_op jit(solution)/shard_map/pallas_call | solution.py:429
  88.8 13.6 %all_to_all.41.parts_ref = bf16[8,128,256]{2,1,0:T(8,128)(2,1)S(1)} all-to-all(bf16[8,128,256]{2,1,0:T(8,128)(2,1)S(1)} %bitcast.16), channel_id=1, replica_groups=mesh['zh'=4,'x'=4,'zl'=2,'y'=8,'core'=2] {'x','core'}, dimensions={0} | all-to-all | bytes 1048576 | tf_op jit(solution)/shard_map/all_to_all | solution.py:445
  102.5 15.3 %all_to_all.42.parts_ref = f32[64,2,256]{2,1,0:T(2,128)S(1)} all-to-all(f32[64,2,256]{2,1,0:T(2,128)S(1)} %shard_map.143), channel_id=1, replica_groups=mesh['zh'=4,'x'=4,'zl'=2,'y'=8,'core'=2] {'zh','zl','y'}, dimensions={0} | all-to-all | bytes 262144 | tf_op jit(solution)/shard_map/all_to_all | solution.py:447
  117.9 14.9 %all_to_all.43.part_ref = bf16[64,2,256]{2,1,0:T(2,128)(2,1)S(1)} all-to-all(bf16[64,2,256]{2,1,0:T(2,128)(2,1)S(1)} %shard_map.144), channel_id=1, replica_groups=mesh['zh'=4,'x'=4,'zl'=2,'y'=8,'core'=2] {'zh','zl','y'}, dimensions={0} | all-to-all | bytes 131072 | tf_op jit(solution)/shard_map/all_to_all | solution.py:449
  133.6 6.8 %all-to-all-start.7 = ((bf16[8,128,256]{2,1,0:T(8,128)(2,1)}), bf16[8,128,256]{2,1,0:T(8,128)(2,1)S(1)}, u32[]{:S(2)}, u32[]{:S(2)}) async-start(bf16[8,128,256]{2,1,0:T(8,128)(2,1)} %shard_map.145), calls=%async_computation.7 | async-start | bytes 1048576 | tf_op jit(solution)/shard_map/all_to_all | solution.py:451
  141.3 8.6 %all-to-all-done.7 = bf16[8,128,256]{2,1,0:T(8,128)(2,1)S(1)} async-done(((bf16[8,128,256]{2,1,0:T(8,128)(2,1)}), bf16[8,128,256]{2,1,0:T(8,128)(2,1)S(1)}, u32[]{:S(2)}, u32[]{:S(2)}) %all-to-all-start.7) | async-done | bytes 524320 | tf_op jit(solution)/shard_map/all_to_all | solution.py:451
  (36 shorter events, 7.0 us)
Async XLA Ops:
  0.6 14.7 %copy-start.8 = (s32[1,2,14,14]{3,1,2,0:T(2,128)S(1)}, s32[1,2,14,14]{3,1,2,0:T(2,128)}, u32[]{:S(2)}) copy-start(s32[1,2,14,14]{3,1,2,0:T(2,128)} %param.10) | copy-start | bytes 4708
  0.6 14.7 %copy-start.7 = (bf16[1,2,14,14,512]{4,1,3,2,0:T(2,128)(2,1)S(1)}, bf16[1,2,14,14,512]{4,1,3,2,0:T(2,128)(2,1)}, u32[]{:S(2)}) copy-start(bf16[1,2,14,14,512]{4,1,3,2,0:T(2,128)(2,1)} %param.17) | copy-start | bytes 1204228
  0.7 14.8 %copy-start.3 = (bf16[3,3,8,256]{3,2,1,0:T(8,128)(2,1)S(1)}, bf16[3,3,8,256]{3,2,1,0:T(8,128)(2,1)}, u32[]{:S(2)}) copy-start(bf16[3,3,8,256]{3,2,1,0:T(8,128)(2,1)} %group_ref.3) | copy-start | bytes 110596
  0.7 14.8 %copy-start.2 = (bf16[256,512]{1,0:T(8,128)(2,1)S(1)}, bf16[256,512]{1,0:T(8,128)(2,1)}, u32[]{:S(2)}) copy-start(bf16[256,512]{1,0:T(8,128)(2,1)} %expand_ref.1) | copy-start | bytes 786436
  0.7 14.8 %copy-start.6 = (f32[256]{0:T(256)S(1)}, f32[256]{0:T(256)}, u32[]{:S(2)}) copy-start(f32[256]{0:T(256)} %param.15) | copy-start | bytes 3076
  0.7 14.8 %copy-start.5 = (f32[256]{0:T(256)S(1)}, f32[256]{0:T(256)}, u32[]{:S(2)}) copy-start(f32[256]{0:T(256)} %param.14) | copy-start | bytes 3076
  1.7 9.8 %collective-permute-start = (bf16[2,14,256]{2,1,0:T(8,128)(2,1)S(1)}, bf16[2,14,256]{2,1,0:T(8,128)(2,1)S(1)}, u32[]{:S(2)}, u32[]{:S(2)}) collective-permute-start(bf16[2,14,256]{2,1,0:T(8,128)(2,1)S(1)} %pad_maximum_fusion), channel_id=1, source_target_pairs={{0,1},{1,0},{2,3},{3,2},{4,5},{5,4},{6,7},{7,6},{8,9},{9,8},{10,11... | collective-permute-start | bytes 43016 | tf_op jit(solution)/shard_map/ppermute | solution.py:371
  10.5 8.0 %copy-start.4 = (s32[1,2,8]{2,1,0:T(2,128)S(1)}, s32[1,2,8]{2,1,0:T(2,128)}, u32[]{:S(2)}) copy-start(s32[1,2,8]{2,1,0:T(2,128)} %links_ref.3) | copy-start | bytes 196
  11.5 0.9 copy-start
  12.8 3.3 %collective-permute-start.1 = (bf16[32,256]{1,0:T(8,128)(2,1)S(1)}, bf16[32,256]{1,0:T(8,128)(2,1)S(1)}, u32[]{:S(2)}, u32[]{:S(2)}) collective-permute-start(bf16[32,256]{1,0:T(8,128)(2,1)S(1)} %get-tuple-element.33), channel_id=1, source_target_pairs={{0,2},{1,3},{2,4},{3,5},{4,6},{5,7},{6,8},{7,9},{8,10},{9,11},{10,... | collective-permute-start | bytes 49160 | tf_op jit(solution)/shard_map/ppermute | solution.py:366
  14.1 4.5 %collective-permute-start.2 = (bf16[32,256]{1,0:T(8,128)(2,1)S(1)}, bf16[32,256]{1,0:T(8,128)(2,1)S(1)}, u32[]{:S(2)}, u32[]{:S(2)}) collective-permute-start(bf16[32,256]{1,0:T(8,128)(2,1)S(1)} %get-tuple-element.34), channel_id=1, source_target_pairs={{2,0},{3,1},{4,2},{5,3},{6,4},{7,5},{8,6},{9,7},{10,8},{11,9},{12,... | collective-permute-start | bytes 49160 | tf_op jit(solution)/shard_map/ppermute | solution.py:367
  33.4 22.0 %all-to-all-start.1 = ((f32[32,1,640]{2,1,0:T(1,128)}), f32[32,1,640]{2,1,0:T(1,128)S(1)}, u32[]{:S(2)}, u32[]{:S(2)}) async-start(f32[32,1,640]{2,1,0:T(1,128)} %get-tuple-element.41), calls=%async_computation.1 | async-start | bytes 163840 | tf_op jit(solution)/shard_map/all_to_all | solution.py:413
  46.3 15.3 %collective-permute-start.3 = (f32[32,640]{1,0:T(8,128)S(1)}, f32[32,640]{1,0:T(8,128)S(1)}, u32[]{:S(2)}, u32[]{:S(2)}) collective-permute-start(f32[32,640]{1,0:T(8,128)S(1)} %get-tuple-element.45), channel_id=1, source_target_pairs={{0,2},{1,3},{2,4},{3,5},{4,6},{5,7},{6,8},{7,9},{8,10},{9,11},{10,... | collective-permute-start | bytes 245768 | tf_op jit(solution)/shard_map/ppermute | solution.py:366
  48.4 13.1 %collective-permute-start.4 = (f32[32,640]{1,0:T(8,128)S(1)}, f32[32,640]{1,0:T(8,128)S(1)}, u32[]{:S(2)}, u32[]{:S(2)}) collective-permute-start(f32[32,640]{1,0:T(8,128)S(1)} %get-tuple-element.46), channel_id=1, source_target_pairs={{2,0},{3,1},{4,2},{5,3},{6,4},{7,5},{8,6},{9,7},{10,8},{11,9},{12,... | collective-permute-start | bytes 245768 | tf_op jit(solution)/shard_map/ppermute | solution.py:367
  56.3 28.8 %copy-start.1 = (bf16[256,256]{1,0:T(8,128)(2,1)S(1)}, bf16[256,256]{1,0:T(8,128)(2,1)}, u32[]{:S(2)}) copy-start(bf16[256,256]{1,0:T(8,128)(2,1)} %w_ref.3) | copy-start | bytes 393220
  56.3 12.7 %all-to-all-start.2 = ((f32[16,1,512]{2,1,0:T(1,128)}), f32[16,1,512]{2,1,0:T(1,128)S(1)}, u32[]{:S(2)}, u32[]{:S(2)}) async-start(f32[16,1,512]{2,1,0:T(1,128)} %get-tuple-element.44), calls=%async_computation.2 | async-start | bytes 65536 | tf_op jit(solution)/shard_map/all_to_all | solution.py:420
  69.7 15.4 %all-to-all-start.3 = ((f32[32,1,512]{2,1,0:T(1,128)}), f32[32,1,512]{2,1,0:T(1,128)S(1)}, u32[]{:S(2)}, u32[]{:S(2)}) async-start(f32[32,1,512]{2,1,0:T(1,128)} %get-tuple-element.47), calls=%async_computation.3 | async-start | bytes 131072 | tf_op jit(solution)/shard_map/all_to_all | solution.py:427
  76.1 3.4 %collective-permute-start.5 = (f32[16,640]{1,0:T(8,128)S(1)}, f32[16,640]{1,0:T(8,128)S(1)}, u32[]{:S(2)}, u32[]{:S(2)}) collective-permute-start(f32[16,640]{1,0:T(8,128)S(1)} %get-tuple-element.48), channel_id=1, source_target_pairs={{0,1},{1,0},{2,3},{3,2},{4,5},{5,4},{6,7},{7,6},{8,9},{9,8},{10,11... | collective-permute-start | bytes 122888 | tf_op jit(solution)/shard_map/ppermute | solution.py:371
  133.6 16.3 %all-to-all-start.7 = ((bf16[8,128,256]{2,1,0:T(8,128)(2,1)}), bf16[8,128,256]{2,1,0:T(8,128)(2,1)S(1)}, u32[]{:S(2)}, u32[]{:S(2)}) async-start(bf16[8,128,256]{2,1,0:T(8,128)(2,1)} %shard_map.145), calls=%async_computation.7 | async-start | bytes 1048576 | tf_op jit(solution)/shard_map/all_to_all | solution.py:451

commit v6 on v5

--- a/solution.py
+++ b/solution.py
@@ -20,6 +20,7 @@
 WIDE = 16
 TILE_ROWS = SIDE * WIDE
 ROWS = 2 * TILE_ROWS
+PIXELS = 2 * SIDE * SIDE
 SPARE = WIDE - 1
 EXT = WIDE * WIDE
 CH = 256
@@ -296,7 +297,12 @@
     in_tile = iota((ROWS, CH), 0) % WIDE < SIDE
     reduced = jnp.where(in_tile, reduced, 0.0).astype(BF16)
     input_grad = dot(reduced, w_ref[...], ((1,), (1,))).astype(BF16)
-    input_grad_ref[0] = input_grad.reshape(2, SIDE, WIDE, CH)[:, :, :SIDE, :]
+    s = iota((PIXELS, 1), 0)
+    pixel = s // 2
+    wanted = s % 2 * TILE_ROWS + pixel // SIDE * WIDE + pixel % SIDE
+    place = (iota((PIXELS, ROWS), 1) == wanted).astype(F32).astype(BF16)
+    input_grad = dot(place, input_grad).astype(BF16)
+    input_grad_ref[...] = input_grad.reshape(input_grad_ref.shape)
     reduce_grad = dot(act, reduced, ((0,), (0,))).astype(BF16)
     packed_ref[:CH] = reduce_grad
     packed_ref[CH : 3 * CH] = expand_grad_ref[...]
@@ -429,7 +435,7 @@
     input_grad, packed, gain_grad, bias_grad = call(
         back_kernel,
         (
-            shape((1, 2, SIDE, SIDE, CH), BF16),
+            shape((SIDE, SIDE, 2, CH), BF16),
             shape((4 * CH, CH), BF16),
             shape((1, CH), F32),
             shape((1, CH), F32),
@@ -455,7 +461,7 @@
         [VMEM],
     )(gathered.reshape(packed.shape))
     return (
-        input_grad,
+        input_grad[None].transpose(0, 3, 1, 2, 4),
         reduce_grad,
         group_grad.reshape(3, 3, 8, CH),
         gain_grad.reshape(CH),

time: 152 us -> 150 us (0.987)
  blocking collectives: 56.4 us -> 71.6 us
  waiting for transfers between devices: 30.5 us -> 21.9 us
  starting transfers between devices: 48.7 us -> 41.9 us
    all_to_all x0 -> x1, blocking collectives: none -> 15.1 us  [body(): gathered = lax.all_to_all(parts, FIRST, 0, 0)]
    all_to_all x1 -> x0, waiting for transfers between devices: 8.61 us -> none  [body(): gathered = lax.all_to_all(parts, FIRST, 0, 0)]
    all_to_all x1 -> x0, starting transfers between devices: 6.76 us -> none  [body(): gathered = lax.all_to_all(parts, FIRST, 0, 0)]
    unnamed x23 -> x22, local copies, waits for them, and re-layouts: 3.86 us -> 2.98 us
  transfers between devices with their start and end apart: 10 -> 9, of which waited for: 6 -> 5; matrix products, arithmetic and copies ran while one was open for 1% -> 1% of each run, Pallas kernels for 1% -> 1%
where the time goes in v6:
time: 150 us; the launch traced here: 149 us
  blocking collectives  71.6 us (48%)
  starting transfers between devices  41.9 us (28%)
  waiting for transfers between devices  21.9 us (15%)
  Pallas kernels  9.85 us (7%)
  local copies, waits for them, and re-layouts  2.98 us (2%)
    all_to_all x1, blocking collectives, body(): parts = lax.all_to_all(total, SECOND, 0, 0)  15.3 us
    all_to_all x1, blocking collectives, body(): gathered = lax.all_to_all(parts, FIRST, 0, 0)  15.1 us
    all_to_all x1, blocking collectives, body(): part = lax.all_to_all(total, SECOND, 0, 0)  14.9 us
    all_to_all x1, blocking collectives, body(): parts = lax.all_to_all(packed.reshape(first, rows, CH), FIRST, 0, 0)  13.6 us
    all_to_all x1, starting transfers between devices, body(): parts = lax.all_to_all(sums, FAR, 0, 0)  12.9 us
    all_to_all x1, blocking collectives, body(): parts = lax.all_to_all(sums, NEAR, 0, 0)  12.6 us
    ppermute x2, starting transfers between devices, column_passed(): return lax.ppermute(column, SPACE, [(i, i ^ 1) for i in range(space)])  11.4 us
    all_to_all x1, waiting for transfers between devices, body(): totals = lax.all_to_all(sums, NEAR, 0, 0)  7.46 us
  transfers between devices with their start and end apart: 9, of which 5 were waited for; matrix products, arithmetic and copies ran while one was open for 1% of the time, Pallas kernels for 1%

profile of v6, /device:TPU:1, one launch (start us, length us, event | category | flops | bytes accessed | tf_op | source)
XLA Modules:
  0.0 149.1 jit_solution(9934497236784298543)
XLA Ops:
  0.7 1.0 copy.21
  1.7 8.8 %collective-permute-start = (bf16[2,14,256]{2,1,0:T(8,128)(2,1)S(1)}, bf16[2,14,256]{2,1,0:T(8,128)(2,1)S(1)}, u32[]{:S(2)}, u32[]{:S(2)}) collective-permute-start(bf16[2,14,256]{2,1,0:T(8,128)(2,1)S(1)} %pad_maximum_fusion), channel_id=1, source_target_pairs={{0,1},{1,0},{2,3},{3,2},{4,5},{5,4},{6,7},{7,6},{8,9},{9,8},{10,11... | collective-permute-start | bytes 43016 | tf_op jit(solution)/shard_map/ppermute | solution.py:377
  10.6 1.0 copy.16.act_ref
  12.8 1.3 collective-permute-start.1
  14.1 1.3 collective-permute-start.2
  16.1 2.4 %collective-permute-done.2.down_ref = bf16[32,256]{1,0:T(8,128)(2,1)S(1)} collective-permute-done((bf16[32,256]{1,0:T(8,128)(2,1)S(1)}, bf16[32,256]{1,0:T(8,128)(2,1)S(1)}, u32[]{:S(2)}, u32[]{:S(2)}) %collective-permute-start.2) | collective-permute-done | bytes 16416 | tf_op jit(solution)/shard_map/ppermute | solution.py:373
  18.6 1.5 shard_map.138
  20.0 12.6 %all_to_all.40.parts_ref = f32[16,1,640]{2,1,0:T(1,128)S(1)} all-to-all(f32[16,1,640]{2,1,0:T(1,128)S(1)} %get-tuple-element.39), channel_id=1, replica_groups=mesh['zh'=4,'x'=4,'zl'=2,'y'=8,'core'=2] {'y','core'}, dimensions={0} | all-to-all | bytes 81920 | tf_op jit(solution)/shard_map/all_to_all | solution.py:414
  33.4 12.9 %all-to-all-start.1 = ((f32[32,1,640]{2,1,0:T(1,128)}), f32[32,1,640]{2,1,0:T(1,128)S(1)}, u32[]{:S(2)}, u32[]{:S(2)}) async-start(f32[32,1,640]{2,1,0:T(1,128)} %get-tuple-element.41), calls=%async_computation.1 | async-start | bytes 163840 | tf_op jit(solution)/shard_map/all_to_all | solution.py:419
  46.3 2.1 %collective-permute-start.3 = (f32[32,640]{1,0:T(8,128)S(1)}, f32[32,640]{1,0:T(8,128)S(1)}, u32[]{:S(2)}, u32[]{:S(2)}) collective-permute-start(f32[32,640]{1,0:T(8,128)S(1)} %get-tuple-element.45), channel_id=1, source_target_pairs={{0,2},{1,3},{2,4},{3,5},{4,6},{5,7},{6,8},{7,9},{8,10},{9,11},{10,... | collective-permute-start | bytes 245768 | tf_op jit(solution)/shard_map/ppermute | solution.py:372
  48.4 1.3 collective-permute-start.4
  49.7 5.6 %all-to-all-done.1.parts_ref = f32[32,1,640]{2,1,0:T(1,128)S(1)} async-done(((f32[32,1,640]{2,1,0:T(1,128)}), f32[32,1,640]{2,1,0:T(1,128)S(1)}, u32[]{:S(2)}, u32[]{:S(2)}) %all-to-all-start.1) | async-done | bytes 81952 | tf_op jit(solution)/shard_map/all_to_all | solution.py:419
  55.3 1.0 shard_map.140
  56.3 5.2 %all-to-all-start.2 = ((f32[16,1,512]{2,1,0:T(1,128)}), f32[16,1,512]{2,1,0:T(1,128)S(1)}, u32[]{:S(2)}, u32[]{:S(2)}) async-start(f32[16,1,512]{2,1,0:T(1,128)} %get-tuple-element.44), calls=%async_computation.2 | async-start | bytes 65536 | tf_op jit(solution)/shard_map/all_to_all | solution.py:426
  61.6 7.5 %all-to-all-done.2.parts_ref = f32[16,1,512]{2,1,0:T(1,128)S(1)} async-done(((f32[16,1,512]{2,1,0:T(1,128)}), f32[16,1,512]{2,1,0:T(1,128)S(1)}, u32[]{:S(2)}, u32[]{:S(2)}) %all-to-all-start.2) | async-done | bytes 32800 | tf_op jit(solution)/shard_map/all_to_all | solution.py:426
  69.7 6.4 %all-to-all-start.3 = ((f32[32,1,512]{2,1,0:T(1,128)}), f32[32,1,512]{2,1,0:T(1,128)S(1)}, u32[]{:S(2)}, u32[]{:S(2)}) async-start(f32[32,1,512]{2,1,0:T(1,128)} %get-tuple-element.47), calls=%async_computation.3 | async-start | bytes 131072 | tf_op jit(solution)/shard_map/all_to_all | solution.py:433
  76.1 2.6 %collective-permute-start.5 = (f32[16,640]{1,0:T(8,128)S(1)}, f32[16,640]{1,0:T(8,128)S(1)}, u32[]{:S(2)}, u32[]{:S(2)}) collective-permute-start(f32[16,640]{1,0:T(8,128)S(1)} %get-tuple-element.48), channel_id=1, source_target_pairs={{0,1},{1,0},{2,3},{3,2},{4,5},{5,4},{6,7},{7,6},{8,9},{9,8},{10,11... | collective-permute-start | bytes 122888 | tf_op jit(solution)/shard_map/ppermute | solution.py:377
  79.5 5.5 %all-to-all-done.3.totals_ref = f32[32,1,512]{2,1,0:T(1,128)S(1)} async-done(((f32[32,1,512]{2,1,0:T(1,128)}), f32[32,1,512]{2,1,0:T(1,128)S(1)}, u32[]{:S(2)}, u32[]{:S(2)}) %all-to-all-start.3) | async-done | bytes 65568 | tf_op jit(solution)/shard_map/all_to_all | solution.py:433
  85.1 3.9 %shard_map.142 = (bf16[14,14,2,256]{3,2,1,0:T(2,128)(2,1)}, bf16[1024,256]{1,0:T(8,128)(2,1)S(1)}, f32[1,256]{1,0:T(1,128)}, f32[1,256]{1,0:T(1,128)}) custom-call(s32[1,2,8]{2,1,0:T(2,128)S(1)} %copy-done.4, f32[32,1,640]{2,1,0:T(1,128)S(1)} %all-to-all-done.1.parts_ref, f32[32,1,512]{2,1,0:T(1,128)S(1)} %all-to-all-done.3.totals_ref, ...), custom_call_target="tpu_custom_call" | custom-call | tf_op jit(solution)/shard_map/pallas_call | solution.py:435
  89.0 13.6 %all_to_all.41.parts_ref = bf16[8,128,256]{2,1,0:T(8,128)(2,1)S(1)} all-to-all(bf16[8,128,256]{2,1,0:T(8,128)(2,1)S(1)} %bitcast.19), channel_id=1, replica_groups=mesh['zh'=4,'x'=4,'zl'=2,'y'=8,'core'=2] {'x','core'}, dimensions={0} | all-to-all | bytes 1048576 | tf_op jit(solution)/shard_map/all_to_all | solution.py:451
  102.7 15.3 %all_to_all.42.parts_ref = f32[64,2,256]{2,1,0:T(2,128)S(1)} all-to-all(f32[64,2,256]{2,1,0:T(2,128)S(1)} %shard_map.143), channel_id=1, replica_groups=mesh['zh'=4,'x'=4,'zl'=2,'y'=8,'core'=2] {'zh','zl','y'}, dimensions={0} | all-to-all | bytes 262144 | tf_op jit(solution)/shard_map/all_to_all | solution.py:453
  118.1 14.9 %all_to_all.43.part_ref = bf16[64,2,256]{2,1,0:T(2,128)(2,1)S(1)} all-to-all(bf16[64,2,256]{2,1,0:T(2,128)(2,1)S(1)} %shard_map.144), channel_id=1, replica_groups=mesh['zh'=4,'x'=4,'zl'=2,'y'=8,'core'=2] {'zh','zl','y'}, dimensions={0} | all-to-all | bytes 131072 | tf_op jit(solution)/shard_map/all_to_all | solution.py:455
  133.1 15.1 %all_to_all.44 = bf16[8,128,256]{2,1,0:T(8,128)(2,1)S(1)} all-to-all(bf16[8,128,256]{2,1,0:T(8,128)(2,1)S(1)} %shard_map.145), channel_id=1, replica_groups=mesh['zh'=4,'x'=4,'zl'=2,'y'=8,'core'=2] {'x','core'}, dimensions={0} | all-to-all | bytes 1048576 | tf_op jit(solution)/shard_map/all_to_all | solution.py:457
  148.2 0.9 shard_map.146
  (34 shorter events, 4.4 us)
Async XLA Ops:
  0.6 14.7 %copy-start.8 = (s32[1,2,14,14]{3,1,2,0:T(2,128)S(1)}, s32[1,2,14,14]{3,1,2,0:T(2,128)}, u32[]{:S(2)}) copy-start(s32[1,2,14,14]{3,1,2,0:T(2,128)} %param.10) | copy-start | bytes 4708
  0.6 14.7 %copy-start.7 = (bf16[1,2,14,14,512]{4,1,3,2,0:T(2,128)(2,1)S(1)}, bf16[1,2,14,14,512]{4,1,3,2,0:T(2,128)(2,1)}, u32[]{:S(2)}) copy-start(bf16[1,2,14,14,512]{4,1,3,2,0:T(2,128)(2,1)} %param.17) | copy-start | bytes 1204228
  0.7 14.8 %copy-start.3 = (bf16[3,3,8,256]{3,2,1,0:T(8,128)(2,1)S(1)}, bf16[3,3,8,256]{3,2,1,0:T(8,128)(2,1)}, u32[]{:S(2)}) copy-start(bf16[3,3,8,256]{3,2,1,0:T(8,128)(2,1)} %group_ref.3) | copy-start | bytes 110596
  0.7 14.8 %copy-start.2 = (bf16[256,512]{1,0:T(8,128)(2,1)S(1)}, bf16[256,512]{1,0:T(8,128)(2,1)}, u32[]{:S(2)}) copy-start(bf16[256,512]{1,0:T(8,128)(2,1)} %expand_ref.1) | copy-start | bytes 786436
  0.7 14.8 %copy-start.6 = (f32[256]{0:T(256)S(1)}, f32[256]{0:T(256)}, u32[]{:S(2)}) copy-start(f32[256]{0:T(256)} %param.15) | copy-start | bytes 3076
  0.7 14.8 %copy-start.5 = (f32[256]{0:T(256)S(1)}, f32[256]{0:T(256)}, u32[]{:S(2)}) copy-start(f32[256]{0:T(256)} %param.14) | copy-start | bytes 3076
  1.7 9.8 %collective-permute-start = (bf16[2,14,256]{2,1,0:T(8,128)(2,1)S(1)}, bf16[2,14,256]{2,1,0:T(8,128)(2,1)S(1)}, u32[]{:S(2)}, u32[]{:S(2)}) collective-permute-start(bf16[2,14,256]{2,1,0:T(8,128)(2,1)S(1)} %pad_maximum_fusion), channel_id=1, source_target_pairs={{0,1},{1,0},{2,3},{3,2},{4,5},{5,4},{6,7},{7,6},{8,9},{9,8},{10,11... | collective-permute-start | bytes 43016 | tf_op jit(solution)/shard_map/ppermute | solution.py:377
  10.5 8.0 %copy-start.4 = (s32[1,2,8]{2,1,0:T(2,128)S(1)}, s32[1,2,8]{2,1,0:T(2,128)}, u32[]{:S(2)}) copy-start(s32[1,2,8]{2,1,0:T(2,128)} %links_ref.3) | copy-start | bytes 196
  11.5 0.9 copy-start
  12.8 3.3 %collective-permute-start.1 = (bf16[32,256]{1,0:T(8,128)(2,1)S(1)}, bf16[32,256]{1,0:T(8,128)(2,1)S(1)}, u32[]{:S(2)}, u32[]{:S(2)}) collective-permute-start(bf16[32,256]{1,0:T(8,128)(2,1)S(1)} %get-tuple-element.33), channel_id=1, source_target_pairs={{0,2},{1,3},{2,4},{3,5},{4,6},{5,7},{6,8},{7,9},{8,10},{9,11},{10,... | collective-permute-start | bytes 49160 | tf_op jit(solution)/shard_map/ppermute | solution.py:372
  14.1 4.5 %collective-permute-start.2 = (bf16[32,256]{1,0:T(8,128)(2,1)S(1)}, bf16[32,256]{1,0:T(8,128)(2,1)S(1)}, u32[]{:S(2)}, u32[]{:S(2)}) collective-permute-start(bf16[32,256]{1,0:T(8,128)(2,1)S(1)} %get-tuple-element.34), channel_id=1, source_target_pairs={{2,0},{3,1},{4,2},{5,3},{6,4},{7,5},{8,6},{9,7},{10,8},{11,9},{12,... | collective-permute-start | bytes 49160 | tf_op jit(solution)/shard_map/ppermute | solution.py:373
  33.4 22.0 %all-to-all-start.1 = ((f32[32,1,640]{2,1,0:T(1,128)}), f32[32,1,640]{2,1,0:T(1,128)S(1)}, u32[]{:S(2)}, u32[]{:S(2)}) async-start(f32[32,1,640]{2,1,0:T(1,128)} %get-tuple-element.41), calls=%async_computation.1 | async-start | bytes 163840 | tf_op jit(solution)/shard_map/all_to_all | solution.py:419
  46.3 15.3 %collective-permute-start.3 = (f32[32,640]{1,0:T(8,128)S(1)}, f32[32,640]{1,0:T(8,128)S(1)}, u32[]{:S(2)}, u32[]{:S(2)}) collective-permute-start(f32[32,640]{1,0:T(8,128)S(1)} %get-tuple-element.45), channel_id=1, source_target_pairs={{0,2},{1,3},{2,4},{3,5},{4,6},{5,7},{6,8},{7,9},{8,10},{9,11},{10,... | collective-permute-start | bytes 245768 | tf_op jit(solution)/shard_map/ppermute | solution.py:372
  48.4 13.1 %collective-permute-start.4 = (f32[32,640]{1,0:T(8,128)S(1)}, f32[32,640]{1,0:T(8,128)S(1)}, u32[]{:S(2)}, u32[]{:S(2)}) collective-permute-start(f32[32,640]{1,0:T(8,128)S(1)} %get-tuple-element.46), channel_id=1, source_target_pairs={{2,0},{3,1},{4,2},{5,3},{6,4},{7,5},{8,6},{9,7},{10,8},{11,9},{12,... | collective-permute-start | bytes 245768 | tf_op jit(solution)/shard_map/ppermute | solution.py:373
  56.3 28.8 %copy-start.1 = (bf16[256,256]{1,0:T(8,128)(2,1)S(1)}, bf16[256,256]{1,0:T(8,128)(2,1)}, u32[]{:S(2)}) copy-start(bf16[256,256]{1,0:T(8,128)(2,1)} %w_ref.3) | copy-start | bytes 393220
  56.3 12.7 %all-to-all-start.2 = ((f32[16,1,512]{2,1,0:T(1,128)}), f32[16,1,512]{2,1,0:T(1,128)S(1)}, u32[]{:S(2)}, u32[]{:S(2)}) async-start(f32[16,1,512]{2,1,0:T(1,128)} %get-tuple-element.44), calls=%async_computation.2 | async-start | bytes 65536 | tf_op jit(solution)/shard_map/all_to_all | solution.py:426
  69.7 15.4 %all-to-all-start.3 = ((f32[32,1,512]{2,1,0:T(1,128)}), f32[32,1,512]{2,1,0:T(1,128)S(1)}, u32[]{:S(2)}, u32[]{:S(2)}) async-start(f32[32,1,512]{2,1,0:T(1,128)} %get-tuple-element.47), calls=%async_computation.3 | async-start | bytes 131072 | tf_op jit(solution)/shard_map/all_to_all | solution.py:433
  76.1 3.4 %collective-permute-start.5 = (f32[16,640]{1,0:T(8,128)S(1)}, f32[16,640]{1,0:T(8,128)S(1)}, u32[]{:S(2)}, u32[]{:S(2)}) collective-permute-start(f32[16,640]{1,0:T(8,128)S(1)} %get-tuple-element.48), channel_id=1, source_target_pairs={{0,1},{1,0},{2,3},{3,2},{4,5},{5,4},{6,7},{7,6},{8,9},{9,8},{10,11... | collective-permute-start | bytes 122888 | tf_op jit(solution)/shard_map/ppermute | solution.py:377

commit v7 on v6

--- a/solution.py
+++ b/solution.py
@@ -332,11 +332,14 @@
         halves.append(jnp.concatenate(taps, axis=0))
     taps = [jnp.concatenate(halves, axis=1)]
     group = jnp.concatenate(taps + [jnp.zeros((CH - 72, CH), F32)], axis=0).astype(BF16)
-    packed_ref[3 * CH :] = group
+    packed_ref[3 * CH :] = group[: packed_ref.shape[0] - 3 * CH]
 
 
 def near_total_kernel(parts_ref, total_ref):
     total = jnp.sum(parts_ref[...].astype(F32), axis=0)
+    spare = total_ref.shape[0] * total_ref.shape[1] - total.shape[0]
+    if spare:
+        total = jnp.concatenate([total, jnp.zeros((spare, CH), F32)], axis=0)
     total_ref[...] = total.reshape(total_ref.shape)
 
 
@@ -346,7 +349,8 @@
 
 
 def repeat_kernel(part_ref, parts_ref):
-    part = part_ref[...].reshape(parts_ref.shape[1:])
+    part = part_ref[...].reshape(part_ref.shape[0] * part_ref.shape[1], CH)
+    part = part[: parts_ref.shape[1]]
     parts_ref[...] = jnp.broadcast_to(part[None], parts_ref.shape)
 
 
@@ -432,11 +436,13 @@
     side = column_passed(column)
     totals = lax.all_to_all(sums, FAR, 0, 0)
 
+    rows = pl.cdiv(3 * CH + 72, first * 16) * 16
+    share = pl.cdiv(rows, second)
     input_grad, packed, gain_grad, bias_grad = call(
         back_kernel,
         (
             shape((SIDE, SIDE, 2, CH), BF16),
-            shape((4 * CH, CH), BF16),
+            shape((first * rows, CH), BF16),
             shape((1, CH), F32),
             shape((1, CH), F32),
         ),
@@ -446,8 +452,6 @@
         neighbours, parts, totals, joint, scale, up, down, side, w_group, padded,
         activations, w_reduce, expand_grad,
     )
-    rows = packed.shape[0] // first
-    share = rows // second
     parts = lax.all_to_all(packed.reshape(first, rows, CH), FIRST, 0, 0)
     total = call(near_total_kernel, shape((second, share, CH), F32), [VMEM])(parts)
     parts = lax.all_to_all(total, SECOND, 0, 0)

time: 150 us -> 148 us (0.987)
  no operation moved by 1% of the time
where the time goes in v7:
time: 148 us
  blocking collectives  70.2 us (47%)
  starting transfers between devices  41.9 us (28%)
  waiting for transfers between devices  21.9 us (15%)
  Pallas kernels  9.83 us (7%)
  local copies, waits for them, and re-layouts  2.98 us (2%)
    all_to_all x1, blocking collectives, body(): parts = lax.all_to_all(total, SECOND, 0, 0)  15.3 us
    all_to_all x1, blocking collectives, body(): part = lax.all_to_all(total, SECOND, 0, 0)  14.9 us
    all_to_all x1, blocking collectives, body(): gathered = lax.all_to_all(parts, FIRST, 0, 0)  14.4 us
    all_to_all x1, blocking collectives, body(): parts = lax.all_to_all(packed.reshape(first, rows, CH), FIRST, 0, 0)  12.9 us
    all_to_all x1, starting transfers between devices, body(): parts = lax.all_to_all(sums, FAR, 0, 0)  12.9 us
    all_to_all x1, blocking collectives, body(): parts = lax.all_to_all(sums, NEAR, 0, 0)  12.6 us
    ppermute x2, starting transfers between devices, column_passed(): return lax.ppermute(column, SPACE, [(i, i ^ 1) for i in range(space)])  11.4 us
    all_to_all x1, waiting for transfers between devices, body(): totals = lax.all_to_all(sums, NEAR, 0, 0)  7.46 us
  transfers between devices with their start and end apart: 9, of which 5 were waited for; matrix products, arithmetic and copies ran while one was open for 1% of the time, Pallas kernels for 1%

profile of v7, /device:TPU:1, one launch (start us, length us, event | category | flops | bytes accessed | tf_op | source)
XLA Modules:
  0.0 147.8 jit_solution(17203094143523539677)
XLA Ops:
  0.7 1.0 copy.21
  1.7 8.8 %collective-permute-start = (bf16[2,14,256]{2,1,0:T(8,128)(2,1)S(1)}, bf16[2,14,256]{2,1,0:T(8,128)(2,1)S(1)}, u32[]{:S(2)}, u32[]{:S(2)}) collective-permute-start(bf16[2,14,256]{2,1,0:T(8,128)(2,1)S(1)} %pad_maximum_fusion), channel_id=1, source_target_pairs={{0,1},{1,0},{2,3},{3,2},{4,5},{5,4},{6,7},{7,6},{8,9},{9,8},{10,11... | collective-permute-start | bytes 43016 | tf_op jit(solution)/shard_map/ppermute | solution.py:381
  10.6 1.0 copy.16.act_ref
  12.8 1.3 collective-permute-start.1
  14.1 1.3 collective-permute-start.2
  16.1 2.4 %collective-permute-done.2.down_ref = bf16[32,256]{1,0:T(8,128)(2,1)S(1)} collective-permute-done((bf16[32,256]{1,0:T(8,128)(2,1)S(1)}, bf16[32,256]{1,0:T(8,128)(2,1)S(1)}, u32[]{:S(2)}, u32[]{:S(2)}) %collective-permute-start.2) | collective-permute-done | bytes 16416 | tf_op jit(solution)/shard_map/ppermute | solution.py:377
  18.6 1.5 shard_map.138
  20.0 12.6 %all_to_all.40.parts_ref = f32[16,1,640]{2,1,0:T(1,128)S(1)} all-to-all(f32[16,1,640]{2,1,0:T(1,128)S(1)} %get-tuple-element.39), channel_id=1, replica_groups=mesh['zh'=4,'x'=4,'zl'=2,'y'=8,'core'=2] {'y','core'}, dimensions={0} | all-to-all | bytes 81920 | tf_op jit(solution)/shard_map/all_to_all | solution.py:418
  33.4 12.9 %all-to-all-start.1 = ((f32[32,1,640]{2,1,0:T(1,128)}), f32[32,1,640]{2,1,0:T(1,128)S(1)}, u32[]{:S(2)}, u32[]{:S(2)}) async-start(f32[32,1,640]{2,1,0:T(1,128)} %get-tuple-element.41), calls=%async_computation.1 | async-start | bytes 163840 | tf_op jit(solution)/shard_map/all_to_all | solution.py:423
  46.3 2.1 %collective-permute-start.3 = (f32[32,640]{1,0:T(8,128)S(1)}, f32[32,640]{1,0:T(8,128)S(1)}, u32[]{:S(2)}, u32[]{:S(2)}) collective-permute-start(f32[32,640]{1,0:T(8,128)S(1)} %get-tuple-element.45), channel_id=1, source_target_pairs={{0,2},{1,3},{2,4},{3,5},{4,6},{5,7},{6,8},{7,9},{8,10},{9,11},{10,... | collective-permute-start | bytes 245768 | tf_op jit(solution)/shard_map/ppermute | solution.py:376
  48.4 1.3 collective-permute-start.4
  49.7 5.6 %all-to-all-done.1.parts_ref = f32[32,1,640]{2,1,0:T(1,128)S(1)} async-done(((f32[32,1,640]{2,1,0:T(1,128)}), f32[32,1,640]{2,1,0:T(1,128)S(1)}, u32[]{:S(2)}, u32[]{:S(2)}) %all-to-all-start.1) | async-done | bytes 81952 | tf_op jit(solution)/shard_map/all_to_all | solution.py:423
  55.3 1.0 shard_map.140
  56.3 5.2 %all-to-all-start.2 = ((f32[16,1,512]{2,1,0:T(1,128)}), f32[16,1,512]{2,1,0:T(1,128)S(1)}, u32[]{:S(2)}, u32[]{:S(2)}) async-start(f32[16,1,512]{2,1,0:T(1,128)} %get-tuple-element.44), calls=%async_computation.2 | async-start | bytes 65536 | tf_op jit(solution)/shard_map/all_to_all | solution.py:430
  61.6 7.5 %all-to-all-done.2.parts_ref = f32[16,1,512]{2,1,0:T(1,128)S(1)} async-done(((f32[16,1,512]{2,1,0:T(1,128)}), f32[16,1,512]{2,1,0:T(1,128)S(1)}, u32[]{:S(2)}, u32[]{:S(2)}) %all-to-all-start.2) | async-done | bytes 32800 | tf_op jit(solution)/shard_map/all_to_all | solution.py:430
  69.7 6.4 %all-to-all-start.3 = ((f32[32,1,512]{2,1,0:T(1,128)}), f32[32,1,512]{2,1,0:T(1,128)S(1)}, u32[]{:S(2)}, u32[]{:S(2)}) async-start(f32[32,1,512]{2,1,0:T(1,128)} %get-tuple-element.47), calls=%async_computation.3 | async-start | bytes 131072 | tf_op jit(solution)/shard_map/all_to_all | solution.py:437
  76.1 2.6 %collective-permute-start.5 = (f32[16,640]{1,0:T(8,128)S(1)}, f32[16,640]{1,0:T(8,128)S(1)}, u32[]{:S(2)}, u32[]{:S(2)}) collective-permute-start(f32[16,640]{1,0:T(8,128)S(1)} %get-tuple-element.48), channel_id=1, source_target_pairs={{0,1},{1,0},{2,3},{3,2},{4,5},{5,4},{6,7},{7,6},{8,9},{9,8},{10,11... | collective-permute-start | bytes 122888 | tf_op jit(solution)/shard_map/ppermute | solution.py:381
  79.5 5.5 %all-to-all-done.3.totals_ref = f32[32,1,512]{2,1,0:T(1,128)S(1)} async-done(((f32[32,1,512]{2,1,0:T(1,128)}), f32[32,1,512]{2,1,0:T(1,128)S(1)}, u32[]{:S(2)}, u32[]{:S(2)}) %all-to-all-start.3) | async-done | bytes 65568 | tf_op jit(solution)/shard_map/all_to_all | solution.py:437
  85.1 3.9 %shard_map.142 = (bf16[14,14,2,256]{3,2,1,0:T(2,128)(2,1)}, bf16[896,256]{1,0:T(8,128)(2,1)S(1)}, f32[1,256]{1,0:T(1,128)}, f32[1,256]{1,0:T(1,128)}) custom-call(s32[1,2,8]{2,1,0:T(2,128)S(1)} %copy-done.4, f32[32,1,640]{2,1,0:T(1,128)S(1)} %all-to-all-done.1.parts_ref, f32[32,1,512]{2,1,0:T(1,128)S(1)} %all-to-all-done.3.totals_ref, ...), custom_call_target="tpu_custom_call" | custom-call | tf_op jit(solution)/shard_map/pallas_call | solution.py:441
  89.0 12.9 %all_to_all.41.parts_ref = bf16[8,112,256]{2,1,0:T(8,128)(2,1)S(1)} all-to-all(bf16[8,112,256]{2,1,0:T(8,128)(2,1)S(1)} %bitcast.19), channel_id=1, replica_groups=mesh['zh'=4,'x'=4,'zl'=2,'y'=8,'core'=2] {'x','core'}, dimensions={0} | all-to-all | bytes 917504 | tf_op jit(solution)/shard_map/all_to_all | solution.py:455
  102.0 15.3 %all_to_all.42.parts_ref = f32[64,2,256]{2,1,0:T(2,128)S(1)} all-to-all(f32[64,2,256]{2,1,0:T(2,128)S(1)} %shard_map.143), channel_id=1, replica_groups=mesh['zh'=4,'x'=4,'zl'=2,'y'=8,'core'=2] {'zh','zl','y'}, dimensions={0} | all-to-all | bytes 262144 | tf_op jit(solution)/shard_map/all_to_all | solution.py:457
  117.5 14.9 %all_to_all.43.part_ref = bf16[64,2,256]{2,1,0:T(2,128)(2,1)S(1)} all-to-all(bf16[64,2,256]{2,1,0:T(2,128)(2,1)S(1)} %shard_map.144), channel_id=1, replica_groups=mesh['zh'=4,'x'=4,'zl'=2,'y'=8,'core'=2] {'zh','zl','y'}, dimensions={0} | all-to-all | bytes 131072 | tf_op jit(solution)/shard_map/all_to_all | solution.py:459
  132.4 14.4 %all_to_all.44 = bf16[8,112,256]{2,1,0:T(8,128)(2,1)S(1)} all-to-all(bf16[8,112,256]{2,1,0:T(8,128)(2,1)S(1)} %shard_map.145), channel_id=1, replica_groups=mesh['zh'=4,'x'=4,'zl'=2,'y'=8,'core'=2] {'x','core'}, dimensions={0} | all-to-all | bytes 917504 | tf_op jit(solution)/shard_map/all_to_all | solution.py:461
  146.8 0.9 shard_map.146
  (34 shorter events, 4.4 us)
Async XLA Ops:
  0.6 14.7 %copy-start.8 = (s32[1,2,14,14]{3,1,2,0:T(2,128)S(1)}, s32[1,2,14,14]{3,1,2,0:T(2,128)}, u32[]{:S(2)}) copy-start(s32[1,2,14,14]{3,1,2,0:T(2,128)} %param.10) | copy-start | bytes 4708
  0.6 14.7 %copy-start.7 = (bf16[1,2,14,14,512]{4,1,3,2,0:T(2,128)(2,1)S(1)}, bf16[1,2,14,14,512]{4,1,3,2,0:T(2,128)(2,1)}, u32[]{:S(2)}) copy-start(bf16[1,2,14,14,512]{4,1,3,2,0:T(2,128)(2,1)} %param.17) | copy-start | bytes 1204228
  0.7 14.8 %copy-start.3 = (bf16[3,3,8,256]{3,2,1,0:T(8,128)(2,1)S(1)}, bf16[3,3,8,256]{3,2,1,0:T(8,128)(2,1)}, u32[]{:S(2)}) copy-start(bf16[3,3,8,256]{3,2,1,0:T(8,128)(2,1)} %group_ref.3) | copy-start | bytes 110596
  0.7 14.8 %copy-start.2 = (bf16[256,512]{1,0:T(8,128)(2,1)S(1)}, bf16[256,512]{1,0:T(8,128)(2,1)}, u32[]{:S(2)}) copy-start(bf16[256,512]{1,0:T(8,128)(2,1)} %expand_ref.1) | copy-start | bytes 786436
  0.7 14.8 %copy-start.6 = (f32[256]{0:T(256)S(1)}, f32[256]{0:T(256)}, u32[]{:S(2)}) copy-start(f32[256]{0:T(256)} %param.15) | copy-start | bytes 3076
  0.7 14.8 %copy-start.5 = (f32[256]{0:T(256)S(1)}, f32[256]{0:T(256)}, u32[]{:S(2)}) copy-start(f32[256]{0:T(256)} %param.14) | copy-start | bytes 3076
  1.7 9.8 %collective-permute-start = (bf16[2,14,256]{2,1,0:T(8,128)(2,1)S(1)}, bf16[2,14,256]{2,1,0:T(8,128)(2,1)S(1)}, u32[]{:S(2)}, u32[]{:S(2)}) collective-permute-start(bf16[2,14,256]{2,1,0:T(8,128)(2,1)S(1)} %pad_maximum_fusion), channel_id=1, source_target_pairs={{0,1},{1,0},{2,3},{3,2},{4,5},{5,4},{6,7},{7,6},{8,9},{9,8},{10,11... | collective-permute-start | bytes 43016 | tf_op jit(solution)/shard_map/ppermute | solution.py:381
  10.5 8.0 %copy-start.4 = (s32[1,2,8]{2,1,0:T(2,128)S(1)}, s32[1,2,8]{2,1,0:T(2,128)}, u32[]{:S(2)}) copy-start(s32[1,2,8]{2,1,0:T(2,128)} %links_ref.3) | copy-start | bytes 196
  11.5 0.9 copy-start
  12.8 3.3 %collective-permute-start.1 = (bf16[32,256]{1,0:T(8,128)(2,1)S(1)}, bf16[32,256]{1,0:T(8,128)(2,1)S(1)}, u32[]{:S(2)}, u32[]{:S(2)}) collective-permute-start(bf16[32,256]{1,0:T(8,128)(2,1)S(1)} %get-tuple-element.33), channel_id=1, source_target_pairs={{0,2},{1,3},{2,4},{3,5},{4,6},{5,7},{6,8},{7,9},{8,10},{9,11},{10,... | collective-permute-start | bytes 49160 | tf_op jit(solution)/shard_map/ppermute | solution.py:376
  14.1 4.5 %collective-permute-start.2 = (bf16[32,256]{1,0:T(8,128)(2,1)S(1)}, bf16[32,256]{1,0:T(8,128)(2,1)S(1)}, u32[]{:S(2)}, u32[]{:S(2)}) collective-permute-start(bf16[32,256]{1,0:T(8,128)(2,1)S(1)} %get-tuple-element.34), channel_id=1, source_target_pairs={{2,0},{3,1},{4,2},{5,3},{6,4},{7,5},{8,6},{9,7},{10,8},{11,9},{12,... | collective-permute-start | bytes 49160 | tf_op jit(solution)/shard_map/ppermute | solution.py:377
  33.4 22.0 %all-to-all-start.1 = ((f32[32,1,640]{2,1,0:T(1,128)}), f32[32,1,640]{2,1,0:T(1,128)S(1)}, u32[]{:S(2)}, u32[]{:S(2)}) async-start(f32[32,1,640]{2,1,0:T(1,128)} %get-tuple-element.41), calls=%async_computation.1 | async-start | bytes 163840 | tf_op jit(solution)/shard_map/all_to_all | solution.py:423
  46.3 15.3 %collective-permute-start.3 = (f32[32,640]{1,0:T(8,128)S(1)}, f32[32,640]{1,0:T(8,128)S(1)}, u32[]{:S(2)}, u32[]{:S(2)}) collective-permute-start(f32[32,640]{1,0:T(8,128)S(1)} %get-tuple-element.45), channel_id=1, source_target_pairs={{0,2},{1,3},{2,4},{3,5},{4,6},{5,7},{6,8},{7,9},{8,10},{9,11},{10,... | collective-permute-start | bytes 245768 | tf_op jit(solution)/shard_map/ppermute | solution.py:376
  48.4 13.1 %collective-permute-start.4 = (f32[32,640]{1,0:T(8,128)S(1)}, f32[32,640]{1,0:T(8,128)S(1)}, u32[]{:S(2)}, u32[]{:S(2)}) collective-permute-start(f32[32,640]{1,0:T(8,128)S(1)} %get-tuple-element.46), channel_id=1, source_target_pairs={{2,0},{3,1},{4,2},{5,3},{6,4},{7,5},{8,6},{9,7},{10,8},{11,9},{12,... | collective-permute-start | bytes 245768 | tf_op jit(solution)/shard_map/ppermute | solution.py:377
  56.3 28.8 %copy-start.1 = (bf16[256,256]{1,0:T(8,128)(2,1)S(1)}, bf16[256,256]{1,0:T(8,128)(2,1)}, u32[]{:S(2)}) copy-start(bf16[256,256]{1,0:T(8,128)(2,1)} %w_ref.3) | copy-start | bytes 393220
  56.3 12.7 %all-to-all-start.2 = ((f32[16,1,512]{2,1,0:T(1,128)}), f32[16,1,512]{2,1,0:T(1,128)S(1)}, u32[]{:S(2)}, u32[]{:S(2)}) async-start(f32[16,1,512]{2,1,0:T(1,128)} %get-tuple-element.44), calls=%async_computation.2 | async-start | bytes 65536 | tf_op jit(solution)/shard_map/all_to_all | solution.py:430
  69.7 15.4 %all-to-all-start.3 = ((f32[32,1,512]{2,1,0:T(1,128)}), f32[32,1,512]{2,1,0:T(1,128)S(1)}, u32[]{:S(2)}, u32[]{:S(2)}) async-start(f32[32,1,512]{2,1,0:T(1,128)} %get-tuple-element.47), calls=%async_computation.3 | async-start | bytes 131072 | tf_op jit(solution)/shard_map/all_to_all | solution.py:437
  76.1 3.4 %collective-permute-start.5 = (f32[16,640]{1,0:T(8,128)S(1)}, f32[16,640]{1,0:T(8,128)S(1)}, u32[]{:S(2)}, u32[]{:S(2)}) collective-permute-start(f32[16,640]{1,0:T(8,128)S(1)} %get-tuple-element.48), channel_id=1, source_target_pairs={{0,1},{1,0},{2,3},{3,2},{4,5},{5,4},{6,7},{7,6},{8,9},{9,8},{10,11... | collective-permute-start | bytes 122888 | tf_op jit(solution)/shard_map/ppermute | solution.py:381

commit v8 on v7

--- a/solution.py
+++ b/solution.py
@@ -340,11 +340,11 @@
     spare = total_ref.shape[0] * total_ref.shape[1] - total.shape[0]
     if spare:
         total = jnp.concatenate([total, jnp.zeros((spare, CH), F32)], axis=0)
-    total_ref[...] = total.reshape(total_ref.shape)
+    total_ref[...] = total.reshape(total_ref.shape).astype(BF16)
 
 
 def total_kernel(parts_ref, total_ref):
-    total = jnp.sum(parts_ref[...], axis=0).astype(BF16)
+    total = jnp.sum(parts_ref[...].astype(F32), axis=0).astype(BF16)
     total_ref[...] = jnp.broadcast_to(total[None], total_ref.shape)
 
 
@@ -453,7 +453,7 @@
         activations, w_reduce, expand_grad,
     )
     parts = lax.all_to_all(packed.reshape(first, rows, CH), FIRST, 0, 0)
-    total = call(near_total_kernel, shape((second, share, CH), F32), [VMEM])(parts)
+    total = call(near_total_kernel, shape((second, share, CH), BF16), [VMEM])(parts)
     parts = lax.all_to_all(total, SECOND, 0, 0)
     total = call(total_kernel, shape((second, share, CH), BF16), [VMEM])(parts)
     part = lax.all_to_all(total, SECOND, 0, 0)

time: 148 us -> 148 us (level)
  no operation moved by 1% of the time
where the time goes in v8:
time: 148 us; the launch traced here: 147 us
  blocking collectives  69.7 us (47%)
  starting transfers between devices  41.9 us (28%)
  waiting for transfers between devices  21.9 us (15%)
  Pallas kernels  9.89 us (7%)
  local copies, waits for them, and re-layouts  2.98 us (2%)
    all_to_all x1, blocking collectives, body(): parts = lax.all_to_all(total, SECOND, 0, 0)  14.9 us
    all_to_all x1, blocking collectives, body(): part = lax.all_to_all(total, SECOND, 0, 0)  14.9 us
    all_to_all x1, blocking collectives, body(): gathered = lax.all_to_all(parts, FIRST, 0, 0)  14.4 us
    all_to_all x1, blocking collectives, body(): parts = lax.all_to_all(packed.reshape(first, rows, CH), FIRST, 0, 0)  12.9 us
    all_to_all x1, starting transfers between devices, body(): parts = lax.all_to_all(sums, FAR, 0, 0)  12.9 us
    all_to_all x1, blocking collectives, body(): parts = lax.all_to_all(sums, NEAR, 0, 0)  12.6 us
    ppermute x2, starting transfers between devices, column_passed(): return lax.ppermute(column, SPACE, [(i, i ^ 1) for i in range(space)])  11.4 us
    all_to_all x1, waiting for transfers between devices, body(): totals = lax.all_to_all(sums, NEAR, 0, 0)  7.46 us
  transfers between devices with their start and end apart: 9, of which 5 were waited for; matrix products, arithmetic and copies ran while one was open for 1% of the time, Pallas kernels for 1%

profile of v8, /device:TPU:1, one launch (start us, length us, event | category | flops | bytes accessed | tf_op | source)
XLA Modules:
  0.0 147.4 jit_solution(7318130544413782733)
XLA Ops:
  0.7 1.0 copy.21
  1.7 8.8 %collective-permute-start = (bf16[2,14,256]{2,1,0:T(8,128)(2,1)S(1)}, bf16[2,14,256]{2,1,0:T(8,128)(2,1)S(1)}, u32[]{:S(2)}, u32[]{:S(2)}) collective-permute-start(bf16[2,14,256]{2,1,0:T(8,128)(2,1)S(1)} %pad_maximum_fusion), channel_id=1, source_target_pairs={{0,1},{1,0},{2,3},{3,2},{4,5},{5,4},{6,7},{7,6},{8,9},{9,8},{10,11... | collective-permute-start | bytes 43016 | tf_op jit(solution)/shard_map/ppermute | solution.py:381
  10.6 1.0 copy.16.act_ref
  12.8 1.3 collective-permute-start.1
  14.1 1.3 collective-permute-start.2
  16.1 2.4 %collective-permute-done.2.down_ref = bf16[32,256]{1,0:T(8,128)(2,1)S(1)} collective-permute-done((bf16[32,256]{1,0:T(8,128)(2,1)S(1)}, bf16[32,256]{1,0:T(8,128)(2,1)S(1)}, u32[]{:S(2)}, u32[]{:S(2)}) %collective-permute-start.2) | collective-permute-done | bytes 16416 | tf_op jit(solution)/shard_map/ppermute | solution.py:377
  18.6 1.5 shard_map.138
  20.0 12.6 %all_to_all.40.parts_ref = f32[16,1,640]{2,1,0:T(1,128)S(1)} all-to-all(f32[16,1,640]{2,1,0:T(1,128)S(1)} %get-tuple-element.39), channel_id=1, replica_groups=mesh['zh'=4,'x'=4,'zl'=2,'y'=8,'core'=2] {'y','core'}, dimensions={0} | all-to-all | bytes 81920 | tf_op jit(solution)/shard_map/all_to_all | solution.py:418
  33.4 12.9 %all-to-all-start.1 = ((f32[32,1,640]{2,1,0:T(1,128)}), f32[32,1,640]{2,1,0:T(1,128)S(1)}, u32[]{:S(2)}, u32[]{:S(2)}) async-start(f32[32,1,640]{2,1,0:T(1,128)} %get-tuple-element.41), calls=%async_computation.1 | async-start | bytes 163840 | tf_op jit(solution)/shard_map/all_to_all | solution.py:423
  46.3 2.1 %collective-permute-start.3 = (f32[32,640]{1,0:T(8,128)S(1)}, f32[32,640]{1,0:T(8,128)S(1)}, u32[]{:S(2)}, u32[]{:S(2)}) collective-permute-start(f32[32,640]{1,0:T(8,128)S(1)} %get-tuple-element.45), channel_id=1, source_target_pairs={{0,2},{1,3},{2,4},{3,5},{4,6},{5,7},{6,8},{7,9},{8,10},{9,11},{10,... | collective-permute-start | bytes 245768 | tf_op jit(solution)/shard_map/ppermute | solution.py:376
  48.4 1.3 collective-permute-start.4
  49.7 5.6 %all-to-all-done.1.parts_ref = f32[32,1,640]{2,1,0:T(1,128)S(1)} async-done(((f32[32,1,640]{2,1,0:T(1,128)}), f32[32,1,640]{2,1,0:T(1,128)S(1)}, u32[]{:S(2)}, u32[]{:S(2)}) %all-to-all-start.1) | async-done | bytes 81952 | tf_op jit(solution)/shard_map/all_to_all | solution.py:423
  55.3 1.0 shard_map.140
  56.3 5.2 %all-to-all-start.2 = ((f32[16,1,512]{2,1,0:T(1,128)}), f32[16,1,512]{2,1,0:T(1,128)S(1)}, u32[]{:S(2)}, u32[]{:S(2)}) async-start(f32[16,1,512]{2,1,0:T(1,128)} %get-tuple-element.44), calls=%async_computation.2 | async-start | bytes 65536 | tf_op jit(solution)/shard_map/all_to_all | solution.py:430
  61.6 7.5 %all-to-all-done.2.parts_ref = f32[16,1,512]{2,1,0:T(1,128)S(1)} async-done(((f32[16,1,512]{2,1,0:T(1,128)}), f32[16,1,512]{2,1,0:T(1,128)S(1)}, u32[]{:S(2)}, u32[]{:S(2)}) %all-to-all-start.2) | async-done | bytes 32800 | tf_op jit(solution)/shard_map/all_to_all | solution.py:430
  69.7 6.4 %all-to-all-start.3 = ((f32[32,1,512]{2,1,0:T(1,128)}), f32[32,1,512]{2,1,0:T(1,128)S(1)}, u32[]{:S(2)}, u32[]{:S(2)}) async-start(f32[32,1,512]{2,1,0:T(1,128)} %get-tuple-element.47), calls=%async_computation.3 | async-start | bytes 131072 | tf_op jit(solution)/shard_map/all_to_all | solution.py:437
  76.1 2.6 %collective-permute-start.5 = (f32[16,640]{1,0:T(8,128)S(1)}, f32[16,640]{1,0:T(8,128)S(1)}, u32[]{:S(2)}, u32[]{:S(2)}) collective-permute-start(f32[16,640]{1,0:T(8,128)S(1)} %get-tuple-element.48), channel_id=1, source_target_pairs={{0,1},{1,0},{2,3},{3,2},{4,5},{5,4},{6,7},{7,6},{8,9},{9,8},{10,11... | collective-permute-start | bytes 122888 | tf_op jit(solution)/shard_map/ppermute | solution.py:381
  79.5 5.5 %all-to-all-done.3.totals_ref = f32[32,1,512]{2,1,0:T(1,128)S(1)} async-done(((f32[32,1,512]{2,1,0:T(1,128)}), f32[32,1,512]{2,1,0:T(1,128)S(1)}, u32[]{:S(2)}, u32[]{:S(2)}) %all-to-all-start.3) | async-done | bytes 65568 | tf_op jit(solution)/shard_map/all_to_all | solution.py:437
  85.1 3.9 %shard_map.142 = (bf16[14,14,2,256]{3,2,1,0:T(2,128)(2,1)}, bf16[896,256]{1,0:T(8,128)(2,1)S(1)}, f32[1,256]{1,0:T(1,128)}, f32[1,256]{1,0:T(1,128)}) custom-call(s32[1,2,8]{2,1,0:T(2,128)S(1)} %copy-done.4, f32[32,1,640]{2,1,0:T(1,128)S(1)} %all-to-all-done.1.parts_ref, f32[32,1,512]{2,1,0:T(1,128)S(1)} %all-to-all-done.3.totals_ref, ...), custom_call_target="tpu_custom_call" | custom-call | tf_op jit(solution)/shard_map/pallas_call | solution.py:441
  89.0 12.9 %all_to_all.41.parts_ref = bf16[8,112,256]{2,1,0:T(8,128)(2,1)S(1)} all-to-all(bf16[8,112,256]{2,1,0:T(8,128)(2,1)S(1)} %bitcast.19), channel_id=1, replica_groups=mesh['zh'=4,'x'=4,'zl'=2,'y'=8,'core'=2] {'x','core'}, dimensions={0} | all-to-all | bytes 917504 | tf_op jit(solution)/shard_map/all_to_all | solution.py:455
  102.1 14.9 %all_to_all.42.parts_ref = bf16[64,2,256]{2,1,0:T(2,128)(2,1)S(1)} all-to-all(bf16[64,2,256]{2,1,0:T(2,128)(2,1)S(1)} %shard_map.143), channel_id=1, replica_groups=mesh['zh'=4,'x'=4,'zl'=2,'y'=8,'core'=2] {'zh','zl','y'}, dimensions={0} | all-to-all | bytes 131072 | tf_op jit(solution)/shard_map/all_to_all | solution.py:457
  117.1 14.9 %all_to_all.43.part_ref = bf16[64,2,256]{2,1,0:T(2,128)(2,1)S(1)} all-to-all(bf16[64,2,256]{2,1,0:T(2,128)(2,1)S(1)} %shard_map.144), channel_id=1, replica_groups=mesh['zh'=4,'x'=4,'zl'=2,'y'=8,'core'=2] {'zh','zl','y'}, dimensions={0} | all-to-all | bytes 131072 | tf_op jit(solution)/shard_map/all_to_all | solution.py:459
  132.0 14.4 %all_to_all.44 = bf16[8,112,256]{2,1,0:T(8,128)(2,1)S(1)} all-to-all(bf16[8,112,256]{2,1,0:T(8,128)(2,1)S(1)} %shard_map.145), channel_id=1, replica_groups=mesh['zh'=4,'x'=4,'zl'=2,'y'=8,'core'=2] {'x','core'}, dimensions={0} | all-to-all | bytes 917504 | tf_op jit(solution)/shard_map/all_to_all | solution.py:461
  146.4 0.9 shard_map.146
  (34 shorter events, 4.4 us)
Async XLA Ops:
  0.6 14.7 %copy-start.8 = (s32[1,2,14,14]{3,1,2,0:T(2,128)S(1)}, s32[1,2,14,14]{3,1,2,0:T(2,128)}, u32[]{:S(2)}) copy-start(s32[1,2,14,14]{3,1,2,0:T(2,128)} %param.10) | copy-start | bytes 4708
  0.6 14.7 %copy-start.7 = (bf16[1,2,14,14,512]{4,1,3,2,0:T(2,128)(2,1)S(1)}, bf16[1,2,14,14,512]{4,1,3,2,0:T(2,128)(2,1)}, u32[]{:S(2)}) copy-start(bf16[1,2,14,14,512]{4,1,3,2,0:T(2,128)(2,1)} %param.17) | copy-start | bytes 1204228
  0.7 14.8 %copy-start.3 = (bf16[3,3,8,256]{3,2,1,0:T(8,128)(2,1)S(1)}, bf16[3,3,8,256]{3,2,1,0:T(8,128)(2,1)}, u32[]{:S(2)}) copy-start(bf16[3,3,8,256]{3,2,1,0:T(8,128)(2,1)} %group_ref.3) | copy-start | bytes 110596
  0.7 14.8 %copy-start.2 = (bf16[256,512]{1,0:T(8,128)(2,1)S(1)}, bf16[256,512]{1,0:T(8,128)(2,1)}, u32[]{:S(2)}) copy-start(bf16[256,512]{1,0:T(8,128)(2,1)} %expand_ref.1) | copy-start | bytes 786436
  0.7 14.8 %copy-start.6 = (f32[256]{0:T(256)S(1)}, f32[256]{0:T(256)}, u32[]{:S(2)}) copy-start(f32[256]{0:T(256)} %param.15) | copy-start | bytes 3076
  0.7 14.8 %copy-start.5 = (f32[256]{0:T(256)S(1)}, f32[256]{0:T(256)}, u32[]{:S(2)}) copy-start(f32[256]{0:T(256)} %param.14) | copy-start | bytes 3076
  1.7 9.8 %collective-permute-start = (bf16[2,14,256]{2,1,0:T(8,128)(2,1)S(1)}, bf16[2,14,256]{2,1,0:T(8,128)(2,1)S(1)}, u32[]{:S(2)}, u32[]{:S(2)}) collective-permute-start(bf16[2,14,256]{2,1,0:T(8,128)(2,1)S(1)} %pad_maximum_fusion), channel_id=1, source_target_pairs={{0,1},{1,0},{2,3},{3,2},{4,5},{5,4},{6,7},{7,6},{8,9},{9,8},{10,11... | collective-permute-start | bytes 43016 | tf_op jit(solution)/shard_map/ppermute | solution.py:381
  10.5 8.0 %copy-start.4 = (s32[1,2,8]{2,1,0:T(2,128)S(1)}, s32[1,2,8]{2,1,0:T(2,128)}, u32[]{:S(2)}) copy-start(s32[1,2,8]{2,1,0:T(2,128)} %links_ref.3) | copy-start | bytes 196
  11.5 0.9 copy-start
  12.8 3.3 %collective-permute-start.1 = (bf16[32,256]{1,0:T(8,128)(2,1)S(1)}, bf16[32,256]{1,0:T(8,128)(2,1)S(1)}, u32[]{:S(2)}, u32[]{:S(2)}) collective-permute-start(bf16[32,256]{1,0:T(8,128)(2,1)S(1)} %get-tuple-element.33), channel_id=1, source_target_pairs={{0,2},{1,3},{2,4},{3,5},{4,6},{5,7},{6,8},{7,9},{8,10},{9,11},{10,... | collective-permute-start | bytes 49160 | tf_op jit(solution)/shard_map/ppermute | solution.py:376
  14.1 4.5 %collective-permute-start.2 = (bf16[32,256]{1,0:T(8,128)(2,1)S(1)}, bf16[32,256]{1,0:T(8,128)(2,1)S(1)}, u32[]{:S(2)}, u32[]{:S(2)}) collective-permute-start(bf16[32,256]{1,0:T(8,128)(2,1)S(1)} %get-tuple-element.34), channel_id=1, source_target_pairs={{2,0},{3,1},{4,2},{5,3},{6,4},{7,5},{8,6},{9,7},{10,8},{11,9},{12,... | collective-permute-start | bytes 49160 | tf_op jit(solution)/shard_map/ppermute | solution.py:377
  33.4 22.0 %all-to-all-start.1 = ((f32[32,1,640]{2,1,0:T(1,128)}), f32[32,1,640]{2,1,0:T(1,128)S(1)}, u32[]{:S(2)}, u32[]{:S(2)}) async-start(f32[32,1,640]{2,1,0:T(1,128)} %get-tuple-element.41), calls=%async_computation.1 | async-start | bytes 163840 | tf_op jit(solution)/shard_map/all_to_all | solution.py:423
  46.3 15.3 %collective-permute-start.3 = (f32[32,640]{1,0:T(8,128)S(1)}, f32[32,640]{1,0:T(8,128)S(1)}, u32[]{:S(2)}, u32[]{:S(2)}) collective-permute-start(f32[32,640]{1,0:T(8,128)S(1)} %get-tuple-element.45), channel_id=1, source_target_pairs={{0,2},{1,3},{2,4},{3,5},{4,6},{5,7},{6,8},{7,9},{8,10},{9,11},{10,... | collective-permute-start | bytes 245768 | tf_op jit(solution)/shard_map/ppermute | solution.py:376
  48.4 13.1 %collective-permute-start.4 = (f32[32,640]{1,0:T(8,128)S(1)}, f32[32,640]{1,0:T(8,128)S(1)}, u32[]{:S(2)}, u32[]{:S(2)}) collective-permute-start(f32[32,640]{1,0:T(8,128)S(1)} %get-tuple-element.46), channel_id=1, source_target_pairs={{2,0},{3,1},{4,2},{5,3},{6,4},{7,5},{8,6},{9,7},{10,8},{11,9},{12,... | collective-permute-start | bytes 245768 | tf_op jit(solution)/shard_map/ppermute | solution.py:377
  56.3 28.8 %copy-start.1 = (bf16[256,256]{1,0:T(8,128)(2,1)S(1)}, bf16[256,256]{1,0:T(8,128)(2,1)}, u32[]{:S(2)}) copy-start(bf16[256,256]{1,0:T(8,128)(2,1)} %w_ref.3) | copy-start | bytes 393220
  56.3 12.7 %all-to-all-start.2 = ((f32[16,1,512]{2,1,0:T(1,128)}), f32[16,1,512]{2,1,0:T(1,128)S(1)}, u32[]{:S(2)}, u32[]{:S(2)}) async-start(f32[16,1,512]{2,1,0:T(1,128)} %get-tuple-element.44), calls=%async_computation.2 | async-start | bytes 65536 | tf_op jit(solution)/shard_map/all_to_all | solution.py:430
  69.7 15.4 %all-to-all-start.3 = ((f32[32,1,512]{2,1,0:T(1,128)}), f32[32,1,512]{2,1,0:T(1,128)S(1)}, u32[]{:S(2)}, u32[]{:S(2)}) async-start(f32[32,1,512]{2,1,0:T(1,128)} %get-tuple-element.47), calls=%async_computation.3 | async-start | bytes 131072 | tf_op jit(solution)/shard_map/all_to_all | solution.py:437
  76.1 3.4 %collective-permute-start.5 = (f32[16,640]{1,0:T(8,128)S(1)}, f32[16,640]{1,0:T(8,128)S(1)}, u32[]{:S(2)}, u32[]{:S(2)}) collective-permute-start(f32[16,640]{1,0:T(8,128)S(1)} %get-tuple-element.48), channel_id=1, source_target_pairs={{0,1},{1,0},{2,3},{3,2},{4,5},{5,4},{6,7},{7,6},{8,9},{9,8},{10,11... | collective-permute-start | bytes 122888 | tf_op jit(solution)/shard_map/ppermute | solution.py:381
